TPU v7x, 32 devices: a whole 2x2x4 slice. The times are simulated.
32 devices in a mesh: dp: 8 (over y, x, core), tensor: 4 (over z).
Axes of the slice: x: 2, y: 2, z: 4, core: 2. Of those that a mesh axis runs over, the one named last changes fastest.
Arguments:
- tokens: bfloat16 [4096, 768], P(('dp', 'tensor')), may hold values from -6 to 6
- segment_ids: int32 [8, 512], P('dp'), may hold values from 0 to 3, never falling along the last dimension, each value on 1 to 256 neighbouring positions
- w_query: bfloat16 [768, 768], P(None, 'tensor'), may hold values from -0.21875 to 0.21875
- b_query: bfloat16 [768], P('tensor'), may hold values from -3 to 3
- w_key: bfloat16 [768, 768], P(None, 'tensor'), may hold values from -0.21875 to 0.21875
- b_key: bfloat16 [768], P('tensor'), may hold values from -3 to 3
- w_value: bfloat16 [768, 768], P(None, 'tensor'), may hold values from -0.21875 to 0.21875
- b_value: bfloat16 [768], P('tensor'), may hold values from -3 to 3
- w_out: bfloat16 [768, 768], P('tensor'), may hold values from -0.625 to 0.625
- b_out: bfloat16 [768], replicated, may hold values from -3 to 3
- gain_mixer: bfloat16 [768], replicated, may hold values from 0.5 to 1.5
- shift_mixer: bfloat16 [768], replicated, may hold values from -3 to 3
- w_up: bfloat16 [768, 3072], P(None, 'tensor'), may hold values from -0.21875 to 0.21875
- b_up: bfloat16 [3072], P('tensor'), may hold values from -3 to 3
- w_down: bfloat16 [3072, 768], P('tensor'), may hold values from -0.15625 to 0.15625
- b_down: bfloat16 [768], replicated, may hold values from -3 to 3
- gain_feed: bfloat16 [768], replicated, may hold values from 0.5 to 1.5
- shift_feed: bfloat16 [768], replicated, may hold values from -3 to 3
- cotangent: bfloat16 [4096, 768], P(('dp', 'tensor')), may hold values from -6 to 6
Outputs:
- layer_out: bfloat16 [4096, 768], P(('dp', 'tensor'))
- grad_tokens: float32 [4096, 768], P(('dp', 'tensor'))
- grad_w_query: float32 [768, 768], P('dp', 'tensor')
- grad_b_query: float32 [768], replicated
- grad_w_key: float32 [768, 768], P('dp', 'tensor')
- grad_b_key: float32 [768], replicated
- grad_w_value: float32 [768, 768], P('dp', 'tensor')
- grad_b_value: float32 [768], replicated
- grad_w_out: float32 [768, 768], P('tensor', 'dp')
- grad_b_out: float32 [768], replicated
- grad_gain_mixer: float32 [768], replicated
- grad_shift_mixer: float32 [768], replicated
- grad_w_up: float32 [768, 3072], P('dp', 'tensor')
- grad_b_up: float32 [3072], replicated
- grad_w_down: float32 [3072, 768], P('tensor', 'dp')
- grad_b_down: float32 [768], replicated
- grad_gain_feed: float32 [768], replicated
- grad_shift_feed: float32 [768], replicated
Inputs may be any that keep to these rules, and one draw needn't show every extreme that they name: `segment_ids`: ids never fall along a row of 512 tokens; each document (a run of equal ids) has 1 to 256 tokens, and some document has exactly 256.
All inputs are finite; a program needn't handle non-finite values.
Results may differ from a plain program's by a relative error of at most 0.017.
Values may be sent and summed in bfloat16 or wider, within the bound.
A program may use at most 64 MiB of HBM per device.

v0:
```python
from functools import partial
import math

import jax
import jax.numpy as jnp
from jax import lax
from jax.sharding import PartitionSpec as P

HD = 64


ln_eps = 1e-12


def layer_norm(values, gain_vec, shift_vec):
    average = jnp.mean(values, axis=-1, keepdims=True)
    centered = values - average
    variance = jnp.mean(centered * centered, axis=-1, keepdims=True)
    return centered * lax.rsqrt(variance + ln_eps) * gain_vec + shift_vec


def exact_gelu(values):
    return jax.nn.gelu(values, approximate=False)


def rotary_tables(segment_rows, head_size):
    seq_count, length = segment_rows.shape
    places = lax.broadcasted_iota(jnp.int32, (seq_count, length), 1)
    earlier = jnp.concatenate(
        [jnp.full((seq_count, 1), -1, jnp.int32), segment_rows[:, :-1]], axis=1
    )
    starts_at = lax.cummax(jnp.where(segment_rows != earlier, places, 0), axis=1)
    position = (places - starts_at).astype(jnp.float32)
    half_size = head_size // 2
    frequency = jnp.exp(jnp.arange(half_size, dtype=jnp.float32) * (-math.log(10000.0) / half_size))
    angles = position[:, :, None] * frequency
    cosine = jnp.concatenate([jnp.cos(angles), jnp.cos(angles)], axis=-1)
    sine = jnp.concatenate([jnp.sin(angles), jnp.sin(angles)], axis=-1)
    return (cosine, sine)


def rotate(values, cosine, sine):
    half_size = values.shape[-1] // 2
    rotated = jnp.concatenate([-values[..., half_size:], values[..., :half_size]], axis=-1)
    return values * cosine[:, :, None, :] + rotated * sine[:, :, None, :]


def rotate_back(grads_in, cosine, sine):
    half_size = grads_in.shape[-1] // 2
    moved = grads_in * sine[:, :, None, :]
    turned = jnp.concatenate([moved[..., half_size:], -moved[..., :half_size]], axis=-1)
    return grads_in * cosine[:, :, None, :] + turned


def project(rows_in, weight, bias):
    return jnp.dot(rows_in, weight, preferred_element_type=jnp.float32) + bias.astype(jnp.float32)


def contract_rows(left_side, right_side):
    return lax.dot_general(
        left_side, right_side, (((0,), (0,)), ((), ())), preferred_element_type=jnp.float32
    )


def times_transposed(left_side, right_side):
    return lax.dot_general(
        left_side, right_side, (((1,), (1,)), ((), ())), preferred_element_type=jnp.float32
    )


def rows_times(left_side, right_side):
    return jnp.dot(left_side, right_side, preferred_element_type=jnp.float32)


def rows_against(left_side, right_side):
    return times_transposed(left_side, right_side)


def input_terms(grad_query, grad_key, grad_value, w_query, w_key, w_value):
    summed = rows_against(grad_query, w_query)
    summed = summed + rows_against(grad_key, w_key)
    return summed + rows_against(grad_value, w_value)


def attend(score_scale, inputs):
    query_blk, key_blk, value_blk, segment_row = inputs
    same_doc = segment_row[:, None] == segment_row[None, :]
    scores = (
        jnp.einsum("qhd,khd->hqk", query_blk, key_blk, preferred_element_type=jnp.float32)
        * score_scale
    )
    scores = jnp.where(same_doc[None], scores, -1e30)
    row_max = jnp.max(scores, axis=-1, keepdims=True)
    weights_exp = jnp.exp(scores - row_max)
    row_total = jnp.sum(weights_exp, axis=-1, keepdims=True)
    attention = (weights_exp / row_total).astype(jnp.bfloat16)
    heads = jnp.einsum("hqk,khd->qhd", attention, value_blk, preferred_element_type=jnp.float32)
    return (heads, row_max[..., 0] + jnp.log(row_total[..., 0]))


def attend_back(score_scale, inputs):
    query_blk, key_blk, value_blk, segment_row, log_total, grad_heads = inputs
    same_doc = segment_row[:, None] == segment_row[None, :]
    scores = (
        jnp.einsum("qhd,khd->hqk", query_blk, key_blk, preferred_element_type=jnp.float32)
        * score_scale
    )
    scores = jnp.where(same_doc[None], scores, -1e30)
    attention = jnp.exp(scores - log_total[..., None])
    grad_attention = jnp.einsum(
        "qhd,khd->hqk", grad_heads, value_blk, preferred_element_type=jnp.float32
    )
    row_dot = jnp.sum(grad_attention * attention, axis=-1, keepdims=True)
    grad_scores = (attention * (grad_attention - row_dot)).astype(jnp.bfloat16)
    grad_value = jnp.einsum(
        "hqk,qhd->khd",
        attention.astype(jnp.bfloat16),
        grad_heads,
        preferred_element_type=jnp.float32,
    ).astype(jnp.bfloat16)
    grad_query = (
        jnp.einsum("hqk,khd->qhd", grad_scores, key_blk, preferred_element_type=jnp.float32)
        * score_scale
    )
    grad_key = (
        jnp.einsum("hqk,qhd->khd", grad_scores, query_blk, preferred_element_type=jnp.float32)
        * score_scale
    )
    return (grad_query, grad_key, grad_value)


def on_device(
    tokens,
    segment_ids,
    w_query,
    b_query,
    w_key,
    b_key,
    w_value,
    b_value,
    w_out,
    b_out,
    gain_mixer,
    shift_mixer,
    w_up,
    b_up,
    w_down,
    b_down,
    gain_feed,
    shift_feed,
    cotangent,
):
    seq_count, length = segment_ids.shape
    local_width = w_query.shape[1]
    local_heads = local_width // HD
    all_rows = seq_count * length
    score_scale = HD ** (-0.5)
    head_shape = (seq_count, length, local_heads, HD)
    gathered = lax.all_gather(tokens, "tensor", axis=0, tiled=True)
    query_pre = project(gathered, w_query, b_query)
    key_pre = project(gathered, w_key, b_key)
    value_low = project(gathered, w_value, b_value).astype(jnp.bfloat16).reshape(head_shape)
    cosine, sine = rotary_tables(segment_ids, HD)
    query_low = rotate(query_pre.reshape(head_shape), cosine, sine).astype(jnp.bfloat16)
    key_low = rotate(key_pre.reshape(head_shape), cosine, sine).astype(jnp.bfloat16)
    heads, log_total = lax.map(
        partial(attend, score_scale), (query_low, key_low, value_low, segment_ids)
    )
    head_rows = heads.reshape(all_rows, local_width).astype(jnp.bfloat16)
    mixed = lax.psum_scatter(
        rows_times(head_rows, w_out), "tensor", scatter_dimension=0, tiled=True
    )
    first_in = tokens.astype(jnp.float32) + mixed + b_out.astype(jnp.float32)
    normed, norm_mixer_pull = jax.vjp(
        layer_norm, first_in, gain_mixer.astype(jnp.float32), shift_mixer.astype(jnp.float32)
    )
    feed_in = lax.all_gather(normed.astype(jnp.bfloat16), "tensor", axis=0, tiled=True)
    hidden_pre = project(feed_in, w_up, b_up)
    activated, gelu_pull = jax.vjp(exact_gelu, hidden_pre)
    act_low = activated.astype(jnp.bfloat16)
    feed_out = lax.psum_scatter(
        rows_times(act_low, w_down), "tensor", scatter_dimension=0, tiled=True
    )
    second_in = normed + feed_out + b_down.astype(jnp.float32)
    result, norm_feed_pull = jax.vjp(
        layer_norm, second_in, gain_feed.astype(jnp.float32), shift_feed.astype(jnp.float32)
    )
    grad_second, grad_gain_feed, grad_shift_feed = norm_feed_pull(cotangent.astype(jnp.float32))
    grad_feed_all = lax.all_gather(grad_second.astype(jnp.bfloat16), "tensor", axis=0, tiled=True)
    grad_w_down = contract_rows(act_low, grad_feed_all)
    grad_act = times_transposed(grad_feed_all, w_down)
    (grad_hidden,) = gelu_pull(grad_act)
    grad_hidden_low = grad_hidden.astype(jnp.bfloat16)
    grad_w_up = contract_rows(feed_in, grad_hidden_low)
    feed_back = lax.psum_scatter(
        rows_against(grad_hidden_low, w_up), "tensor", scatter_dimension=0, tiled=True
    )
    grad_normed = grad_second + feed_back
    grad_first, grad_gain_mixer, grad_shift_mixer = norm_mixer_pull(grad_normed)
    grad_mixer_all = lax.all_gather(grad_first.astype(jnp.bfloat16), "tensor", axis=0, tiled=True)
    grad_w_out = contract_rows(head_rows, grad_mixer_all)
    grad_heads = times_transposed(grad_mixer_all, w_out).astype(jnp.bfloat16).reshape(head_shape)
    grad_query, grad_key, grad_value = lax.map(
        partial(attend_back, score_scale),
        (query_low, key_low, value_low, segment_ids, log_total, grad_heads),
    )
    grad_query_low = (
        rotate_back(grad_query, cosine, sine).reshape(all_rows, local_width).astype(jnp.bfloat16)
    )
    grad_key_low = (
        rotate_back(grad_key, cosine, sine).reshape(all_rows, local_width).astype(jnp.bfloat16)
    )
    grad_value_low = grad_value.reshape(all_rows, local_width)
    grad_w_query = contract_rows(gathered, grad_query_low)
    grad_w_key = contract_rows(gathered, grad_key_low)
    grad_w_value = contract_rows(gathered, grad_value_low)
    input_back = lax.psum_scatter(
        input_terms(grad_query_low, grad_key_low, grad_value_low, w_query, w_key, w_value).astype(
            jnp.bfloat16
        ),
        "tensor",
        scatter_dimension=0,
        tiled=True,
    ).astype(jnp.float32)
    grad_tokens = grad_first + input_back
    sum_query, sum_key, sum_value, sum_out, sum_up, sum_down = (
        lax.psum_scatter(grad_w_query, "dp", scatter_dimension=0, tiled=True),
        lax.psum_scatter(grad_w_key, "dp", scatter_dimension=0, tiled=True),
        lax.psum_scatter(grad_w_value, "dp", scatter_dimension=0, tiled=True),
        lax.psum_scatter(grad_w_out, "dp", scatter_dimension=1, tiled=True),
        lax.psum_scatter(grad_w_up, "dp", scatter_dimension=0, tiled=True),
        lax.psum_scatter(grad_w_down, "dp", scatter_dimension=1, tiled=True),
    )
    tensor_place = lax.axis_index("tensor")

    def place_piece(piece_sum, full_size):
        offset = tensor_place * piece_sum.shape[0]
        return lax.dynamic_update_slice(jnp.zeros((full_size,), jnp.float32), piece_sum, (offset,))

    model_width = tokens.shape[1]
    bias_query = place_piece(jnp.sum(grad_query_low, axis=0, dtype=jnp.float32), model_width)
    bias_key = place_piece(jnp.sum(grad_key_low, axis=0, dtype=jnp.float32), model_width)
    bias_value = place_piece(jnp.sum(grad_value_low, axis=0, dtype=jnp.float32), model_width)
    bias_up = place_piece(
        jnp.sum(grad_hidden_low, axis=0, dtype=jnp.float32), w_up.shape[1] * lax.axis_size("tensor")
    )
    bias_out = jnp.sum(grad_first, axis=0)
    bias_down = jnp.sum(grad_second, axis=0)
    vectors = lax.psum(
        (
            bias_query,
            bias_key,
            bias_value,
            bias_out,
            grad_gain_mixer,
            grad_shift_mixer,
            bias_up,
            bias_down,
            grad_gain_feed,
            grad_shift_feed,
        ),
        ("dp", "tensor"),
    )
    return (
        result.astype(jnp.bfloat16),
        grad_tokens,
        sum_query,
        vectors[0],
        sum_key,
        vectors[1],
        sum_value,
        vectors[2],
        sum_out,
        vectors[3],
        vectors[4],
        vectors[5],
        sum_up,
        vectors[6],
        sum_down,
        vectors[7],
        vectors[8],
        vectors[9],
    )


def solution(mesh):
    in_specs = (
        P(("dp", "tensor"), None),
        P("dp", None),
        P(None, "tensor"),
        P("tensor"),
        P(None, "tensor"),
        P("tensor"),
        P(None, "tensor"),
        P("tensor"),
        P("tensor", None),
        P(),
        P(),
        P(),
        P(None, "tensor"),
        P("tensor"),
        P("tensor", None),
        P(),
        P(),
        P(),
        P(("dp", "tensor"), None),
    )
    out_specs = (
        P(("dp", "tensor"), None),
        P(("dp", "tensor"), None),
        P("dp", "tensor"),
        P(),
        P("dp", "tensor"),
        P(),
        P("dp", "tensor"),
        P(),
        P("tensor", "dp"),
        P(),
        P(),
        P(),
        P("dp", "tensor"),
        P(),
        P("tensor", "dp"),
        P(),
        P(),
        P(),
    )
    return jax.shard_map(
        on_device, mesh=mesh, in_specs=in_specs, out_specs=out_specs, check_vma=False
    )
```

profile of v0, /device:TPU:1, one launch (start us, length us, event | category | flops | bytes accessed | tf_op | source)
XLA Modules:
  0.0 504.9 jit_solution(17240226687160521350)
XLA Ops:
  12.0 18.2 %all_gather.12 = bf16[512,768]{1,0:T(8,128)(2,1)S(1)} all-gather(bf16[128,768]{1,0:T(8,128)(2,1)} %param.19), channel_id=1, replica_groups=mesh['dp'=8,'tensor'=4] {'tensor'}, dimensions={0}, use_global_device_ids=true | all-gather | bytes 983040 | tf_op jit(solution)/shard_map/all_gather | solution.py:159
  36.6 1.6 fusion.44
  38.3 37.1 %reduce-scatter.19.cloned.1.call-done = f32[128,768]{1,0:T(8,128)} async-done(((f32[512,768]{1,0:T(8,128)}), f32[128,768]{1,0:T(8,128)}) %reduce-scatter.19.cloned.1.call-update) | async-done | bytes 393232 | tf_op jit(solution)/shard_map/reduce_scatter | solution.py:170
  77.0 15.6 %all_gather.13 = bf16[512,768]{1,0:T(8,128)(2,1)S(1)} all-gather(bf16[128,768]{1,0:T(8,128)(2,1)S(1)} %fusion.27), channel_id=1, replica_groups=mesh['dp'=8,'tensor'=4] {'tensor'}, dimensions={0}, use_global_device_ids=true | all-gather | bytes 983040 | tf_op jit(solution)/shard_map/all_gather | solution.py:177
  92.5 5.5 %multiply_convert_fusion.1 = (bf16[512,768]{1,0:T(8,128)(2,1)S(1)}, f32[512,768]{1,0:T(8,128)}, f32[512,768]{1,0:T(8,128)}) fusion(f32[768]{0:T(1024)S(1)} %convert_element_type.164, bf16[512,768]{1,0:T(8,128)(2,1)S(1)} %all_gather.13, bf16[768,768]{1,0:T(8,128)(2,1)S(1)} %copy-done), kind=kOutput, calls=%fused_computation.15 | convolution fusion | flops 629932032 | bytes 5901312 | tf_op jit(solution)/shard_map/dot_general | solution.py:56
  99.0 1.9 fusion.45
  102.2 36.0 %reduce-scatter.21.cloned.1.call-done = f32[128,768]{1,0:T(8,128)} async-done(((f32[512,768]{1,0:T(8,128)}), f32[128,768]{1,0:T(8,128)}) %reduce-scatter.21.cloned.1.call-update) | async-done | bytes 393232 | tf_op jit(solution)/shard_map/reduce_scatter | solution.py:181
  138.3 1.4 fusion.40
  140.7 1.9 fusion.39
  143.2 15.5 %all_gather.14 = bf16[512,768]{1,0:T(8,128)(2,1)S(1)} all-gather(bf16[128,768]{1,0:T(8,128)(2,1)S(1)} %get-tuple-element.158), channel_id=1, replica_groups=mesh['dp'=8,'tensor'=4] {'tensor'}, dimensions={0}, use_global_device_ids=true | all-gather | bytes 983040 | tf_op jit(solution)/shard_map/all_gather | solution.py:189
  158.8 1.8 convert_reduce_fusion
  161.5 2.0 fusion.46
  163.5 1.7 broadcast_multiply_fusion
  165.9 34.8 %reduce-scatter.23.cloned.1.call-done = f32[128,768]{1,0:T(8,128)} async-done(((f32[512,768]{1,0:T(8,128)}), f32[128,768]{1,0:T(8,128)}) %reduce-scatter.23.cloned.1.call-update) | async-done | bytes 393232 | tf_op jit(solution)/shard_map/reduce_scatter | solution.py:195
  200.8 1.9 multiply_reduce_fusion.1
  203.6 15.7 %all_gather.15 = bf16[512,768]{1,0:T(8,128)(2,1)S(1)} all-gather(bf16[128,768]{1,0:T(8,128)(2,1)S(1)} %get-tuple-element.160), channel_id=1, replica_groups=mesh['dp'=8,'tensor'=4] {'tensor'}, dimensions={0}, use_global_device_ids=true | all-gather | bytes 983040 | tf_op jit(solution)/shard_map/all_gather | solution.py:200
  219.7 1.4 convolution_bitcast_fusion
  221.1 2.7 multiply_reduce_fusion
  227.0 1.2 multiply_bitcast_fusion
  231.1 1.3 convert_reduce_fusion.2
  232.4 1.3 add_convert_fusion
  233.8 3.7 fusion.50
  237.6 3.4 fusion.49
  244.6 1.2 copy.64
  247.1 43.2 %all-reduce = (f32[768]{0:T(1024)}, f32[768]{0:T(1024)}, f32[768]{0:T(1024)}, f32[768]{0:T(1024)}, f32[768]{0:T(1024)}, /*index=5*/f32[768]{0:T(1024)}, f32[3072...) all-reduce(f32[768]{0:T(1024)S(1)} %dynamic_update_slice.25, ...), channel_id=1, replica_groups=mesh['dp'=8,'tensor'=4] {'dp','tensor'}, use_global_device_ids=true, to_apply=%region_19.20 | all-reduce | flops 9984 | bytes 79872 | tf_op jit(solution)/shard_map/psum | solution.py:249
  290.3 1.6 copy.69
  291.9 1.8 convert_add_fusion
  293.7 41.8 %reduce-scatter.29.cloned.1.call-done = f32[768,96]{0,1:T(8,128)} async-done(((f32[768,768]{0,1:T(8,128)}), f32[768,96]{0,1:T(8,128)}) %reduce-scatter.29.cloned.1.call-update) | async-done | bytes 294928 | tf_op jit(solution)/shard_map/reduce_scatter | solution.py:232
  335.5 46.8 %reduce-scatter.27.cloned.1.call-done = f32[96,768]{1,0:T(8,128)} async-done(((f32[768,768]{1,0:T(8,128)}), f32[96,768]{1,0:T(8,128)}) %reduce-scatter.27.cloned.1.call-update) | async-done | bytes 294928 | tf_op jit(solution)/shard_map/reduce_scatter | solution.py:231
  382.3 38.4 %reduce-scatter.35.cloned.1.call-done = f32[96,192]{1,0:T(8,128)} async-done(((f32[768,192]{1,0:T(8,128)}), f32[96,192]{1,0:T(8,128)}) %reduce-scatter.35.cloned.1.call-update) | async-done | bytes 73744
  420.7 38.8 %reduce-scatter.31.cloned.1.call-done = f32[96,192]{1,0:T(8,128)} async-done(((f32[768,192]{1,0:T(8,128)}), f32[96,192]{1,0:T(8,128)}) %reduce-scatter.31.cloned.1.call-update) | async-done | bytes 73744
  459.5 38.6 %reduce-scatter.33.cloned.1.call-done = f32[96,192]{1,0:T(8,128)} async-done(((f32[768,192]{1,0:T(8,128)}), f32[96,192]{1,0:T(8,128)}) %reduce-scatter.33.cloned.1.call-update) | async-done | bytes 73744
  (225 shorter events, 30.2 us)
Async XLA Ops:
  7.2 85.4 %copy-start = (bf16[768,768]{1,0:T(8,128)(2,1)S(1)}, bf16[768,768]{1,0:T(8,128)(2,1)}, u32[]{:S(2)}) copy-start(bf16[768,768]{1,0:T(8,128)(2,1)} %param.31) | copy-start | bytes 3538948
  7.2 24.0 %copy-start.31 = (bf16[768,192]{0,1:T(8,128)(2,1)S(1)}, bf16[768,192]{0,1:T(8,128)(2,1)}, u32[]{:S(2)}) copy-start(bf16[768,192]{0,1:T(8,128)(2,1)} %param.25) | copy-start | bytes 884740
  7.2 24.4 %copy-start.21 = (bf16[768,192]{0,1:T(8,128)(2,1)S(1)}, bf16[768,192]{0,1:T(8,128)(2,1)}, u32[]{:S(2)}) copy-start(bf16[768,192]{0,1:T(8,128)(2,1)} %param.23) | copy-start | bytes 884740
  7.2 68.2 %reduce-scatter.19.cloned.1.call-start = ((), (), s32[]{:S(2)}) async-start(), calls=%async_computation.10 | async-start | bytes 1966080 | tf_op jit(solution)/shard_map/reduce_scatter | solution.py:170
  36.6 38.9 %copy-start.24 = (bf16[128,768]{1,0:T(8,128)(2,1)S(1)}, bf16[128,768]{1,0:T(8,128)(2,1)}, u32[]{:S(2)}) copy-start(bf16[128,768]{1,0:T(8,128)(2,1)} %param.19) | copy-start | bytes 589828
  38.2 100.1 %reduce-scatter.21.cloned.1.call-start = ((), (), s32[]{:S(2)}) async-start(), calls=%async_computation.11 | async-start | bytes 1966080 | tf_op jit(solution)/shard_map/reduce_scatter | solution.py:181
  76.6 61.7 %copy-start.42 = (f32[128]{0:T(128)}, f32[128]{0:T(128)S(1)}, u32[]{:S(2)}) copy-start(f32[128]{0:T(128)S(1)} %broadcast_multiply_fusion.3) | copy-start | bytes 1540
  76.8 21.2 %copy-start.60 = (f32[128]{0:T(128)}, f32[128]{0:T(128)S(1)}, u32[]{:S(2)}) copy-start(f32[128]{0:T(128)S(1)} %multiply_reduce_fusion.4) | copy-start | bytes 1540
  76.8 61.5 %copy-start.44 = (f32[128]{0:T(128)}, f32[128]{0:T(128)S(1)}, u32[]{:S(2)}) copy-start(f32[128]{0:T(128)S(1)} %fusion.34) | copy-start | bytes 1540
  92.5 6.4 %copy-start.62 = (bf16[768,768]{1,0:T(8,128)(2,1)S(1)}, bf16[768,768]{1,0:T(8,128)(2,1)}, u32[]{:S(2)}) copy-start(bf16[768,768]{1,0:T(8,128)(2,1)} %param.33) | copy-start | bytes 3538948
  100.9 38.9 %copy-start.23 = (bf16[128,768]{1,0:T(8,128)(2,1)S(1)}, bf16[128,768]{1,0:T(8,128)(2,1)}, u32[]{:S(2)}) copy-start(bf16[128,768]{1,0:T(8,128)(2,1)} %param.37) | copy-start | bytes 589828
  101.0 99.8 %reduce-scatter.23.cloned.1.call-start = ((), (), s32[]{:S(2)}) async-start(), calls=%async_computation.12 | async-start | bytes 1966080 | tf_op jit(solution)/shard_map/reduce_scatter | solution.py:195
  138.3 20.5 %copy-start.65 = (f32[512,768]{1,0:T(8,128)S(1)}, f32[512,768]{1,0:T(8,128)}, u32[]{:S(2)}) copy-start(f32[512,768]{1,0:T(8,128)} %get-tuple-element.179) | copy-start | bytes 4718596
  139.9 18.9 %copy-start.63 = (bf16[768,768]{1,0:T(8,128)(2,1)S(1)}, bf16[768,768]{1,0:T(8,128)(2,1)}, u32[]{:S(2)}) copy-start(bf16[768,768]{1,0:T(8,128)(2,1)} %param.33) | copy-start | bytes 3538948
  139.9 18.9 %copy-start.64 = (f32[512,768]{1,0:T(8,128)S(1)}, f32[512,768]{1,0:T(8,128)}, u32[]{:S(2)}) copy-start(f32[512,768]{1,0:T(8,128)} %get-tuple-element.153) | copy-start | bytes 4718596
  142.5 18.0 %copy-start.59 = (f32[128]{0:T(128)}, f32[128]{0:T(128)S(1)}, u32[]{:S(2)}) copy-start(f32[128]{0:T(128)S(1)} %negate_multiply_fusion.2) | copy-start | bytes 1540
  163.5 126.8 %reduce-scatter.37.cloned.1.call-start = ((), (), s32[]{:S(2)}) async-start(), calls=%async_computation.19 | async-start | bytes 884736
  202.7 16.6 %copy-start.18 = (bf16[192,768]{1,0:T(8,128)(2,1)S(1)}, bf16[192,768]{1,0:T(8,128)(2,1)}, u32[]{:S(2)}) copy-start(bf16[192,768]{1,0:T(8,128)(2,1)} %param.27) | copy-start | bytes 884740
  203.0 16.7 %copy-start.27 = (bf16[3,64,512]{2,1,0:T(8,128)(2,1)S(1)}, bf16[3,64,512]{2,1,0:T(8,128)(2,1)}, u32[]{:S(2)}) copy-start(bf16[3,64,512]{2,1,0:T(8,128)(2,1)} %copy-done.26) | copy-start | bytes 589828
  219.7 4.1 copy-start.7
  221.1 2.8 copy-start.2
  226.9 65.0 %reduce-scatter.25.cloned.1.call-start = ((), (), s32[]{:S(2)}) async-start(), calls=%async_computation.13 | async-start | bytes 983040 | tf_op jit(solution)/shard_map/reduce_scatter | solution.py:217
  233.8 101.7 %reduce-scatter.29.cloned.1.call-start = ((), (), s32[]{:S(2)}) async-start(), calls=%async_computation.15 | async-start | bytes 2654208 | tf_op jit(solution)/shard_map/reduce_scatter | solution.py:232
  237.5 144.7 %reduce-scatter.27.cloned.1.call-start = ((), (), s32[]{:S(2)}) async-start(), calls=%async_computation.14 | async-start | bytes 2654208 | tf_op jit(solution)/shard_map/reduce_scatter | solution.py:231
  241.0 179.7 %reduce-scatter.35.cloned.1.call-start = ((), (), s32[]{:S(2)}) async-start(), calls=%async_computation.18 | async-start | bytes 884736
  242.5 216.9 %reduce-scatter.31.cloned.1.call-start = ((), (), s32[]{:S(2)}) async-start(), calls=%async_computation.16 | async-start | bytes 884736
  244.2 2.9 copy-start.37
  244.2 2.9 copy-start.38
  244.2 2.9 copy-start.39
  244.2 2.9 copy-start.40
  244.2 253.8 %reduce-scatter.33.cloned.1.call-start = ((), (), s32[]{:S(2)}) async-start(), calls=%async_computation.17 | async-start | bytes 884736
  244.6 47.3 %copy-start.51 = (f32[128]{0:T(128)S(1)}, f32[128]{0:T(128)}, u32[]{:S(2)}) copy-start(f32[128]{0:T(128)} %copy-done.50) | copy-start | bytes 1540
  (44 other events, 62.3 us)
Sparse Core Ops, SparseCore 0:
  38.3 37.0 reduce-scatter.18
  101.1 37.1 reduce-scatter.20
  163.6 37.1 reduce-scatter.22
  227.0 36.8 reduce-scatter.36
  266.1 22.9 reduce-scatter.24
  292.9 42.5 reduce-scatter.28
  339.8 42.4 reduce-scatter.26
  386.0 34.6 reduce-scatter.34
  424.4 34.9 reduce-scatter.30
  463.0 34.9 reduce-scatter.32
where the time goes:
time: 507 us; the launch traced here: 505 us
  waiting for transfers between devices  313 us (62%)
  blocking collectives  108 us (21%)
  matrix products  33.1 us (7%)
  other arithmetic  21.8 us (4%)
  between operations  15 us (3%)
  local copies, waits for them, and re-layouts  14 us (3%)
    unnamed x14, waiting for transfers between devices  116 us
    reduce_scatter x1, waiting for transfers between devices, on_device(): lax.psum_scatter(grad_w_up, 'dp', scatter_dimension=0, tiled=True)  46.8 us
    psum x1, blocking collectives, on_device(): lax.psum((bias_query, bias_key, bias_value, bias_out, grad_gain_mixer, gr...  43.2 us
    reduce_scatter x1, waiting for transfers between devices, on_device(): lax.psum_scatter(grad_w_down, 'dp', scatter_dimension=1, tiled=True)  41.8 us
    reduce_scatter x1, waiting for transfers between devices, on_device(): lax.psum_scatter(rows_times(head_rows, w_out), 'tensor', scatter_dimensio...  37.1 us
    reduce_scatter x1, waiting for transfers between devices, on_device(): lax.psum_scatter(rows_times(act_low, w_down), 'tensor', scatter_dimension...  36 us
    reduce_scatter x1, waiting for transfers between devices, on_device(): lax.psum_scatter(rows_against(grad_hidden_low, w_up), 'tensor', scatter_d...  34.8 us
    all_gather x1, blocking collectives, on_device(): gathered = lax.all_gather(tokens, 'tensor', axis=0, tiled=True)  18.2 us
  transfers between devices with their start and end apart: 10, of which 8 were waited for; matrix products, arithmetic and copies ran while one was open for 5% of the time, Pallas kernels for 0%

commit v1 on v0

v1 whole, which is shorter than its diff:
```python
from functools import partial
import math

import jax
import jax.numpy as jnp
from jax import lax
from jax.experimental import pallas as pl
from jax.experimental.pallas import tpu as pltpu
from jax.sharding import PartitionSpec as P

HD = 64
MESH = pl.DeviceIdType.MESH
F32 = jnp.float32
BF16 = jnp.bfloat16
LN_EPS = 1e-12
B_QKV, B_UP, B_OUT, G_MIX, S_MIX, B_DOWN, G_FEED, S_FEED = range(8)
DOWN, UP, OUT, QKV = range(4)


def nn(left, right):
    return lax.dot_general(left, right, (((1,), (0,)), ((), ())), preferred_element_type=F32)


def nt(left, right):
    return lax.dot_general(left, right, (((1,), (1,)), ((), ())), preferred_element_type=F32)


def norm_stats(values):
    centered = values - jnp.mean(values, axis=-1, keepdims=True)
    factor = lax.rsqrt(jnp.mean(centered * centered, axis=-1, keepdims=True) + LN_EPS)
    return centered * factor, factor


def norm_back(grads, normalized, factor, gain):
    scaled = grads * gain
    first = jnp.mean(scaled, axis=-1, keepdims=True)
    second = jnp.mean(scaled * normalized, axis=-1, keepdims=True)
    return factor * (scaled - first - normalized * second)


def copy_to(src, dst, send, recv, device):
    return pltpu.make_async_remote_copy(
        src_ref=src, dst_ref=dst, send_sem=send, recv_sem=recv, device_id=device,
        device_id_type=MESH,
    )


def layer_kernel(
    tight,
    tokens, cotangent, small, w_query, w_key, w_value, w_out, w_up, w_down,
    result_o, grad_o, sums_a, sums_b, vec_o,
    x_all, h_all, g2_all, g1_all, x_t, h_t, g2_t, g1_t,
    parts, landed, passed,
    small_v, cot_v, land, staged, wqkv, wo, wu, wd,
    seg_cols, cos_t, sin_t,
    qkv_s, k2_s, probs, probs_low, ds_s, o_s, act, dgelu, dz_s, do_s, dqkv_s,
    q_t, do_t, dk_t, dv_t, h_own, g_own, own_part,
    grads, grads_in, grads_sum, vec, vec_in, vec_col,
    ag_s, ag_r, rs_s, rs_r, sw_s, sw_r, wx_s, wx_r, dx_s, dx_r, dz_sem_s, dz_sem_r,
    vx_s, vx_r, vc_s, vc_r, out_s, out_r, loc,
):
    grad_pieces = grads
    dp, ten = lax.axis_index("dp"), lax.axis_index("tensor")
    low = lax.rem(ten, 2)
    if tight:
        col, core, half = dp // 2, lax.rem(dp, 2), ten // 2
        slot = low + 2 * core
        mate_slot = low + 2 * (1 - core)
        far_slot = 1 - low + 2 * core
        last_slot = 1 - low + 2 * (1 - core)
        mate = {"dp": col * 2 + 1 - core, "tensor": ten}
        far = {"dp": dp, "tensor": ten + 1 - 2 * low}
        other = lax.rem(ten + 2, 4)
        partner = {"dp": col * 2 + 1 - core, "tensor": other}
        across = {"dp": dp, "tensor": other}
        cols = [{"dp": lax.rem(col + j, 4) * 2 + core, "tensor": ten} for j in (1, 2, 3)]
        home = core == half
        away = core != half
    else:
        slot = ten
        mate_slot = ten + 1 - 2 * low
        far_slot = lax.rem(ten + 2, 4)
        last_slot = 3 - ten
        mate = {"dp": dp, "tensor": mate_slot}
        far = {"dp": dp, "tensor": far_slot}

    def all_column():
        for dz in (1, 2, 3):
            yield {"dp": dp, "tensor": lax.rem(ten + dz, 4)}
        for dz in (0, 1, 2, 3):
            yield {"dp": col * 2 + 1 - core, "tensor": lax.rem(ten + dz, 4)}

    rows = x_all.shape[1]
    length = 4 * rows

    def local(src, dst, sem):
        return pltpu.make_async_copy(src, dst, sem)

    raw = [local(w, land.at[i], loc.at[i]) for i, w in enumerate((w_query, w_key, w_value))]
    for copy in raw:
        copy.start()

    to_small = local(small, small_v, sw_r.at[0])
    to_tokens = local(tokens, x_all.at[slot], sw_r.at[1])
    to_cot = local(cotangent, cot_v, sw_r.at[2])
    wo_rows = w_out.shape[0]
    to_out = local(w_out, wo.at[pl.ds(0, wo_rows)], loc.at[3])
    to_up = local(w_up, wu, loc.at[4])
    to_down = local(w_down, wd, loc.at[5])

    def load_own():
        for copy in (to_small, to_tokens, to_out, to_up, to_down, to_cot):
            copy.start()

    if tight:
        pl.when(home)(load_own)
    else:
        load_own()

    barrier = pltpu.get_barrier_semaphore()
    met = list(all_column()) + cols if tight else [mate, far]
    for device in met:
        pl.semaphore_signal(barrier, inc=1, device_id=device, device_id_type=MESH)
    zeros_low = jnp.zeros((wo.shape[0] - wo_rows, wo.shape[1]), BF16)
    wo[wo_rows:, :] = zeros_low
    pl.semaphore_wait(barrier, len(met))

    def assemble(dst, take):
        parts3 = [land[i, take, :] for i in range(3)]
        for i in range(3):
            dst[:, i * 128:(i + 1) * 128] = parts3[i][:, :128]
        dst[:, 384:512] = jnp.concatenate([parts3[0][:, 128:], parts3[1][:, 128:]], axis=1)
        dst[:, 512:] = jnp.concatenate(
            [parts3[2][:, 128:], jnp.zeros_like(parts3[2][:, 128:])], axis=1
        )

    quarter = wqkv.shape[0] // 4
    wo_quarter = wo_rows // 4

    def swap_weight(i):
        size = wo_quarter if i == OUT else quarter
        take = pl.ds(col * size, size)
        dst = (wd, wu, wo, wqkv)[i].at[take]
        src = (w_down, w_up, w_out, None)[i]
        src = staged if src is None else src.at[take]
        return copy_to(src, dst, sw_s.at[3 + i], sw_r.at[3 + i], partner)

    def spread(i, j):
        size = wo_quarter if i == OUT else quarter
        ref = (wd, wu, wo, wqkv)[i].at[pl.ds(col * size, size)]
        return copy_to(ref, ref, wx_s.at[i, j], wx_r.at[i, j], cols[j])

    def spread_in(i, j):
        size = wo_quarter if i == OUT else quarter
        ref = (wd, wu, wo, wqkv)[i].at[pl.ds(lax.rem(col + 3 - j, 4) * size, size)]
        return copy_to(ref, ref, wx_s.at[i, j], wx_r.at[i, j], cols[j])

    def swap_arrays():
        return (
            copy_to(small, small_v, sw_s.at[0], sw_r.at[0], partner),
            copy_to(tokens, x_all.at[mate_slot], sw_s.at[1], sw_r.at[1], partner),
            copy_to(cotangent, cot_v, sw_s.at[2], sw_r.at[2], partner),
        )

    if tight:
        @pl.when(away)
        def _():
            first = swap_arrays()
            first[0].start()
            first[1].start()
            for copy in raw:
                copy.wait()
            assemble(staged, pl.ds(col * quarter, quarter))
            for i in (QKV, OUT, UP, DOWN):
                swap_weight(i).start()
            first[2].start()

        @pl.when(home)
        def _():
            for copy in raw:
                copy.wait()
            assemble(wqkv, slice(None))
    else:
        for copy in raw:
            copy.wait()
        assemble(wqkv, slice(None))

    def ag_own(i, buf):
        copy_to(buf.at[slot], buf.at[slot], ag_s.at[i, 0], ag_r.at[i, 0], mate).start()
        copy_to(buf.at[slot], buf.at[slot], ag_s.at[i, 1], ag_r.at[i, 1], far).start()

    def ag_mate(i, buf):
        ref = buf.at[mate_slot]
        copy_to(ref, ref, ag_s.at[i, 0], ag_r.at[i, 0], mate).wait_recv()

    def ag_far(i, buf):
        ref = buf.at[far_slot]
        copy_to(ref, ref, ag_s.at[i, 1], ag_r.at[i, 1], far).wait_recv()
        copy_to(ref, ref, ag_s.at[i, 2], ag_r.at[i, 2], mate).start()

    def ag_last(i, buf):
        ref = buf.at[last_slot]
        copy_to(ref, ref, ag_s.at[i, 2], ag_r.at[i, 2], mate).wait_recv()

    def ag_done(i, buf):
        copy_to(buf.at[slot], buf.at[slot], ag_s.at[i, 0], ag_r.at[i, 0], mate).wait_send()
        copy_to(buf.at[slot], buf.at[slot], ag_s.at[i, 1], ag_r.at[i, 1], far).wait_send()
        ref = buf.at[far_slot]
        copy_to(ref, ref, ag_s.at[i, 2], ag_r.at[i, 2], mate).wait_send()

    def rs_copy(i, j):
        src = (parts.at[i, 0], parts.at[i, 1], passed.at[i])[j]
        return copy_to(
            src, landed.at[i, j], rs_s.at[i, j], rs_r.at[i, j], far if j == 2 else mate
        )

    def reduce_scatter(i, piece):
        parts[i, 0] = piece(last_slot).astype(BF16)
        rs_copy(i, 0).start()
        parts[i, 1] = piece(mate_slot).astype(BF16)
        rs_copy(i, 1).start()
        own_part[...] = piece(far_slot)
        rs_copy(i, 0).wait_recv()
        passed[i] = (own_part[...] + landed[i, 0].astype(F32)).astype(BF16)
        rs_copy(i, 2).start()
        own_part[...] = piece(slot)

    def reduced(i):
        rs_copy(i, 1).wait_recv()
        rs_copy(i, 2).wait_recv()
        return own_part[...] + landed[i, 1].astype(F32) + landed[i, 2].astype(F32)

    to_small.wait()
    to_tokens.wait()
    ag_own(0, x_all)

    seg_row = small_v[8:9, :length]
    seg_cols[...] = jnp.transpose(jnp.broadcast_to(seg_row, (128, length)))
    segs = seg_cols[...]
    place = lax.broadcasted_iota(jnp.int32, (length, 128), 0).astype(F32)
    start = jnp.zeros((length, 128), F32)
    for s in range(4):
        before = jnp.sum(jnp.where(seg_row < s, 1.0, 0.0), axis=1, keepdims=True)
        start = jnp.where(segs == s, before, start)
    lane = lax.broadcasted_iota(jnp.int32, (1, 128), 1)
    frequency = jnp.exp(lax.rem(lane, 32).astype(F32) * (-math.log(10000.0) / 32))
    angle = (place - start) * frequency
    sign = jnp.where(lax.rem(lane, 64) < 32, -1.0, 1.0)
    cos_t[...] = jnp.cos(angle)
    sin_t[...] = jnp.sin(angle) * sign

    if tight:
        @pl.when(away)
        def _():
            for i in (QKV, OUT, UP, DOWN):
                swap_weight(i).wait_recv()
                for j in range(3):
                    spread(i, j).start()
                if i == QKV:
                    for j in range(3):
                        spread_in(i, j).wait_recv()

    def take(s):
        return pl.ds(pl.multiple_of(s * rows, rows), rows)

    low_lane = lane < 64

    def turn(values):
        return jnp.where(
            lax.rem(lane, 64) < 32, pltpu.roll(values, 96, 1), pltpu.roll(values, 32, 1)
        )

    def project_rows(s):
        here = take(s)
        x = x_all[s]
        x_t[:, here] = jnp.transpose(x)
        pre = nn(x, wqkv[...]) + small_v[B_QKV:B_QKV + 1, :640]
        cosine, sine = cos_t[here, :], sin_t[here, :]

        def rot(block):
            return block * cosine + turn(block) * sine

        scale = HD ** (-0.5)
        query, key, mixed = rot(pre[:, :128]), rot(pre[:, 128:256]), rot(pre[:, 384:512])
        qkv_s[here, 0:128] = (query.astype(BF16) * scale).astype(BF16)
        qkv_s[here, 128:256] = key.astype(BF16)
        qkv_s[here, 256:384] = pre[:, 256:384].astype(BF16)
        qkv_s[here, 384:512] = (jnp.where(low_lane, mixed, 0.0).astype(BF16) * scale).astype(BF16)
        qkv_s[here, 512:640] = pre[:, 512:640].astype(BF16)
        k2_s[here, :] = jnp.where(low_lane, pltpu.roll(mixed, 64, 1), 0.0).astype(BF16)

    project_rows(slot)
    ag_mate(0, x_all)
    project_rows(mate_slot)
    ag_far(0, x_all)
    project_rows(far_slot)
    ag_last(0, x_all)
    project_rows(last_slot)

    def masked(block, head):
        if head == 2:
            return block
        keep = low_lane if head == 0 else ~low_lane
        return jnp.where(keep, block, jnp.zeros_like(block))

    def attend(s, carry):
        here = take(s)
        same = seg_cols[here, 0:1] == seg_row
        outs = []
        for head in range(3):
            q_at, v_at = (0, 256) if head < 2 else (384, 512)
            query = masked(qkv_s[here, q_at:q_at + 128], head)
            keys = qkv_s[:, 128:256] if head < 2 else k2_s[...]
            scores = jnp.where(same, nt(query, keys), -1e30)
            scores = jnp.exp(scores - jnp.max(scores, axis=1, keepdims=True))
            weight = scores / jnp.sum(scores, axis=1, keepdims=True)
            probs[head, here, :] = weight
            weight_low = weight.astype(BF16)
            probs_low[head, here, :] = weight_low
            outs.append(nn(weight_low, qkv_s[:, v_at:v_at + 128]))
        o_s[here, 0:128] = jnp.where(low_lane, outs[0], outs[1]).astype(BF16)
        o_s[here, 128:256] = outs[2].astype(BF16)
        return carry

    lax.fori_loop(0, 4, attend, 0)

    if tight:
        @pl.when(home)
        def _():
            to_out.wait()

        @pl.when(away)
        def _():
            for j in range(3):
                spread_in(OUT, j).wait_recv()
    else:
        to_out.wait()

    reduce_scatter(0, lambda s: nn(o_s[take(s), :], wo[...]))
    first_in = reduced(0) + x_all[slot].astype(F32) + small_v[B_OUT:B_OUT + 1, :]
    normal1, factor1 = norm_stats(first_in)
    normed = normal1 * small_v[G_MIX:G_MIX + 1, :] + small_v[S_MIX:S_MIX + 1, :]
    h_own[0] = normed
    h_own[1] = normal1
    h_all[slot] = normed.astype(BF16)
    ag_own(1, h_all)

    if tight:
        @pl.when(home)
        def _():
            to_up.wait()
            to_down.wait()

        @pl.when(away)
        def _():
            for i in (UP, DOWN):
                for j in range(3):
                    spread_in(i, j).wait_recv()
    else:
        to_up.wait()
        to_down.wait()

    def feed(s):
        here = take(s)
        h = h_all[s]
        h_t[:, here] = jnp.transpose(h)
        z = nn(h, wu[...]) + small_v[B_UP:B_UP + 1, :]
        phi = 0.5 * (1.0 + lax.erf(z * (2.0 ** -0.5)))
        act[here, :] = (z * phi).astype(BF16)
        dgelu[here, :] = phi + z * (jnp.exp(-0.5 * z * z) * (1.0 / math.sqrt(2.0 * math.pi)))

    feed(slot)
    ag_mate(1, h_all)
    feed(mate_slot)
    ag_far(1, h_all)
    feed(far_slot)
    ag_last(1, h_all)
    feed(last_slot)
    reduce_scatter(1, lambda s: nn(act[take(s), :], wd[...]))
    second_in = reduced(1) + h_own[0] + small_v[B_DOWN:B_DOWN + 1, :]
    normal2, factor2 = norm_stats(second_in)
    out_rows = normal2 * small_v[G_FEED:G_FEED + 1, :] + small_v[S_FEED:S_FEED + 1, :]
    parts[4, 0] = out_rows.astype(BF16)

    def hand_out(i, src, dst):
        keep = local(src, dst, out_r.at[i])
        if not tight:
            keep.start()
            return
        pl.when(home)(keep.start)
        pl.when(away)(copy_to(src, dst, out_s.at[i], out_r.at[i], partner).start)

    hand_out(0, parts.at[4, 0], result_o)
    to_cot.wait()
    dy = cot_v[...].astype(F32)
    grad2 = norm_back(dy, normal2, factor2, small_v[G_FEED:G_FEED + 1, :])
    vec[3:4, :] = jnp.sum(grad2, axis=0, keepdims=True)
    vec[4:5, :] = jnp.sum(dy * normal2, axis=0, keepdims=True)
    vec[5:6, :] = jnp.sum(dy, axis=0, keepdims=True)
    g_own[0] = grad2
    g2_all[slot] = grad2.astype(BF16)
    ag_own(2, g2_all)

    def feed_back(s):
        here = take(s)
        g = g2_all[s]
        g2_t[:, here] = jnp.transpose(g)
        dz_s[here, :] = (nt(g, wd[...]) * dgelu[here, :]).astype(BF16)

    feed_back(slot)
    ag_mate(2, g2_all)
    feed_back(mate_slot)
    ag_far(2, g2_all)
    feed_back(far_slot)
    ag_last(2, g2_all)
    feed_back(last_slot)
    reduce_scatter(2, lambda s: nt(dz_s[take(s), :], wu[...]))

    def weight_grad(i, left, right):
        width = right.shape[1]
        size = left.shape[0] // 4

        def step(q, carry):
            at = pl.ds(pl.multiple_of(q * size, size), size)
            grad_pieces[i][q] = nn(left[at, :], right[...]).astype(BF16)
            return carry

        lax.fori_loop(0, 4, step, 0)
        if tight:
            for j in range(3):
                to = lax.rem(col + 1 + j, 4)
                copy_to(
                    grad_pieces[i].at[to], grads_in[i].at[j], dx_s.at[i, j], dx_r.at[i, j], cols[j]
                ).start()

    def grads_land(i):
        for j in range(3):
            to = lax.rem(col + 1 + j, 4)
            copy_to(
                grad_pieces[i].at[to], grads_in[i].at[j], dx_s.at[i, j], dx_r.at[i, j], cols[j]
            ).wait_recv()
        total = grad_pieces[i][col].astype(F32)
        for j in range(3):
            total = total + grads_in[i][j].astype(F32)
        grads_sum[i][...] = total.astype(BF16).reshape(grads_sum[i].shape)

        @pl.when(home)
        def _():
            keep_sum(i).start()
            mate_sum(i).start()

        @pl.when(away)
        def _():
            for copy in away_sums(i):
                copy.start()

    def keep_sum(i):
        return local(grads_sum[i].at[core], sums_a[i], dz_sem_r.at[i, 0])

    def mate_sum(i):
        return copy_to(
            grads_sum[i].at[1 - core], sums_a[i], dz_sem_s.at[i, 0], dz_sem_r.at[i, 0], mate
        )

    def away_sums(i):
        return (
            copy_to(
                grads_sum[i].at[core], sums_b[i], dz_sem_s.at[i, 0], dz_sem_r.at[i, 1], across
            ),
            copy_to(
                grads_sum[i].at[1 - core], sums_b[i], dz_sem_s.at[i, 1], dz_sem_r.at[i, 1], partner
            ),
        )

    weight_grad(DOWN, g2_t, act)
    weight_grad(UP, h_t, dz_s)
    vec[6:7, :] = jnp.sum(dz_s[...].astype(F32), axis=0, keepdims=True)

    dh = reduced(2) + g_own[0]
    normal1 = h_own[1]
    grad1 = norm_back(dh, normal1, factor1, small_v[G_MIX:G_MIX + 1, :])
    vec[0:1, :] = jnp.sum(grad1, axis=0, keepdims=True)
    vec[1:2, :] = jnp.sum(dh * normal1, axis=0, keepdims=True)
    vec[2:3, :] = jnp.sum(dh, axis=0, keepdims=True)
    g_own[1] = grad1
    g1_all[slot] = grad1.astype(BF16)
    ag_own(3, g1_all)

    def heads_back(s):
        here = take(s)
        g = g1_all[s]
        g1_t[:, here] = jnp.transpose(g)
        do_s[here, :] = nt(g, wo[...]).astype(BF16)

    heads_back(slot)
    ag_mate(3, g1_all)
    heads_back(mate_slot)
    ag_far(3, g1_all)
    heads_back(far_slot)
    ag_last(3, g1_all)
    heads_back(last_slot)
    weight_grad(OUT, g1_t, o_s)

    q_t[0:128, :] = jnp.transpose(qkv_s[:, 0:128])
    q_t[128:256, :] = jnp.transpose(qkv_s[:, 384:512])
    do_t[0:128, :] = jnp.transpose(do_s[:, 0:128])
    do_t[128:256, :] = jnp.transpose(do_s[:, 128:256])

    def back(values, here):
        return values * cos_t[here, :] - turn(values) * sin_t[here, :]

    def attend_back(s, carry):
        here = take(s)
        outs = []
        for head in range(3):
            v_at, o_at = (256, 0) if head < 2 else (512, 128)
            grad_o = masked(do_s[here, o_at:o_at + 128], head)
            grad_p = nt(grad_o, qkv_s[:, v_at:v_at + 128])
            weight = probs[head, here, :]
            dot = jnp.sum(grad_p * weight, axis=1, keepdims=True)
            ds = (weight * (grad_p - dot)).astype(BF16)
            ds_s[head, here, :] = ds
            keys = qkv_s[:, 128:256] if head < 2 else k2_s[...]
            outs.append(nn(ds, keys) * HD ** (-0.5))
        dqkv_s[here, 0:128] = back(jnp.where(low_lane, outs[0], outs[1]), here).astype(BF16)
        dqkv_s[here, 384:512] = back(outs[2], here).astype(BF16)
        return carry

    lax.fori_loop(0, 4, attend_back, 0)
    for head in range(3):
        at = slice(head * 64, head * 64 + 64)
        dk_t[at, :] = nn(q_t[at, :], ds_s[head])
        dv_t[at, :] = nn(do_t[at, :], probs_low[head])
    dk_t[192:, :] = jnp.zeros((64, length), F32)
    dv_t[192:, :] = jnp.zeros((64, length), F32)

    everything = slice(None)
    dqkv_s[:, 128:256] = back(jnp.transpose(dk_t[0:128, :]), everything).astype(BF16)
    key2 = back(jnp.transpose(dk_t[128:256, :]), everything)
    query2 = dqkv_s[:, 384:512].astype(F32)
    dqkv_s[:, 384:512] = jnp.where(low_lane, query2, pltpu.roll(key2, 64, 1)).astype(BF16)
    dqkv_s[:, 256:384] = jnp.transpose(dv_t[0:128, :]).astype(BF16)
    dqkv_s[:, 512:640] = jnp.transpose(dv_t[128:256, :]).astype(BF16)

    reduce_scatter(3, lambda s: nt(dqkv_s[take(s), :], wqkv[...]))
    weight_grad(QKV, x_t, dqkv_s)
    vec[7:8, 0:640] = jnp.sum(dqkv_s[...].astype(F32), axis=0, keepdims=True)
    vec[7:8, 640:] = jnp.zeros((1, vec.shape[1] - 640), F32)

    if tight:
        for j in range(3):
            copy_to(vec, vec_in.at[j], vx_s.at[j], vx_r.at[j], cols[j]).start()
        grads_land(DOWN)
        grads_land(UP)

    parts[4, 1] = (reduced(3) + g_own[1]).astype(BF16)
    hand_out(1, parts.at[4, 1], grad_o)

    if tight:
        for j in range(3):
            copy_to(vec, vec_in.at[j], vx_s.at[j], vx_r.at[j], cols[j]).wait_recv()
        mine = half * 4 + slot
        vec_col[mine] = vec[...] + vec_in[0] + vec_in[1] + vec_in[2]
        column = list(all_column())
        for j, device in enumerate(column):
            copy_to(vec_col.at[mine], vec_col.at[mine], vc_s.at[j], vc_r.at[j], device).start()
        grads_land(OUT)
        grads_land(QKV)

        sources = [(core, lax.rem(ten + 4 - dz, 4)) for dz in (1, 2, 3)]
        sources += [(1 - core, lax.rem(ten + 4 - dz, 4)) for dz in (0, 1, 2, 3)]
        for j, (core_j, ten_j) in enumerate(sources):
            at = (ten_j // 2) * 4 + lax.rem(ten_j, 2) + 2 * core_j
            ref = vec_col.at[at]
            copy_to(ref, ref, vc_s.at[j], vc_r.at[j], column[j]).wait_recv()
        keep = local(vec_col, vec_o, loc.at[6])
    else:
        keep = local(vec, vec_o, loc.at[6])
    keep.start()

    if not tight:
        outs = [local(grad_pieces[i], sums_a[i], dx_s.at[i, 0]) for i in range(4)]
        for copy in outs:
            copy.start()
        for copy in outs:
            copy.wait()
    local(parts.at[4, 0], result_o, out_r.at[0]).wait()
    local(parts.at[4, 1], grad_o, out_r.at[1]).wait()
    for i, buf in enumerate((x_all, h_all, g2_all, g1_all)):
        ag_done(i, buf)
        for j in range(3):
            rs_copy(i, j).wait_send()
    keep.wait()
    if tight:
        for i in range(4):
            keep_sum(i).wait()
            away_sums(i)[0].wait_recv()
            for j in range(3):
                to = lax.rem(col + 1 + j, 4)
                copy_to(
                    grad_pieces[i].at[to], grads_in[i].at[j], dx_s.at[i, j], dx_r.at[i, j], cols[j]
                ).wait_send()
        for j in range(3):
            copy_to(vec, vec_in.at[j], vx_s.at[j], vx_r.at[j], cols[j]).wait_send()
        for j, device in enumerate(column):
            copy_to(
                vec_col.at[mine], vec_col.at[mine], vc_s.at[j], vc_r.at[j], device
            ).wait_send()

        @pl.when(home)
        def _():
            for i in range(4):
                mate_sum(i).wait_send()

        @pl.when(away)
        def _():
            for i in range(4):
                for copy in away_sums(i):
                    copy.wait_send()
                for j in range(3):
                    spread(i, j).wait_send()
                swap_weight(i).wait_send()
            for copy in swap_arrays():
                copy.wait_send()
            copy_to(parts.at[4, 0], result_o, out_s.at[0], out_r.at[0], partner).wait_send()
            copy_to(parts.at[4, 1], grad_o, out_s.at[1], out_r.at[1], partner).wait_send()


def layer_call(tight, tokens, cotangent, small, w_query, w_key, w_value, w_out, w_up, w_down):
    rows, width = tokens.shape
    hidden = w_up.shape[1]
    length = 4 * rows
    heads_wide, qkv_wide = 256, 640
    widths = (hidden, hidden, heads_wide, qkv_wide)
    any_space = pl.BlockSpec(memory_space=pl.ANY)
    vmem = pl.BlockSpec(memory_space=pltpu.VMEM)
    slice_rows = width // 8
    if tight:
        sums = [jax.ShapeDtypeStruct((slice_rows, w), BF16) for w in widths]
        vec_shape = jax.ShapeDtypeStruct((8, 8, width), F32)
    else:
        sums = [jax.ShapeDtypeStruct((4, width // 4, w), BF16) for w in widths]
        vec_shape = jax.ShapeDtypeStruct((8, width), F32)
    sums_b = [jax.ShapeDtypeStruct((slice_rows, w), BF16) for w in widths]
    out_shape = (
        jax.ShapeDtypeStruct((rows, width), BF16),
        jax.ShapeDtypeStruct((rows, width), BF16),
        sums,
        sums_b,
        vec_shape,
    )
    V = pltpu.VMEM
    D = pltpu.SemaphoreType.DMA
    scratch = [
        *[V((4, rows, width), BF16)] * 4,
        *[V((width, length), BF16)] * 4,
        V((5, 2, rows, width), BF16), V((4, 3, rows, width), BF16), V((4, rows, width), BF16),
        V((16, width), F32), V((rows, width), BF16), V((3, width, 192), BF16),
        V((width // 4, qkv_wide), BF16), V((width, qkv_wide), BF16), V((heads_wide, width), BF16),
        V((width, hidden), BF16), V((hidden, width), BF16),
        V((length, 128), F32), V((length, 128), F32), V((length, 128), F32),
        V((length, qkv_wide), BF16), V((length, 128), BF16), V((3, length, length), F32),
        V((3, length, length), BF16), V((3, length, length), BF16), V((length, heads_wide), BF16),
        V((length, hidden), BF16), V((length, hidden), F32), V((length, hidden), BF16),
        V((length, heads_wide), BF16), V((length, qkv_wide), BF16),
        V((heads_wide, length), BF16), V((heads_wide, length), BF16),
        V((heads_wide, length), F32), V((heads_wide, length), F32),
        V((2, rows, width), F32), V((2, rows, width), F32), V((rows, width), F32),
        [V((4, width // 4, w), BF16) for w in widths],
        [V((3, width // 4, w), BF16) for w in widths],
        [V((2, width // 8, w), BF16) for w in widths],
        V((8, width), F32), V((3, 8, width), F32), V((8, 8, width), F32),
        D((4, 3)), D((4, 3)), D((4, 3)), D((4, 3)), D((7,)), D((7,)), D((4, 3)), D((4, 3)),
        D((4, 3)), D((4, 3)), D((4, 2)), D((4, 2)), D((3,)), D((3,)), D((7,)), D((7,)),
        D((2,)), D((2,)), D((7,)),
    ]
    return pl.pallas_call(
        partial(layer_kernel, tight),
        out_shape=out_shape,
        in_specs=[any_space] * 9,
        out_specs=jax.tree.map(lambda _: any_space, out_shape),
        scratch_shapes=scratch,
        compiler_params=pltpu.CompilerParams(
            collective_id=0, has_side_effects=True, vmem_limit_bytes=60 << 20
        ),
    )(tokens, cotangent, small, w_query, w_key, w_value, w_out, w_up, w_down)


def split_qkv(block):
    query = jnp.concatenate([block[..., :128], block[..., 384:448]], axis=-1)
    key = jnp.concatenate([block[..., 128:256], block[..., 448:512]], axis=-1)
    value = jnp.concatenate([block[..., 256:384], block[..., 512:576]], axis=-1)
    return query, key, value


def on_device(
    tight,
    tokens,
    segment_ids,
    w_query,
    b_query,
    w_key,
    b_key,
    w_value,
    b_value,
    w_out,
    b_out,
    gain_mixer,
    shift_mixer,
    w_up,
    b_up,
    w_down,
    b_down,
    gain_feed,
    shift_feed,
    cotangent,
):
    width = tokens.shape[1]
    vectors = [
        jnp.concatenate(
            [
                b_query[:128], b_key[:128], b_value[:128],
                b_query[128:], b_key[128:], b_value[128:],
                jnp.zeros((width - 576,), b_query.dtype),
            ]
        ),
        b_up, b_out, gain_mixer, shift_mixer, b_down, gain_feed, shift_feed,
    ]
    segment_row = jnp.pad(segment_ids[0].astype(F32), (0, width - segment_ids.shape[1]))
    small = jnp.concatenate(
        [
            jnp.stack(vectors).astype(F32),
            jnp.broadcast_to(segment_row[None], (8, width)),
        ]
    )
    result, grad_rows, sums_a, sums_b, vec = layer_call(
        tight, tokens, cotangent, small, w_query, w_key, w_value, w_out, w_up, w_down
    )
    grad_tokens = grad_rows.astype(F32)
    if tight:
        down, up, out, qkv = (
            a.astype(F32) + b.astype(F32) for a, b in zip(sums_a, sums_b)
        )
        totals = jnp.sum(vec, axis=0)
        by_slot = vec[:4] + vec[4:]
        bias_up = by_slot[:, 6].reshape(-1)
        biases = [b.reshape(-1) for b in split_qkv(by_slot[:, 7, :640])]
        sum_query, sum_key, sum_value = split_qkv(qkv)
        sum_out, sum_down, sum_up = out[:, :192].T, down.T, up
    else:
        flat = [a.reshape(width, a.shape[-1]).astype(F32) for a in sums_a]
        scatter = partial(lax.psum_scatter, axis_name="dp", scatter_dimension=0, tiled=True)
        sum_query, sum_key, sum_value = (scatter(b) for b in split_qkv(flat[QKV]))
        sum_out, sum_down = scatter(flat[OUT][:, :192]).T, scatter(flat[DOWN]).T
        sum_up = scatter(flat[UP])
        totals = lax.psum(vec, ("dp", "tensor"))
        by_slot = lax.all_gather(lax.psum(vec[6:], "dp"), "tensor")
        bias_up = by_slot[:, 0].reshape(-1)
        biases = [b.reshape(-1) for b in split_qkv(by_slot[:, 1, :640])]
    return (
        result,
        grad_tokens,
        sum_query,
        biases[0],
        sum_key,
        biases[1],
        sum_value,
        biases[2],
        sum_out,
        totals[0],
        totals[1],
        totals[2],
        sum_up,
        bias_up,
        sum_down,
        totals[3],
        totals[4],
        totals[5],
    )


def solution(mesh):
    in_specs = (
        P(("dp", "tensor"), None),
        P("dp", None),
        P(None, "tensor"),
        P("tensor"),
        P(None, "tensor"),
        P("tensor"),
        P(None, "tensor"),
        P("tensor"),
        P("tensor", None),
        P(),
        P(),
        P(),
        P(None, "tensor"),
        P("tensor"),
        P("tensor", None),
        P(),
        P(),
        P(),
        P(("dp", "tensor"), None),
    )
    out_specs = (
        P(("dp", "tensor"), None),
        P(("dp", "tensor"), None),
        P("dp", "tensor"),
        P(),
        P("dp", "tensor"),
        P(),
        P("dp", "tensor"),
        P(),
        P("tensor", "dp"),
        P(),
        P(),
        P(),
        P("dp", "tensor"),
        P(),
        P("tensor", "dp"),
        P(),
        P(),
        P(),
    )
    tight = mesh.shape["dp"] == 8
    return jax.shard_map(
        partial(on_device, tight), mesh=mesh, in_specs=in_specs, out_specs=out_specs,
        check_vma=False,
    )
```

time: 507 us -> 162 us (0.32)
  waiting for transfers between devices: 313 us -> 0 us
  Pallas kernels: 0 us -> 135 us
  blocking collectives: 108 us -> 0 us
  matrix products: 33.1 us -> 0 us
  other arithmetic: 21.8 us -> 7.12 us
  between operations: 15 us -> 0.78 us
    reduce_scatter x6 -> x0, waiting for transfers between devices: 197 us -> none  [the longest x1 46.8 us: on_device(): lax.psum_scatter(grad_w_up, 'dp', scatter_dimension=0, tiled=True)]
    pallas_call x0 -> x1, Pallas kernels: none -> 135 us  [layer_call(): pl.pallas_call(partial(layer_kernel, tight), out_shape=out_shape, in_spec...]
    unnamed x14 -> x0, waiting for transfers between devices: 116 us -> none
    all_gather x4 -> x0, blocking collectives: 65 us -> none  [the longest x1 18.2 us: on_device(): gathered = lax.all_gather(tokens, 'tensor', axis=0, tiled=True)]
    psum x1 -> x0, blocking collectives: 43.2 us -> none  [on_device(): lax.psum((bias_query, bias_key, bias_value, bias_out, grad_gain_mixer, gr...]
    dot_general x23 -> x0, matrix products: 31.7 us -> none  [the longest x5 8.03 us: contract_rows(): lax.dot_general(left_side, right_side, (((0,), (0,)), ((), ())), preferre...]
    reduce_sum x12 -> x1, other arithmetic: 9.66 us -> 0.99 us  [on_device(): totals = jnp.sum(vec, axis=0)]
    unnamed x136 -> x24, local copies, waits for them, and re-layouts: 12.5 us -> 6.13 us
  transfers between devices with their start and end apart: 10 -> 0, of which waited for: 8 -> 0; matrix products, arithmetic and copies ran while one was open for 5% -> 0% of each run, Pallas kernels for 0% -> 0%
where the time goes in v1:
time: 162 us
  Pallas kernels  135 us (83%)
  local copies, waits for them, and re-layouts  18.5 us (11%)
  other arithmetic  7.12 us (4%)
    pallas_call x1, Pallas kernels, layer_call(): pl.pallas_call(partial(layer_kernel, tight), out_shape=out_shape, in_spec...  135 us
    unnamed x24, local copies, waits for them, and re-layouts  6.13 us
    another operation x9, local copies, waits for them, and re-layouts, on_device(): jnp.stack(vectors).astype(F32)  4.85 us

profile of v1, /device:TPU:1, one launch (start us, length us, event | category | flops | bytes accessed | tf_op | source)
XLA Modules:
  0.0 161.5 jit_solution(8942247752744313701)
XLA Ops:
  0.7 0.7 slice.90
  1.4 0.7 slice.91
  2.0 0.7 slice.92
  2.7 2.1 %concatenate.24 = bf16[768]{0:T(1024)(128)(2,1)S(1)} concatenate(bf16[128]{0:T(256)(128)(2,1)} %bitcast.16, bf16[128]{0:T(256)(128)(2,1)} %bitcast.17, bf16[128]{0:T(256)(128)(2,1)} %bitcast.18, bf16[64]{0:T(256)(128)(2,1)S(1)} %slice.90, bf16[64]{0:T(256)(128)(2,1)S(1)} %slice.91, bf16[64]{0:T(256)(128)(2,1)S(1)} %slice.92, bf16[192]{0:T(256)(128)(2,1)S(1)} %broadcast_in_dim.4), dimensions={0} | concatenate | bytes 3072 | tf_op jit(solution)/shard_map/concatenate | solution.py:720
  4.8 0.7 convert_element_type.39
  5.5 0.7 stack.29
  6.2 0.7 stack.30
  6.8 0.7 stack.31
  7.5 0.7 stack.28
  8.2 0.7 stack.32
  8.9 0.7 stack.33
  9.6 0.7 stack.34
  10.3 0.6 pad_maximum_fusion.3.small
  11.0 1.9 %copy.37.w_query = bf16[768,192]{1,0:T(8,128)(2,1)} copy(bf16[768,192]{0,1:T(8,128)(2,1)} %param.21) | data formatting | bytes 589824 | tf_op args[2]
  12.8 1.9 %copy.38.w_key = bf16[768,192]{1,0:T(8,128)(2,1)} copy(bf16[768,192]{0,1:T(8,128)(2,1)} %param.23) | data formatting | bytes 589824 | tf_op args[4]
  14.7 0.9 copy.39.w_value
  15.6 135.1 %shard_map.322 = (bf16[128,768]{1,0:T(8,128)(2,1)}, bf16[128,768]{1,0:T(8,128)(2,1)}, bf16[96,768]{1,0:T(8,128)(2,1)}, bf16[96,768]{1,0:T(8,128)(2,1)}, bf16[96,...) custom-call(bf16[128,768]{1,0:T(8,128)(2,1)} %tokens.1, ...), custom_call_target="tpu_custom_call" | custom-call | tf_op jit(solution)/shard_map/pallas_call | solution.py:677
  150.8 1.0 reduce_sum.9
  151.7 1.0 slice_add_fusion
  152.7 0.6 slice_reduce_fusion
  153.4 0.6 slice.134
  154.1 0.7 reshape.49
  154.7 0.7 reshape.47
  155.4 0.7 reshape.48
  156.1 0.8 add_bitcast_fusion.1
  156.9 0.7 copy.40
  157.7 0.1 fusion.1
  157.8 0.6 pad_maximum_fusion.2
  158.5 0.7 pad_maximum_fusion
  159.2 0.8 convert_element_type.41
  160.0 0.9 add_bitcast_fusion
  160.8 0.7 copy.45
  (32 shorter events, 0.3 us)
Async XLA Ops:
  0.7 14.1 %copy-start = (bf16[768,192]{0,1:T(8,128)(2,1)S(1)}, bf16[768,192]{0,1:T(8,128)(2,1)}, u32[]{:S(2)}) copy-start(bf16[768,192]{0,1:T(8,128)(2,1)} %param.25) | copy-start | bytes 884740
  150.7 6.9 %copy-start.7 = (bf16[96,640]{1,0:T(8,128)(2,1)S(1)}, bf16[96,640]{1,0:T(8,128)(2,1)}, u32[]{:S(2)}) copy-start(bf16[96,640]{1,0:T(8,128)(2,1)} %get-tuple-element.31) | copy-start | bytes 368644
  150.7 6.9 %copy-start.8 = (bf16[96,640]{1,0:T(8,128)(2,1)S(1)}, bf16[96,640]{1,0:T(8,128)(2,1)}, u32[]{:S(2)}) copy-start(bf16[96,640]{1,0:T(8,128)(2,1)} %get-tuple-element.32) | copy-start | bytes 368644
  152.7 6.5 %copy-start.2 = (bf16[128,768]{1,0:T(8,128)(2,1)S(1)}, bf16[128,768]{1,0:T(8,128)(2,1)}, u32[]{:S(2)}) copy-start(bf16[128,768]{1,0:T(8,128)(2,1)} %get-tuple-element.30) | copy-start | bytes 589828
  157.7 2.3 %copy-start.3 = (bf16[96,768]{1,0:T(8,128)(2,1)S(1)}, bf16[96,768]{1,0:T(8,128)(2,1)}, u32[]{:S(2)}) copy-start(bf16[96,768]{1,0:T(8,128)(2,1)} %get-tuple-element.38) | copy-start | bytes 442372
  157.7 2.3 %copy-start.4 = (bf16[96,768]{1,0:T(8,128)(2,1)S(1)}, bf16[96,768]{1,0:T(8,128)(2,1)}, u32[]{:S(2)}) copy-start(bf16[96,768]{1,0:T(8,128)(2,1)} %get-tuple-element.36) | copy-start | bytes 442372
  157.7 2.3 %copy-start.5 = (bf16[96,768]{1,0:T(8,128)(2,1)S(1)}, bf16[96,768]{1,0:T(8,128)(2,1)}, u32[]{:S(2)}) copy-start(bf16[96,768]{1,0:T(8,128)(2,1)} %get-tuple-element.39) | copy-start | bytes 442372
  157.7 2.3 %copy-start.6 = (bf16[96,768]{1,0:T(8,128)(2,1)S(1)}, bf16[96,768]{1,0:T(8,128)(2,1)}, u32[]{:S(2)}) copy-start(bf16[96,768]{1,0:T(8,128)(2,1)} %get-tuple-element.37) | copy-start | bytes 442372
  157.8 3.0 %copy-start.1 = (bf16[128,768]{1,0:T(8,128)(2,1)S(1)}, bf16[128,768]{1,0:T(8,128)(2,1)}, u32[]{:S(2)}) copy-start(bf16[128,768]{1,0:T(8,128)(2,1)} %get-tuple-element.100) | copy-start | bytes 589828

commit v2 on v1

v2 whole, which is shorter than its diff:
```python
from functools import partial
import math

import jax
import jax.numpy as jnp
from jax import lax
from jax.experimental import pallas as pl
from jax.experimental.pallas import tpu as pltpu
from jax.sharding import PartitionSpec as P

HD = 64
MESH = pl.DeviceIdType.MESH
F32 = jnp.float32
BF16 = jnp.bfloat16
LN_EPS = 1e-12
B_QKV, B_UP, B_OUT, G_MIX, S_MIX, B_DOWN, G_FEED, S_FEED = range(8)
DOWN, UP, OUT, QKV = range(4)


def nn(left, right):
    return lax.dot_general(left, right, (((1,), (0,)), ((), ())), preferred_element_type=F32)


def nt(left, right):
    return lax.dot_general(left, right, (((1,), (1,)), ((), ())), preferred_element_type=F32)


def norm_stats(values):
    centered = values - jnp.mean(values, axis=-1, keepdims=True)
    factor = lax.rsqrt(jnp.mean(centered * centered, axis=-1, keepdims=True) + LN_EPS)
    return centered * factor, factor


def norm_back(grads, normalized, factor, gain):
    scaled = grads * gain
    first = jnp.mean(scaled, axis=-1, keepdims=True)
    second = jnp.mean(scaled * normalized, axis=-1, keepdims=True)
    return factor * (scaled - first - normalized * second)


def copy_to(src, dst, send, recv, device):
    return pltpu.make_async_remote_copy(
        src_ref=src, dst_ref=dst, send_sem=send, recv_sem=recv, device_id=device,
        device_id_type=MESH,
    )


def layer_kernel(
    tight,
    tokens, cotangent, wq_t, wk_t, wv_t, w_out, w_up, w_down,
    segment_ids, b_query, b_key, b_value, b_up, b_out, gain_mixer, shift_mixer, b_down,
    gain_feed, shift_feed,
    result_o, grad_o, sums_a, sums_b, vec_o, bias_o,
    x_all, h_all, g2_all, g1_all, x_t, h_t, g2_t, g1_t,
    part_last, part_mate, land_last, land_mate, land_far, passed, out_rows,
    small_own, small_v, cot_v, staged, wqkv, wo, wu, wd,
    seg_nat, seg_cols, cos_t, sin_t,
    qkv_s, k2_s, probs, probs_low, ds_s, o_s, act, dgelu, dz_s, do_s, dqkv_s,
    q_t, do_t, dk_t, dv_t, h_own, g_own, own_part,
    grads, first_in, second_in, grads_mid, grads_in, grads_sum,
    vec, vec_in, vec_col, bias, bias_in, bias_col,
    ag_s, ag_r, rs_s, rs_r, sw_s, sw_r, wx_s, wx_r, dx_s, dx_r, dq_s, dq_r, dz_sem_s, dz_sem_r,
    vx_s, vx_r, vc_s, vc_r, bx_s, bx_r, bc_s, bc_r, out_s, out_r, loc,
):
    dp, ten = lax.axis_index("dp"), lax.axis_index("tensor")
    low = lax.rem(ten, 2)
    if tight:
        col, core, half = dp // 2, lax.rem(dp, 2), ten // 2
        col_x, col_y = lax.rem(col, 2), col // 2
        slot = low + 2 * core
        mate_slot = low + 2 * (1 - core)
        far_slot = 1 - low + 2 * core
        last_slot = 1 - low + 2 * (1 - core)
        mate = {"dp": col * 2 + 1 - core, "tensor": ten}
        far = {"dp": dp, "tensor": ten + 1 - 2 * low}
        other = lax.rem(ten + 2, 4)
        partner = {"dp": col * 2 + 1 - core, "tensor": other}
        across = {"dp": dp, "tensor": other}
        cols = [{"dp": lax.rem(col + j, 4) * 2 + core, "tensor": ten} for j in (1, 2, 3)]
        next_x = {"dp": (col_y * 2 + 1 - col_x) * 2 + core, "tensor": ten}
        next_y = {"dp": ((1 - col_y) * 2 + col_x) * 2 + core, "tensor": ten}
        home = core == half
        away = core != half
        column = [{"dp": dp, "tensor": lax.rem(ten + dz, 4)} for dz in (1, 2, 3)]
        column += [
            {"dp": col * 2 + 1 - core, "tensor": lax.rem(ten + dz, 4)} for dz in (0, 1, 2, 3)
        ]
        met = column + cols
    else:
        slot = ten
        mate_slot = ten + 1 - 2 * low
        far_slot = lax.rem(ten + 2, 4)
        last_slot = 3 - ten
        mate = {"dp": dp, "tensor": mate_slot}
        far = {"dp": dp, "tensor": far_slot}
        met = [mate, far]

    rows, width = tokens.shape
    length = 4 * rows
    chunk = rows // 2
    units = ((0, 2 * rows), (2 * rows, rows), (3 * rows, rows))

    def local(src, dst, sem):
        return pltpu.make_async_copy(src, dst, sem)

    raw = []
    qkv_ref = staged if tight else wqkv
    for i, w in enumerate((wq_t, wk_t, wv_t)):
        raw.append((w.at[pl.ds(0, 128)], i * 128, 128))
        raw.append((w.at[pl.ds(128, 64)], 384 + i * 64, 64))

    def raw_copy(i, ref):
        src, at, size = raw[i]
        return local(src, ref.at[pl.ds(at, size)], loc.at[i])

    to_tokens = [
        local(tokens.at[pl.ds(c * chunk, chunk)], x_all.at[pl.ds(c * chunk, chunk)], sw_r.at[4 + c])
        for c in range(2)
    ]
    to_small = local(small_own, small_v, sw_r.at[0])
    to_cot = local(cotangent, cot_v, sw_r.at[11])
    wo_rows = w_out.shape[0]
    to_out = local(w_out, wo.at[pl.ds(0, wo_rows)], loc.at[6])
    to_up = local(w_up, wu, loc.at[7])
    to_down = local(w_down, wd, loc.at[8])

    def load_own():
        for copy in to_tokens:
            copy.start()
        for i in range(6):
            raw_copy(i, wqkv).start()
        for copy in (to_out, to_up, to_down, to_cot):
            copy.start()

    def stage_own():
        for i in range(6):
            raw_copy(i, staged).start()

    if tight:
        pl.when(home)(load_own)
        pl.when(away)(stage_own)
    else:
        load_own()

    barrier = pltpu.get_barrier_semaphore()
    for device in met:
        pl.semaphore_signal(barrier, inc=1, device_id=device, device_id_type=MESH)
    wo[wo_rows:, :] = jnp.zeros((wo.shape[0] - wo_rows, width), BF16)
    wqkv[576:, :] = jnp.zeros((wqkv.shape[0] - 576, width), BF16)

    def vector(ref):
        return ref[...].astype(F32).reshape(1, ref.shape[0])

    bq, bk, bv = vector(b_query), vector(b_key), vector(b_value)
    for i, b in enumerate((bq, bk, bv)):
        small_own[0:1, i * 128:(i + 1) * 128] = b[:, :128]
    small_own[0:1, 384:512] = jnp.concatenate([bq[:, 128:], bk[:, 128:]], axis=1)
    small_own[0:1, 512:640] = jnp.concatenate([bv[:, 128:], jnp.zeros((1, 64), F32)], axis=1)
    small_own[0:1, 640:] = jnp.zeros((1, width - 640), F32)
    for at, ref in (
        (B_UP, b_up), (B_OUT, b_out), (G_MIX, gain_mixer), (S_MIX, shift_mixer),
        (B_DOWN, b_down), (G_FEED, gain_feed), (S_FEED, shift_feed),
    ):
        small_own[at:at + 1, :] = vector(ref)
    small_own[8:16, :] = jnp.zeros((8, width), F32)
    small_own[8:9, :length] = segment_ids[...].astype(F32)
    pl.semaphore_wait(barrier, len(met))

    weight_items = {
        1: (wqkv, staged, 576, 0, 3), 2: (wqkv, staged, 576, 1, 3), 3: (wqkv, staged, 576, 2, 3),
        6: (wo, w_out, wo_rows, 0, 1),
        7: (wu, w_up, width, 0, 2), 8: (wu, w_up, width, 1, 2),
        9: (wd, w_down, width, 0, 2), 10: (wd, w_down, width, 1, 2),
    }
    item_rank = {item: i for i, item in enumerate(weight_items)}

    def item_rows(item, q):
        _, _, total, part, count = weight_items[item]
        size = total // 4 // count
        return pl.ds(q * (total // 4) + part * size, size)

    def swap(item):
        if item in weight_items:
            dst, src = weight_items[item][:2]
            at = item_rows(item, col)
            src, dst = src.at[at], dst.at[at]
        elif item == 0:
            src, dst = small_own, small_v
        elif item == 11:
            src, dst = cotangent, cot_v
        else:
            at = pl.ds((item - 4) * chunk, chunk)
            src, dst = tokens.at[at], x_all.at[at]
        return copy_to(src, dst, sw_s.at[item], sw_r.at[item], partner)

    def spread(item, j):
        ref = weight_items[item][0].at[item_rows(item, col)]
        rank = item_rank[item]
        return copy_to(ref, ref, wx_s.at[rank, j], wx_r.at[rank, j], cols[j])

    def spread_in(item, j):
        ref = weight_items[item][0].at[item_rows(item, lax.rem(col + 3 - j, 4))]
        rank = item_rank[item]
        return copy_to(ref, ref, wx_s.at[rank, j], wx_r.at[rank, j], cols[j])

    def relay(*items):
        if tight:
            @pl.when(away)
            def _():
                for item in items:
                    swap(item).wait_recv()
                    for j in range(3):
                        spread(item, j).start()

    def weights_ready(copies, *items):
        if not tight:
            for copy in copies:
                copy.wait()
            return

        @pl.when(home)
        def _():
            for copy in copies:
                copy.wait()

        @pl.when(away)
        def _():
            for item in items:
                for j in range(3):
                    spread_in(item, j).wait_recv()

    if tight:
        @pl.when(away)
        def _():
            swap(0).start()
            for i in range(6):
                raw_copy(i, staged).wait()
            for item in (1, 2, 3, 4, 5):
                swap(item).start()

        pl.when(home)(to_small.start)
    else:
        to_small.start()

    def at_own(c):
        return pl.ds(c * chunk, chunk)

    def at_mate(c):
        return pl.ds(rows + c * chunk, chunk)

    def at_far(c):
        return pl.ds(2 * rows + 2 * c * chunk, chunk)

    def at_last(c):
        return pl.ds(2 * rows + (2 * c + 1) * chunk, chunk)

    def gather_copy(i, buf, c, kind):
        src, dst, device = (
            (at_own(c), at_mate(c), mate), (at_own(c), at_far(c), far), (at_far(c), at_last(c), mate)
        )[kind]
        return copy_to(
            buf.at[src], buf.at[dst], ag_s.at[i, c, kind], ag_r.at[i, c, kind], device
        )

    def ag_own(i, buf, c):
        gather_copy(i, buf, c, 1).start()
        gather_copy(i, buf, c, 0).start()

    def ag_mate(i, buf):
        for c in range(2):
            gather_copy(i, buf, c, 0).wait_recv()

    def ag_unit(i, buf, c):
        gather_copy(i, buf, c, 1).wait_recv()
        gather_copy(i, buf, c, 2).start()
        gather_copy(i, buf, c, 2).wait_recv()

    def rs_copy(i, c, kind):
        src, dst, device = (
            (part_last.at[i, c], land_last.at[i, c], mate),
            (part_mate.at[i, c], land_mate.at[i, c], mate),
            (passed.at[i, c], land_far.at[i, c], far),
        )[kind]
        return copy_to(src, dst, rs_s.at[i, c, kind], rs_r.at[i, c, kind], device)

    def rs_unit(i, c, term):
        part_last[i, c] = term[chunk:].astype(BF16)
        rs_copy(i, c, 0).start()
        own_part[rows + c * chunk:rows + (c + 1) * chunk, :] = term[:chunk]

    def rs_pass(i, c):
        rs_copy(i, c, 0).wait_recv()
        term = own_part[rows + c * chunk:rows + (c + 1) * chunk, :]
        passed[i, c] = (term + land_last[i, c].astype(F32)).astype(BF16)
        rs_copy(i, c, 2).start()

    def rs_mate(i, term):
        for c in range(2):
            part_mate[i, c] = term[rows + c * chunk:rows + (c + 1) * chunk].astype(BF16)
            rs_copy(i, c, 1).start()
        own_part[0:rows, :] = term[:rows]

    def reduced(i, c):
        rs_copy(i, c, 1).wait_recv()
        rs_copy(i, c, 2).wait_recv()
        term = own_part[c * chunk:(c + 1) * chunk, :]
        return term + land_mate[i, c].astype(F32) + land_far[i, c].astype(F32)

    if not tight:
        for c in range(2):
            to_tokens[c].wait()
            ag_own(0, x_all, c)
    else:
        @pl.when(home)
        def _():
            for c in range(2):
                to_tokens[c].wait()
                ag_own(0, x_all, c)

    to_small.wait()
    seg_row = small_v[8:9, :length]
    seg_nat[...] = jnp.transpose(jnp.broadcast_to(seg_row, (128, length)))
    segs = seg_nat[...]
    place = lax.broadcasted_iota(jnp.int32, (length, 128), 0).astype(F32)
    start = jnp.zeros((length, 128), F32)
    for s in range(4):
        before = jnp.sum(jnp.where(seg_row < s, 1.0, 0.0), axis=1, keepdims=True)
        start = jnp.where(segs == s, before, start)
    cos_t[...] = place - start
    order = [(0, slot, 0), (1, slot, 1), (2, mate_slot, 0), (3, mate_slot, 1)]
    order += [(4, far_slot, 0), (5, last_slot, 0), (6, far_slot, 1), (7, last_slot, 1)]
    for to, from_slot, c in order:
        at = pl.ds(pl.multiple_of(from_slot * rows + c * chunk, chunk), chunk)
        seg_cols[to * chunk:(to + 1) * chunk, :] = seg_nat[at, :]
        sin_t[to * chunk:(to + 1) * chunk, :] = cos_t[at, :]
    lane = lax.broadcasted_iota(jnp.int32, (1, 128), 1)
    frequency = jnp.exp(lax.rem(lane, 32).astype(F32) * (-math.log(10000.0) / 32))
    sign = jnp.where(lax.rem(lane, 64) < 32, -1.0, 1.0)
    angle = sin_t[...] * frequency
    cos_t[...] = jnp.cos(angle)
    sin_t[...] = jnp.sin(angle) * sign
    seg_row = jnp.transpose(seg_cols[...])[0:1, :]

    if tight:
        @pl.when(away)
        def _():
            for item, follow in ((1, 6), (2, 7), (3, 8)):
                swap(item).wait_recv()
                for j in range(3):
                    spread(item, j).start()
                swap(follow).start()
            for c, follow in ((0, 9), (1, 10)):
                swap(4 + c).wait_recv()
                ag_own(0, x_all, c)
                swap(follow).start()
            swap(11).start()

    low_lane = lane < 64

    def turn(values):
        return jnp.where(
            lax.rem(lane, 64) < 32, pltpu.roll(values, 96, 1), pltpu.roll(values, 32, 1)
        )

    scale = HD ** (-0.5)

    def project_rows(lo, n):
        here = slice(lo, lo + n)
        x = x_all[here, :]
        pre = nt(x, wqkv[...]) + small_v[B_QKV:B_QKV + 1, :640]
        cosine, sine = cos_t[here, :], sin_t[here, :]

        def rot(block):
            return block * cosine + turn(block) * sine

        query, key, mixed = rot(pre[:, :128]), rot(pre[:, 128:256]), rot(pre[:, 384:512])
        qkv_s[here, 0:128] = (query.astype(BF16) * scale).astype(BF16)
        qkv_s[here, 128:256] = key.astype(BF16)
        qkv_s[here, 256:384] = pre[:, 256:384].astype(BF16)
        qkv_s[here, 384:512] = (jnp.where(low_lane, mixed, 0.0).astype(BF16) * scale).astype(BF16)
        qkv_s[here, 512:640] = pre[:, 512:640].astype(BF16)
        k2_s[here, :] = jnp.where(low_lane, pltpu.roll(mixed, 64, 1), 0.0).astype(BF16)
        x_t[:, here] = jnp.transpose(x)

    weights_ready([raw_copy(i, wqkv) for i in range(6)], 1, 2, 3)
    ag_mate(0, x_all)
    project_rows(*units[0])
    ag_unit(0, x_all, 0)
    project_rows(*units[1])
    ag_unit(0, x_all, 1)
    project_rows(*units[2])
    relay(6, 7)

    def masked(block, head):
        if head == 2:
            return block
        keep = low_lane if head == 0 else ~low_lane
        return jnp.where(keep, block, jnp.zeros_like(block))

    def attend(s, carry):
        here = pl.ds(pl.multiple_of(s * rows, rows), rows)
        same = seg_cols[here, 0:1] == seg_row
        outs = []
        for head in range(3):
            q_at, v_at = (0, 256) if head < 2 else (384, 512)
            query = masked(qkv_s[here, q_at:q_at + 128], head)
            keys = qkv_s[:, 128:256] if head < 2 else k2_s[...]
            scores = jnp.where(same, nt(query, keys), -1e30)
            scores = jnp.exp(scores - jnp.max(scores, axis=1, keepdims=True))
            weight = scores / jnp.sum(scores, axis=1, keepdims=True)
            probs[head, here, :] = weight
            weight_low = weight.astype(BF16)
            probs_low[head, here, :] = weight_low
            outs.append(nn(weight_low, qkv_s[:, v_at:v_at + 128]))
        o_s[here, 0:128] = jnp.where(low_lane, outs[0], outs[1]).astype(BF16)
        o_s[here, 128:256] = outs[2].astype(BF16)
        return carry

    def mix(lo, n):
        return nn(o_s[lo:lo + n, :], wo[...])

    attend(2, 0)
    weights_ready([to_out], 6)
    rs_unit(0, 0, mix(*units[1]))
    relay(8)
    attend(3, 0)
    rs_unit(0, 1, mix(*units[2]))
    rs_pass(0, 0)
    lax.fori_loop(0, 1, attend, 0)
    rs_pass(0, 1)
    relay(9)
    lax.fori_loop(1, 2, attend, 0)
    rs_mate(0, mix(*units[0]))
    factors = []

    def spot(c):
        return slice(c * chunk, (c + 1) * chunk)

    def row_of(at):
        return small_v[at:at + 1, :]

    for c in range(2):
        here = spot(c)
        into = reduced(0, c) + x_all[here, :].astype(F32) + row_of(B_OUT)
        normal1, factor1 = norm_stats(into)
        factors.append(factor1)
        normed = normal1 * row_of(G_MIX) + row_of(S_MIX)
        h_own[0, here, :] = normed
        h_own[1, here, :] = normal1
        h_all[here, :] = normed.astype(BF16)
        ag_own(1, h_all, c)
    relay(10)

    def feed(lo, n):
        here = slice(lo, lo + n)
        h = h_all[here, :]
        z = nn(h, wu[...]) + row_of(B_UP)
        phi = 0.5 * (1.0 + lax.erf(z * (2.0 ** -0.5)))
        act[here, :] = (z * phi).astype(BF16)
        dgelu[here, :] = phi + z * (jnp.exp(-0.5 * z * z) * (1.0 / math.sqrt(2.0 * math.pi)))

    def shrink(lo, n):
        return nn(act[lo:lo + n, :], wd[...])

    weights_ready([to_up], 7, 8)
    ag_mate(1, h_all)
    feed(*units[0])
    ag_unit(1, h_all, 0)
    feed(*units[1])
    weights_ready([to_down], 9, 10)
    rs_unit(1, 0, shrink(*units[1]))
    ag_unit(1, h_all, 1)
    rs_pass(1, 0)
    feed(*units[2])
    rs_unit(1, 1, shrink(*units[2]))
    rs_mate(1, shrink(*units[0]))
    rs_pass(1, 1)
    h_t[...] = jnp.transpose(h_all[...])

    def hand_out(i, src, dst, c):
        src, dst = src.at[pl.ds(c * chunk, chunk)], dst.at[pl.ds(c * chunk, chunk)]
        keep = local(src, dst, out_r.at[i, c])
        send = copy_to(src, dst, out_s.at[i, c], out_r.at[i, c], partner) if tight else None
        return keep, send

    def hand_start(*args):
        keep, send = hand_out(*args)
        if tight:
            pl.when(home)(keep.start)
            pl.when(away)(send.start)
        else:
            keep.start()

    to_cot.wait()
    sums = [0.0, 0.0, 0.0]
    for c in range(2):
        here = spot(c)
        into = reduced(1, c) + h_own[0, here, :] + row_of(B_DOWN)
        normal2, factor2 = norm_stats(into)
        dy = cot_v[here, :].astype(F32)
        grad2 = norm_back(dy, normal2, factor2, row_of(G_FEED))
        g_own[0, here, :] = grad2
        g2_all[here, :] = grad2.astype(BF16)
        ag_own(2, g2_all, c)
        out_rows[0, here, :] = (normal2 * row_of(G_FEED) + row_of(S_FEED)).astype(BF16)
        hand_start(0, out_rows.at[0], result_o, c)
        for i, term in enumerate((grad2, dy * normal2, dy)):
            sums[i] = sums[i] + jnp.sum(term, axis=0, keepdims=True)
    for i in range(3):
        vec[3 + i:4 + i, :] = sums[i]

    def feed_back(lo, n):
        here = slice(lo, lo + n)
        dz_s[here, :] = (nt(g2_all[here, :], wd[...]) * dgelu[here, :]).astype(BF16)

    def widen(lo, n):
        return nt(dz_s[lo:lo + n, :], wu[...])

    ag_mate(2, g2_all)
    feed_back(*units[0])
    ag_unit(2, g2_all, 0)
    feed_back(*units[1])
    rs_unit(2, 0, widen(*units[1]))
    ag_unit(2, g2_all, 1)
    rs_pass(2, 0)
    feed_back(*units[2])
    rs_unit(2, 1, widen(*units[2]))
    rs_mate(2, widen(*units[0]))
    rs_pass(2, 1)

    def weight_grad(i, left, right):
        quarter = width // 4

        def step(q, carry):
            at = pl.ds(pl.multiple_of(q * quarter, quarter), quarter)
            grads[i][q // 2, lax.rem(q, 2)] = nn(left[at, :], right[...]).astype(BF16)
            return carry

        lax.fori_loop(0, 4, step, 0)

    along_x = {DOWN: True, UP: False, OUT: True}

    def first_copy(i):
        if along_x[i]:
            src, device = grads[i].at[:, 1 - col_x], next_x
        else:
            src, device = grads[i].at[1 - col_y], next_y
        return copy_to(src, first_in[i], dx_s.at[i, 0], dx_r.at[i, 0], device)

    def second_copy(i):
        keep, device = (1 - col_y, next_y) if along_x[i] else (1 - col_x, next_x)
        return copy_to(
            grads_mid[i].at[keep], second_in[i], dx_s.at[i, 1], dx_r.at[i, 1], device
        )

    def first_land(i):
        if not tight:
            return
        first_copy(i).wait_recv()
        for j in range(2):
            own = grads[i][j, col_x] if along_x[i] else grads[i][col_y, j]
            grads_mid[i][j] = (own.astype(F32) + first_in[i][j].astype(F32)).astype(BF16)
        second_copy(i).start()

    def second_land(i):
        if not tight:
            return
        second_copy(i).wait_recv()
        own = grads_mid[i][col_y if along_x[i] else col_x]
        total = own.astype(F32) + second_in[i][...].astype(F32)
        finish_sum(i, total)

    def finish_sum(i, total):
        grads_sum[i][...] = total.astype(BF16).reshape(grads_sum[i].shape)

        @pl.when(home)
        def _():
            keep_sum(i).start()
            mate_sum(i).start()

        @pl.when(away)
        def _():
            for copy in away_sums(i):
                copy.start()

    def direct_copy(j):
        to = lax.rem(col + 1 + j, 4)
        return copy_to(
            grads[QKV].at[to // 2, lax.rem(to, 2)], grads_in.at[j], dq_s.at[j], dq_r.at[j], cols[j]
        )

    def keep_sum(i):
        return local(grads_sum[i].at[core], sums_a[i], dz_sem_r.at[i, 0])

    def mate_sum(i):
        return copy_to(
            grads_sum[i].at[1 - core], sums_a[i], dz_sem_s.at[i, 0], dz_sem_r.at[i, 0], mate
        )

    def away_sums(i):
        return (
            copy_to(
                grads_sum[i].at[core], sums_b[i], dz_sem_s.at[i, 0], dz_sem_r.at[i, 1], across
            ),
            copy_to(
                grads_sum[i].at[1 - core], sums_b[i], dz_sem_s.at[i, 1], dz_sem_r.at[i, 1], partner
            ),
        )

    def first_send(i):
        if tight:
            first_copy(i).start()

    g2_t[...] = jnp.transpose(g2_all[...])
    weight_grad(DOWN, g2_t, act)
    first_send(DOWN)
    weight_grad(UP, h_t, dz_s)
    first_send(UP)
    vec[6:7, :] = jnp.sum(dz_s[...].astype(F32), axis=0, keepdims=True)

    sums = [0.0, 0.0, 0.0]
    for c in range(2):
        here = spot(c)
        dh = reduced(2, c) + g_own[0, here, :]
        normal1 = h_own[1, here, :]
        grad1 = norm_back(dh, normal1, factors[c], row_of(G_MIX))
        g_own[1, here, :] = grad1
        g1_all[here, :] = grad1.astype(BF16)
        ag_own(3, g1_all, c)
        for i, term in enumerate((grad1, dh * normal1, dh)):
            sums[i] = sums[i] + jnp.sum(term, axis=0, keepdims=True)
    for i in range(3):
        vec[i:i + 1, :] = sums[i]
    vec[7:8, :] = jnp.zeros((1, width), F32)

    def vec_copy(j):
        return copy_to(vec, vec_in.at[j], vx_s.at[j], vx_r.at[j], cols[j])

    def bias_copy(j):
        return copy_to(bias, bias_in.at[j], bx_s.at[j], bx_r.at[j], cols[j])

    if tight:
        mine = half * 4 + slot
        for j in range(3):
            vec_copy(j).start()

    def column_out(j, ref, send, recv):
        return copy_to(ref.at[mine], ref.at[mine], send.at[j], recv.at[j], column[j])

    def column_in(j, ref, send, recv):
        core_j = core if j < 3 else 1 - core
        ten_j = lax.rem(ten + 3 - j, 4) if j < 3 else lax.rem(ten + 4 - (j - 3), 4)
        at = (ten_j // 2) * 4 + lax.rem(ten_j, 2) + 2 * core_j
        return copy_to(ref.at[at], ref.at[at], send.at[j], recv.at[j], column[j])

    def heads_back(lo, n):
        here = slice(lo, lo + n)
        do_s[here, :] = nt(g1_all[here, :], wo[...]).astype(BF16)

    def back(values, here):
        return values * cos_t[here, :] - turn(values) * sin_t[here, :]

    def attend_back(s, carry):
        here = pl.ds(pl.multiple_of(s * rows, rows), rows)
        outs = []
        for head in range(3):
            v_at, o_at = (256, 0) if head < 2 else (512, 128)
            grad_o = masked(do_s[here, o_at:o_at + 128], head)
            grad_p = nt(grad_o, qkv_s[:, v_at:v_at + 128])
            weight = probs[head, here, :]
            dot = jnp.sum(grad_p * weight, axis=1, keepdims=True)
            ds = (weight * (grad_p - dot)).astype(BF16)
            ds_s[head, here, :] = ds
            keys = qkv_s[:, 128:256] if head < 2 else k2_s[...]
            outs.append(nn(ds, keys) * scale)
        dqkv_s[here, 0:128] = back(jnp.where(low_lane, outs[0], outs[1]), here).astype(BF16)
        dqkv_s[here, 384:512] = back(outs[2], here).astype(BF16)
        return carry

    q_t[0:128, :] = jnp.transpose(qkv_s[:, 0:128])
    q_t[128:256, :] = jnp.transpose(qkv_s[:, 384:512])
    ag_mate(3, g1_all)
    heads_back(*units[0])
    lax.fori_loop(0, 2, attend_back, 0)
    ag_unit(3, g1_all, 0)
    heads_back(*units[1])
    first_land(DOWN)
    lax.fori_loop(2, 3, attend_back, 0)
    ag_unit(3, g1_all, 1)
    heads_back(*units[2])
    first_land(UP)
    lax.fori_loop(3, 4, attend_back, 0)
    g1_t[...] = jnp.transpose(g1_all[...])
    weight_grad(OUT, g1_t, o_s)
    first_send(OUT)
    do_t[0:128, :] = jnp.transpose(do_s[:, 0:128])
    do_t[128:256, :] = jnp.transpose(do_s[:, 128:256])
    for head in range(3):
        at = slice(head * 64, head * 64 + 64)
        dk_t[at, :] = nn(q_t[at, :], ds_s[head])
        dv_t[at, :] = nn(do_t[at, :], probs_low[head])
    dk_t[192:, :] = jnp.zeros((64, length), F32)
    dv_t[192:, :] = jnp.zeros((64, length), F32)

    everything = slice(None)
    dqkv_s[:, 128:256] = back(jnp.transpose(dk_t[0:128, :]), everything).astype(BF16)
    key2 = back(jnp.transpose(dk_t[128:256, :]), everything)
    query2 = dqkv_s[:, 384:512].astype(F32)
    dqkv_s[:, 384:512] = jnp.where(low_lane, query2, pltpu.roll(key2, 64, 1)).astype(BF16)
    dqkv_s[:, 256:384] = jnp.transpose(dv_t[0:128, :]).astype(BF16)
    dqkv_s[:, 512:640] = jnp.transpose(dv_t[128:256, :]).astype(BF16)

    weight_grad(QKV, x_t, dqkv_s)
    if tight:
        for j in range(3):
            direct_copy(j).start()

    def to_input(lo, n):
        return nn(dqkv_s[lo:lo + n, :], wqkv[...])

    rs_unit(3, 0, to_input(*units[1]))
    rs_unit(3, 1, to_input(*units[2]))
    rs_pass(3, 0)
    rs_pass(3, 1)
    rs_mate(3, to_input(*units[0]))
    total = jnp.sum(dqkv_s[...].astype(F32), axis=0, keepdims=True)
    bias[...] = jnp.zeros((8, 128), F32)
    for i in range(5):
        bias[i:i + 1, :] = total[:, i * 128:(i + 1) * 128]
    if tight:
        for j in range(3):
            bias_copy(j).start()
        second_land(DOWN)
        second_land(UP)
        for j in range(3):
            vec_copy(j).wait_recv()
        vec_col[mine] = vec[...] + vec_in[0] + vec_in[1] + vec_in[2]
        for j in range(7):
            column_out(j, vec_col, vc_s, vc_r).start()
        first_land(OUT)

    for c in range(2):
        here = spot(c)
        out_rows[1, here, :] = (reduced(3, c) + g_own[1, here, :]).astype(BF16)
        hand_start(1, out_rows.at[1], grad_o, c)

    if tight:
        for j in range(3):
            bias_copy(j).wait_recv()
        bias_col[mine] = bias[...] + bias_in[0] + bias_in[1] + bias_in[2]
        for j in range(7):
            column_out(j, bias_col, bc_s, bc_r).start()
        second_land(OUT)
        for j in range(3):
            direct_copy(j).wait_recv()
        total = grads[QKV][col_y, col_x].astype(F32)
        for j in range(3):
            total = total + grads_in[j].astype(F32)
        finish_sum(QKV, total)
        for j in range(7):
            column_in(j, vec_col, vc_s, vc_r).wait_recv()
            column_in(j, bias_col, bc_s, bc_r).wait_recv()
        keep = [local(vec_col, vec_o, loc.at[0]), local(bias_col, bias_o, loc.at[1])]
    else:
        keep = [local(vec, vec_o, loc.at[0]), local(bias, bias_o, loc.at[1])]
        keep += [local(grads[i], sums_a[i], loc.at[2 + i]) for i in range(4)]
    for copy in keep:
        copy.start()

    for i, dst in enumerate((result_o, grad_o)):
        for c in range(2):
            hand_out(i, out_rows.at[i], dst, c)[0].wait()
    for i, buf in enumerate((x_all, h_all, g2_all, g1_all)):
        for c in range(2):
            for kind in range(3):
                gather_copy(i, buf, c, kind).wait_send()
                rs_copy(i, c, kind).wait_send()
    for copy in keep:
        copy.wait()
    if tight:
        for i in range(4):
            keep_sum(i).wait()
            away_sums(i)[0].wait_recv()
        for i in (DOWN, UP, OUT):
            first_copy(i).wait_send()
            second_copy(i).wait_send()
        for j in range(3):
            direct_copy(j).wait_send()
            vec_copy(j).wait_send()
            bias_copy(j).wait_send()
        for j in range(7):
            column_out(j, vec_col, vc_s, vc_r).wait_send()
            column_out(j, bias_col, bc_s, bc_r).wait_send()

        @pl.when(home)
        def _():
            for i in range(4):
                mate_sum(i).wait_send()

        @pl.when(away)
        def _():
            for i in range(4):
                for copy in away_sums(i):
                    copy.wait_send()
            for item in weight_items:
                for j in range(3):
                    spread(item, j).wait_send()
            for item in range(12):
                swap(item).wait_send()
            for i, dst in enumerate((result_o, grad_o)):
                for c in range(2):
                    hand_out(i, out_rows.at[i], dst, c)[1].wait_send()


def layer_call(tight, shapes, *args):
    rows, width = shapes
    hidden = width
    length = 4 * rows
    chunk = rows // 2
    heads_wide, qkv_wide = 256, 640
    widths = (hidden, hidden, heads_wide, qkv_wide)
    any_space = pl.BlockSpec(memory_space=pl.ANY)
    vmem = pl.BlockSpec(memory_space=pltpu.VMEM)
    quarter = width // 4
    vec_rows = (8, 8) if tight else (8,)
    if tight:
        sums = [jax.ShapeDtypeStruct((quarter // 2, w), BF16) for w in widths]
    else:
        sums = [jax.ShapeDtypeStruct((2, 2, quarter, w), BF16) for w in widths]
    out_shape = (
        jax.ShapeDtypeStruct((rows, width), BF16),
        jax.ShapeDtypeStruct((rows, width), BF16),
        sums,
        [jax.ShapeDtypeStruct((quarter // 2, w), BF16) for w in widths],
        jax.ShapeDtypeStruct((*vec_rows, width), F32),
        jax.ShapeDtypeStruct((*vec_rows, 128), F32),
    )
    V = pltpu.VMEM
    D = pltpu.SemaphoreType.DMA
    pieces = V((4, 2, chunk, width), BF16)
    scratch = [
        *[V((length, width), BF16)] * 4,
        *[V((width, length), BF16)] * 4,
        *[pieces] * 6, V((2, rows, width), BF16),
        V((16, width), F32), V((16, width), F32), V((rows, width), BF16),
        V((576, width), BF16), V((qkv_wide, width), BF16), V((heads_wide, width), BF16),
        V((width, hidden), BF16), V((hidden, width), BF16),
        *[V((length, 128), F32)] * 4,
        V((length, qkv_wide), BF16), V((length, 128), BF16), V((3, length, length), F32),
        V((3, length, length), BF16), V((3, length, length), BF16), V((length, heads_wide), BF16),
        V((length, hidden), BF16), V((length, hidden), F32), V((length, hidden), BF16),
        V((length, heads_wide), BF16), V((length, qkv_wide), BF16),
        V((heads_wide, length), BF16), V((heads_wide, length), BF16),
        V((heads_wide, length), F32), V((heads_wide, length), F32),
        V((2, rows, width), F32), V((2, rows, width), F32), V((2 * rows, width), F32),
        [V((2, 2, quarter, w), BF16) for w in widths],
        [V((2, quarter, w), BF16) for w in widths[:3]],
        [V((quarter, w), BF16) for w in widths[:3]],
        [V((2, quarter, w), BF16) for w in widths[:3]],
        V((3, quarter, qkv_wide), BF16),
        [V((2, quarter // 2, w), BF16) for w in widths],
        V((8, width), F32), V((3, 8, width), F32), V((8, 8, width), F32),
        V((8, 128), F32), V((3, 8, 128), F32), V((8, 8, 128), F32),
        *[D((4, 2, 3))] * 4, D((12,)), D((12,)), D((8, 3)), D((8, 3)),
        D((3, 2)), D((3, 2)), D((3,)), D((3,)), D((4, 2)), D((4, 2)),
        D((3,)), D((3,)), D((7,)), D((7,)), D((3,)), D((3,)), D((7,)), D((7,)),
        D((2, 2)), D((2, 2)), D((9,)),
    ]
    return pl.pallas_call(
        partial(layer_kernel, tight),
        out_shape=out_shape,
        in_specs=[any_space] * 8 + [vmem] * 11,
        out_specs=jax.tree.map(lambda _: any_space, out_shape),
        scratch_shapes=scratch,
        compiler_params=pltpu.CompilerParams(
            collective_id=0, has_side_effects=True, vmem_limit_bytes=61 << 20
        ),
    )(*args)


def finish_kernel(*refs):
    sources, refs = refs[:12], refs[12:]
    outs, refs = refs[:18], refs[18:]
    held, sem = refs[:12], refs[12]
    (
        o_result, o_tokens, o_query, o_b_query, o_key, o_b_key, o_value, o_b_value, o_out, o_b_out,
        o_gain_mixer, o_shift_mixer, o_up, o_b_up, o_down, o_b_down, o_gain_feed, o_shift_feed,
    ) = outs
    copies = [
        pltpu.make_async_copy(src, dst, sem.at[i]) for i, (src, dst) in enumerate(zip(sources, held))
    ]
    for copy in copies:
        copy.start()

    def take(i):
        copies[i].wait()
        return held[i][...]

    def total(i):
        return take(2 + i).astype(F32) + take(6 + i).astype(F32)

    o_result[...] = take(0)
    o_tokens[...] = take(1).astype(F32)
    o_down[...] = total(DOWN)
    o_up[...] = total(UP)
    o_out[...] = jnp.transpose(total(OUT))[:192, :]
    for ref, part in zip((o_query, o_key, o_value), split_qkv(total(QKV))):
        ref[...] = part
    vec, bias = take(10), take(11)
    everywhere = jnp.sum(vec, axis=0)
    rows = (o_b_out, o_gain_mixer, o_shift_mixer, o_b_down, o_gain_feed, o_shift_feed)
    for i, ref in enumerate(rows):
        ref[...] = everywhere[i]
    by_slot = [vec[k, 6:7, :] + vec[4 + k, 6:7, :] for k in range(4)]
    o_b_up[...] = jnp.concatenate(by_slot, axis=1).reshape(o_b_up.shape)
    blocks = [bias[k] + bias[4 + k] for k in range(4)]
    for ref, (i, at) in zip((o_b_query, o_b_key, o_b_value), ((0, 0), (1, 64), (2, 0))):
        j = 4 if i == 2 else 3
        parts = []
        for b in blocks:
            parts += [b[i:i + 1, :], b[j:j + 1, at:at + 64]]
        ref[...] = jnp.concatenate(parts, axis=1).reshape(ref.shape)


def finish_call(shapes, *args):
    vmem = pl.BlockSpec(memory_space=pltpu.VMEM)
    return pl.pallas_call(
        finish_kernel,
        out_shape=shapes,
        in_specs=[pl.BlockSpec(memory_space=pl.ANY)] * len(args),
        out_specs=tuple(vmem for _ in shapes),
        scratch_shapes=[
            *[pltpu.VMEM(a.shape, a.dtype) for a in args], pltpu.SemaphoreType.DMA((len(args),))
        ],
        compiler_params=pltpu.CompilerParams(vmem_limit_bytes=61 << 20),
    )(*args)


def split_qkv(block):
    query = jnp.concatenate([block[..., :128], block[..., 384:448]], axis=-1)
    key = jnp.concatenate([block[..., 128:256], block[..., 448:512]], axis=-1)
    value = jnp.concatenate([block[..., 256:384], block[..., 512:576]], axis=-1)
    return query, key, value


def on_device(
    tight,
    tokens,
    segment_ids,
    w_query,
    b_query,
    w_key,
    b_key,
    w_value,
    b_value,
    w_out,
    b_out,
    gain_mixer,
    shift_mixer,
    w_up,
    b_up,
    w_down,
    b_down,
    gain_feed,
    shift_feed,
    cotangent,
):
    rows, width = tokens.shape
    result, grad_rows, sums_a, sums_b, vec, bias = layer_call(
        tight, (rows, width), tokens, cotangent, w_query.T, w_key.T, w_value.T, w_out, w_up, w_down,
        segment_ids, b_query, b_key, b_value, b_up, b_out, gain_mixer, shift_mixer, b_down,
        gain_feed, shift_feed,
    )
    if tight:
        ranks = lax.axis_size("tensor")
        share, here = width // lax.axis_size("dp"), w_query.shape[1]
        hidden = w_up.shape[1]

        def shape(*dims):
            return jax.ShapeDtypeStruct(dims, F32)

        head = (shape(share, here), shape(width)) * 3
        shapes = (
            jax.ShapeDtypeStruct((rows, width), BF16), shape(rows, width), *head,
            shape(here, share), shape(width), shape(width), shape(width),
            shape(share, hidden), shape(hidden * ranks), shape(share, hidden),
            shape(width), shape(width), shape(width),
        )
        outs = finish_call(shapes, result, grad_rows, *sums_a, *sums_b, vec, bias)
        return (*outs[:14], outs[14].T, *outs[15:])
    flat = [a.reshape(width, a.shape[-1]).astype(F32) for a in sums_a]
    scatter = partial(lax.psum_scatter, axis_name="dp", scatter_dimension=0, tiled=True)
    sum_query, sum_key, sum_value = (scatter(b) for b in split_qkv(flat[QKV]))
    sum_out, sum_down = scatter(flat[OUT][:, :192]).T, scatter(flat[DOWN]).T
    totals = lax.psum(vec, ("dp", "tensor"))
    bias_up = lax.all_gather(lax.psum(vec[6], "dp"), "tensor").reshape(-1)
    rows_qkv = lax.all_gather(lax.psum(bias[:5], "dp"), "tensor").reshape(-1, 640)
    biases = [b.reshape(-1) for b in split_qkv(rows_qkv)]
    return (
        result,
        grad_rows.astype(F32),
        sum_query,
        biases[0],
        sum_key,
        biases[1],
        sum_value,
        biases[2],
        sum_out,
        totals[0],
        totals[1],
        totals[2],
        scatter(flat[UP]),
        bias_up,
        sum_down,
        totals[3],
        totals[4],
        totals[5],
    )


def solution(mesh):
    in_specs = (
        P(("dp", "tensor"), None),
        P("dp", None),
        P(None, "tensor"),
        P("tensor"),
        P(None, "tensor"),
        P("tensor"),
        P(None, "tensor"),
        P("tensor"),
        P("tensor", None),
        P(),
        P(),
        P(),
        P(None, "tensor"),
        P("tensor"),
        P("tensor", None),
        P(),
        P(),
        P(),
        P(("dp", "tensor"), None),
    )
    out_specs = (
        P(("dp", "tensor"), None),
        P(("dp", "tensor"), None),
        P("dp", "tensor"),
        P(),
        P("dp", "tensor"),
        P(),
        P("dp", "tensor"),
        P(),
        P("tensor", "dp"),
        P(),
        P(),
        P(),
        P("dp", "tensor"),
        P(),
        P("tensor", "dp"),
        P(),
        P(),
        P(),
    )
    tight = mesh.shape["dp"] == 8
    return jax.shard_map(
        partial(on_device, tight), mesh=mesh, in_specs=in_specs, out_specs=out_specs,
        check_vma=False,
    )
```

time: 162 us -> 128 us (0.79)
  local copies, waits for them, and re-layouts: 18.5 us -> 0 us
  Pallas kernels: 135 us -> 127 us
  other arithmetic: 7.12 us -> 0 us
    pallas_call x1, Pallas kernels: 135 us -> 124 us  [layer_call(): pl.pallas_call(partial(layer_kernel, tight), out_shape=out_shape, in_spec...]
    unnamed x24 -> x0, local copies, waits for them, and re-layouts: 6.13 us -> none
    another operation x9 -> x0, local copies, waits for them, and re-layouts: 4.85 us -> none  [on_device(): jnp.stack(vectors).astype(F32)]
    slice x10 -> x0, local copies, waits for them, and re-layouts: 3.46 us -> none  [the longest x1 0.71 us: on_device(): b_query[128:]]
    pallas_call x0 -> x1, Pallas kernels: none -> 2.89 us  [finish_call(): pl.pallas_call(finish_kernel, out_shape=shapes, in_specs=[pl.BlockSpec(me...]
    concatenate x1 -> x0, local copies, waits for them, and re-layouts: 2.08 us -> none  [on_device(): jnp.concatenate([b_query[:128], b_key[:128], b_value[:128], b_query[128:]...]
    reshape x3 -> x0, local copies, waits for them, and re-layouts: 2.01 us -> none  [on_device(): biases = [b.reshape(-1) for b in split_qkv(by_slot[:, 7, :640])]]
    concatenate x5 -> x0, other arithmetic: 1.97 us -> none  [the longest x2 0.69 us: split_qkv(): query = jnp.concatenate([block[..., :128], block[..., 384:448]], axis=-1)]
where the time goes in v2:
time: 128 us
  Pallas kernels  127 us (99%)
    pallas_call x1, Pallas kernels, layer_call(): pl.pallas_call(partial(layer_kernel, tight), out_shape=out_shape, in_spec...  124 us
    pallas_call x1, Pallas kernels, finish_call(): pl.pallas_call(finish_kernel, out_shape=shapes, in_specs=[pl.BlockSpec(me...  2.89 us

profile of v2, /device:TPU:1, one launch (start us, length us, event | category | flops | bytes accessed | tf_op | source)
XLA Modules:
  0.0 127.9 jit_solution(3242730837235591567)
XLA Ops:
  0.7 124.2 %shard_map.322 = (bf16[128,768]{1,0:T(8,128)(2,1)}, bf16[128,768]{1,0:T(8,128)(2,1)}, bf16[96,768]{1,0:T(8,128)(2,1)}, bf16[96,768]{1,0:T(8,128)(2,1)}, bf16[96,...) custom-call(bf16[128,768]{1,0:T(8,128)(2,1)} %tokens.1, ...), custom_call_target="tpu_custom_call" | custom-call | tf_op jit(solution)/shard_map/pallas_call | solution.py:869
  124.8 2.9 %shard_map.323 = (bf16[128,768]{1,0:T(8,128)(2,1)}, f32[128,768]{1,0:T(8,128)}, f32[96,192]{1,0:T(8,128)}, f32[768]{0:T(1024)}, f32[96,192]{1,0:T(8,128)}, /*ind...) custom-call(bf16[128,768]{1,0:T(8,128)(2,1)} %get-tuple-element.48.r, ...), custom_call_target="tpu_custom_call" | custom-call | tf_op jit(solution)/shard_map/pallas_call | solution.py:927

commit v3 on v2

--- a/solution.py
+++ b/solution.py
@@ -14,7 +14,7 @@
 BF16 = jnp.bfloat16
 LN_EPS = 1e-12
 B_QKV, B_UP, B_OUT, G_MIX, S_MIX, B_DOWN, G_FEED, S_FEED = range(8)
-DOWN, UP, OUT, QKV = range(4)
+DOWN, UP, OV, QK = range(4)
 
 
 def nn(left, right):
@@ -48,19 +48,27 @@
 def layer_kernel(
     tight,
     tokens, cotangent, wq_t, wk_t, wv_t, w_out, w_up, w_down,
-    segment_ids, b_query, b_key, b_value, b_up, b_out, gain_mixer, shift_mixer, b_down,
-    gain_feed, shift_feed,
+    segment_ids, *rest,
+):
+    b_refs, rest = rest[:10], rest[10:]
+    layer_body(tight, tokens, cotangent, wq_t, wk_t, wv_t, w_out, w_up, w_down, segment_ids,
+               b_refs, *rest)
+
+
+def layer_body(
+    tight,
+    tokens, cotangent, wq_t, wk_t, wv_t, w_out, w_up, w_down, segment_ids, b_refs,
     result_o, grad_o, sums_a, sums_b, vec_o, bias_o,
     x_all, h_all, g2_all, g1_all, x_t, h_t, g2_t, g1_t,
     part_last, part_mate, land_last, land_mate, land_far, passed, out_rows,
     small_own, small_v, cot_v, staged, wqkv, wo, wu, wd,
     seg_nat, seg_cols, cos_t, sin_t,
-    qkv_s, k2_s, probs, probs_low, ds_s, o_s, act, dgelu, dz_s, do_s, dqkv_s,
+    qkv_s, k2_s, probs, probs_low, ds_s, o_s, act, dgelu, dz_s, do_s, dqk_s, dv_s,
     q_t, do_t, dk_t, dv_t, h_own, g_own, own_part,
     grads, first_in, second_in, grads_mid, grads_in, grads_sum,
-    vec, vec_in, vec_col, bias, bias_in, bias_col,
+    vec, vec_x, vec_in, bias, bias_x, bias_in, seg_v, b_v,
     ag_s, ag_r, rs_s, rs_r, sw_s, sw_r, wx_s, wx_r, dx_s, dx_r, dq_s, dq_r, dz_sem_s, dz_sem_r,
-    vx_s, vx_r, vc_s, vc_r, bx_s, bx_r, bc_s, bc_r, out_s, out_r, loc,
+    vec_s, vec_r, bias_s, bias_r, out_s, out_r, loc, b_sem,
 ):
     dp, ten = lax.axis_index("dp"), lax.axis_index("tensor")
     low = lax.rem(ten, 2)
@@ -81,11 +89,7 @@
         next_y = {"dp": ((1 - col_y) * 2 + col_x) * 2 + core, "tensor": ten}
         home = core == half
         away = core != half
-        column = [{"dp": dp, "tensor": lax.rem(ten + dz, 4)} for dz in (1, 2, 3)]
-        column += [
-            {"dp": col * 2 + 1 - core, "tensor": lax.rem(ten + dz, 4)} for dz in (0, 1, 2, 3)
-        ]
-        met = column + cols
+        met = [mate, far, across, partner, *cols]
     else:
         slot = ten
         mate_slot = ten + 1 - 2 * low
@@ -103,11 +107,18 @@
     def local(src, dst, sem):
         return pltpu.make_async_copy(src, dst, sem)
 
+    barrier = pltpu.get_barrier_semaphore()
+    for device in met:
+        pl.semaphore_signal(barrier, inc=1, device_id=device, device_id_type=MESH)
+
+    b_copies = [local(src, dst, b_sem.at[i]) for i, (src, dst) in enumerate(zip(b_refs, b_v))]
+    b_copies.append(local(segment_ids, seg_v, b_sem.at[10]))
+    for copy in b_copies:
+        copy.start()
     raw = []
-    qkv_ref = staged if tight else wqkv
     for i, w in enumerate((wq_t, wk_t, wv_t)):
-        raw.append((w.at[pl.ds(0, 128)], i * 128, 128))
-        raw.append((w.at[pl.ds(128, 64)], 384 + i * 64, 64))
+        raw.append((w.at[pl.ds(0, 128)], (0, 128, 384)[i], 128))
+        raw.append((w.at[pl.ds(128, 64)], (256, 320, 512)[i], 64))
 
     def raw_copy(i, ref):
         src, at, size = raw[i]
@@ -142,28 +153,24 @@
     else:
         load_own()
 
-    barrier = pltpu.get_barrier_semaphore()
-    for device in met:
-        pl.semaphore_signal(barrier, inc=1, device_id=device, device_id_type=MESH)
     wo[wo_rows:, :] = jnp.zeros((wo.shape[0] - wo_rows, width), BF16)
     wqkv[576:, :] = jnp.zeros((wqkv.shape[0] - 576, width), BF16)
 
     def vector(ref):
         return ref[...].astype(F32).reshape(1, ref.shape[0])
 
-    bq, bk, bv = vector(b_query), vector(b_key), vector(b_value)
-    for i, b in enumerate((bq, bk, bv)):
-        small_own[0:1, i * 128:(i + 1) * 128] = b[:, :128]
-    small_own[0:1, 384:512] = jnp.concatenate([bq[:, 128:], bk[:, 128:]], axis=1)
+    for copy in b_copies:
+        copy.wait()
+    bq, bk, bv = (vector(b_v[i]) for i in range(3))
+    for at, b in ((0, bq), (128, bk), (384, bv)):
+        small_own[0:1, at:at + 128] = b[:, :128]
+    small_own[0:1, 256:384] = jnp.concatenate([bq[:, 128:], bk[:, 128:]], axis=1)
     small_own[0:1, 512:640] = jnp.concatenate([bv[:, 128:], jnp.zeros((1, 64), F32)], axis=1)
     small_own[0:1, 640:] = jnp.zeros((1, width - 640), F32)
-    for at, ref in (
-        (B_UP, b_up), (B_OUT, b_out), (G_MIX, gain_mixer), (S_MIX, shift_mixer),
-        (B_DOWN, b_down), (G_FEED, gain_feed), (S_FEED, shift_feed),
-    ):
-        small_own[at:at + 1, :] = vector(ref)
+    for i in range(7):
+        small_own[B_UP + i:B_UP + i + 1, :] = vector(b_v[3 + i])
     small_own[8:16, :] = jnp.zeros((8, width), F32)
-    small_own[8:9, :length] = segment_ids[...].astype(F32)
+    small_own[8:9, :length] = seg_v[...].astype(F32)
     pl.semaphore_wait(barrier, len(met))
 
     weight_items = {
@@ -203,14 +210,15 @@
         rank = item_rank[item]
         return copy_to(ref, ref, wx_s.at[rank, j], wx_r.at[rank, j], cols[j])
 
-    def relay(*items):
+    def relay(item, follow=None):
         if tight:
             @pl.when(away)
             def _():
-                for item in items:
-                    swap(item).wait_recv()
-                    for j in range(3):
-                        spread(item, j).start()
+                swap(item).wait_recv()
+                for j in range(3):
+                    spread(item, j).start()
+                if follow is not None:
+                    swap(follow).start()
 
     def weights_ready(copies, *items):
         if not tight:
@@ -344,16 +352,20 @@
     if tight:
         @pl.when(away)
         def _():
-            for item, follow in ((1, 6), (2, 7), (3, 8)):
+            for item in (1, 2, 3):
                 swap(item).wait_recv()
                 for j in range(3):
                     spread(item, j).start()
-                swap(follow).start()
-            for c, follow in ((0, 9), (1, 10)):
+            swap(6).start()
+            swap(7).start()
+            for c, follow in ((0, 8), (1, 9)):
                 swap(4 + c).wait_recv()
                 ag_own(0, x_all, c)
                 swap(follow).start()
-            swap(11).start()
+            swap(6).wait_recv()
+            for j in range(3):
+                spread(6, j).start()
+            swap(10).start()
 
     low_lane = lane < 64
 
@@ -373,12 +385,11 @@
         def rot(block):
             return block * cosine + turn(block) * sine
 
-        query, key, mixed = rot(pre[:, :128]), rot(pre[:, 128:256]), rot(pre[:, 384:512])
+        query, key, mixed = rot(pre[:, :128]), rot(pre[:, 128:256]), rot(pre[:, 256:384])
         qkv_s[here, 0:128] = (query.astype(BF16) * scale).astype(BF16)
         qkv_s[here, 128:256] = key.astype(BF16)
-        qkv_s[here, 256:384] = pre[:, 256:384].astype(BF16)
-        qkv_s[here, 384:512] = (jnp.where(low_lane, mixed, 0.0).astype(BF16) * scale).astype(BF16)
-        qkv_s[here, 512:640] = pre[:, 512:640].astype(BF16)
+        qkv_s[here, 256:384] = (jnp.where(low_lane, mixed, 0.0).astype(BF16) * scale).astype(BF16)
+        qkv_s[here, 384:640] = pre[:, 384:640].astype(BF16)
         k2_s[here, :] = jnp.where(low_lane, pltpu.roll(mixed, 64, 1), 0.0).astype(BF16)
         x_t[:, here] = jnp.transpose(x)
 
@@ -389,7 +400,7 @@
     project_rows(*units[1])
     ag_unit(0, x_all, 1)
     project_rows(*units[2])
-    relay(6, 7)
+    relay(7, 11)
 
     def masked(block, head):
         if head == 2:
@@ -402,12 +413,12 @@
         same = seg_cols[here, 0:1] == seg_row
         outs = []
         for head in range(3):
-            q_at, v_at = (0, 256) if head < 2 else (384, 512)
+            q_at, v_at = (0, 384) if head < 2 else (256, 512)
             query = masked(qkv_s[here, q_at:q_at + 128], head)
             keys = qkv_s[:, 128:256] if head < 2 else k2_s[...]
             scores = jnp.where(same, nt(query, keys), -1e30)
             scores = jnp.exp(scores - jnp.max(scores, axis=1, keepdims=True))
-            weight = scores / jnp.sum(scores, axis=1, keepdims=True)
+            weight = scores * (1.0 / jnp.sum(scores, axis=1, keepdims=True))
             probs[head, here, :] = weight
             weight_low = weight.astype(BF16)
             probs_low[head, here, :] = weight_low
@@ -420,9 +431,9 @@
         return nn(o_s[lo:lo + n, :], wo[...])
 
     attend(2, 0)
+    relay(8)
     weights_ready([to_out], 6)
     rs_unit(0, 0, mix(*units[1]))
-    relay(8)
     attend(3, 0)
     rs_unit(0, 1, mix(*units[2]))
     rs_pass(0, 0)
@@ -431,6 +442,7 @@
     relay(9)
     lax.fori_loop(1, 2, attend, 0)
     rs_mate(0, mix(*units[0]))
+    relay(10)
     factors = []
 
     def spot(c):
@@ -449,7 +461,6 @@
         h_own[1, here, :] = normal1
         h_all[here, :] = normed.astype(BF16)
         ag_own(1, h_all, c)
-    relay(10)
 
     def feed(lo, n):
         here = slice(lo, lo + n)
@@ -473,8 +484,8 @@
     rs_pass(1, 0)
     feed(*units[2])
     rs_unit(1, 1, shrink(*units[2]))
+    rs_pass(1, 1)
     rs_mate(1, shrink(*units[0]))
-    rs_pass(1, 1)
     h_t[...] = jnp.transpose(h_all[...])
 
     def hand_out(i, src, dst, c):
@@ -506,8 +517,9 @@
         hand_start(0, out_rows.at[0], result_o, c)
         for i, term in enumerate((grad2, dy * normal2, dy)):
             sums[i] = sums[i] + jnp.sum(term, axis=0, keepdims=True)
+    vec[...] = jnp.zeros(vec.shape, F32)
     for i in range(3):
-        vec[3 + i:4 + i, :] = sums[i]
+        vec[0, 3 + i:4 + i, :] = sums[i]
 
     def feed_back(lo, n):
         here = slice(lo, lo + n)
@@ -518,6 +530,7 @@
 
     ag_mate(2, g2_all)
     feed_back(*units[0])
+    g2_t[:, :2 * rows] = jnp.transpose(g2_all[:2 * rows, :])
     ag_unit(2, g2_all, 0)
     feed_back(*units[1])
     rs_unit(2, 0, widen(*units[1]))
@@ -525,50 +538,63 @@
     rs_pass(2, 0)
     feed_back(*units[2])
     rs_unit(2, 1, widen(*units[2]))
+    rs_pass(2, 1)
     rs_mate(2, widen(*units[0]))
-    rs_pass(2, 1)
-
-    def weight_grad(i, left, right):
+
+    def weight_grad(at_piece, value):
         quarter = width // 4
 
         def step(q, carry):
             at = pl.ds(pl.multiple_of(q * quarter, quarter), quarter)
-            grads[i][q // 2, lax.rem(q, 2)] = nn(left[at, :], right[...]).astype(BF16)
+            found = value(at).astype(BF16)
+            for h in range(found.shape[1] // 384):
+                part = found[:, h * 384:(h + 1) * 384]
+                grads[at_piece + h][q // 2, lax.rem(q, 2)] = part
             return carry
 
         lax.fori_loop(0, 4, step, 0)
 
-    along_x = {DOWN: True, UP: False, OUT: True}
-
-    def first_copy(i):
-        if along_x[i]:
-            src, device = grads[i].at[:, 1 - col_x], next_x
+    def first_copy(i, h):
+        if h == 0:
+            src, device = grads[2 * i].at[:, 1 - col_x], next_x
         else:
-            src, device = grads[i].at[1 - col_y], next_y
-        return copy_to(src, first_in[i], dx_s.at[i, 0], dx_r.at[i, 0], device)
-
-    def second_copy(i):
-        keep, device = (1 - col_y, next_y) if along_x[i] else (1 - col_x, next_x)
+            src, device = grads[2 * i + 1].at[1 - col_y], next_y
         return copy_to(
-            grads_mid[i].at[keep], second_in[i], dx_s.at[i, 1], dx_r.at[i, 1], device
+            src, first_in.at[2 * i + h], dx_s.at[i, h, 0], dx_r.at[i, h, 0], device
         )
+
+    def second_copy(i, h):
+        keep, device = (1 - col_y, next_y) if h == 0 else (1 - col_x, next_x)
+        return copy_to(
+            grads_mid.at[2 * i + h, keep], second_in.at[2 * i + h], dx_s.at[i, h, 1],
+            dx_r.at[i, h, 1], device,
+        )
+
+    def first_send(i):
+        if tight:
+            for h in range(2):
+                first_copy(i, h).start()
 
     def first_land(i):
         if not tight:
             return
-        first_copy(i).wait_recv()
-        for j in range(2):
-            own = grads[i][j, col_x] if along_x[i] else grads[i][col_y, j]
-            grads_mid[i][j] = (own.astype(F32) + first_in[i][j].astype(F32)).astype(BF16)
-        second_copy(i).start()
+        for h in range(2):
+            first_copy(i, h).wait_recv()
+            for j in range(2):
+                own = grads[2 * i][j, col_x] if h == 0 else grads[2 * i + 1][col_y, j]
+                came = first_in[2 * i + h, j].astype(F32)
+                grads_mid[2 * i + h, j] = (own.astype(F32) + came).astype(BF16)
+            second_copy(i, h).start()
 
     def second_land(i):
         if not tight:
             return
-        second_copy(i).wait_recv()
-        own = grads_mid[i][col_y if along_x[i] else col_x]
-        total = own.astype(F32) + second_in[i][...].astype(F32)
-        finish_sum(i, total)
+        totals = []
+        for h in range(2):
+            second_copy(i, h).wait_recv()
+            own = grads_mid[2 * i + h, col_y if h == 0 else col_x]
+            totals.append(own.astype(F32) + second_in[2 * i + h].astype(F32))
+        finish_sum(i, jnp.concatenate(totals, axis=1))
 
     def finish_sum(i, total):
         grads_sum[i][...] = total.astype(BF16).reshape(grads_sum[i].shape)
@@ -583,11 +609,26 @@
             for copy in away_sums(i):
                 copy.start()
 
-    def direct_copy(j):
+    def direct_copy(i, j):
         to = lax.rem(col + 1 + j, 4)
         return copy_to(
-            grads[QKV].at[to // 2, lax.rem(to, 2)], grads_in.at[j], dq_s.at[j], dq_r.at[j], cols[j]
+            grads[i + 2].at[to // 2, lax.rem(to, 2)], grads_in.at[i - OV, j],
+            dq_s.at[i - OV, j], dq_r.at[i - OV, j], cols[j],
         )
+
+    def direct_send(i):
+        if tight:
+            for j in range(3):
+                direct_copy(i, j).start()
+
+    def direct_land(i):
+        if not tight:
+            return
+        total = grads[i + 2][col_y, col_x].astype(F32)
+        for j in range(3):
+            direct_copy(i, j).wait_recv()
+            total = total + grads_in[i - OV, j].astype(F32)
+        finish_sum(i, total)
 
     def keep_sum(i):
         return local(grads_sum[i].at[core], sums_a[i], dz_sem_r.at[i, 0])
@@ -607,16 +648,11 @@
             ),
         )
 
-    def first_send(i):
-        if tight:
-            first_copy(i).start()
-
-    g2_t[...] = jnp.transpose(g2_all[...])
-    weight_grad(DOWN, g2_t, act)
+    g2_t[:, 2 * rows:] = jnp.transpose(g2_all[2 * rows:, :])
+    weight_grad(0, lambda at: nn(g2_t[at, :], act[...]))
     first_send(DOWN)
-    weight_grad(UP, h_t, dz_s)
-    first_send(UP)
-    vec[6:7, :] = jnp.sum(dz_s[...].astype(F32), axis=0, keepdims=True)
+    weight_grad(2, lambda at: nn(h_t[at, :], dz_s[...]))
+    vec[1, pl.ds(slot, 1), :] = jnp.sum(dz_s[...].astype(F32), axis=0, keepdims=True)
 
     sums = [0.0, 0.0, 0.0]
     for c in range(2):
@@ -630,28 +666,44 @@
         for i, term in enumerate((grad1, dh * normal1, dh)):
             sums[i] = sums[i] + jnp.sum(term, axis=0, keepdims=True)
     for i in range(3):
-        vec[i:i + 1, :] = sums[i]
-    vec[7:8, :] = jnp.zeros((1, width), F32)
-
-    def vec_copy(j):
-        return copy_to(vec, vec_in.at[j], vx_s.at[j], vx_r.at[j], cols[j])
-
-    def bias_copy(j):
-        return copy_to(bias, bias_in.at[j], bx_s.at[j], bx_r.at[j], cols[j])
-
-    if tight:
-        mine = half * 4 + slot
-        for j in range(3):
-            vec_copy(j).start()
-
-    def column_out(j, ref, send, recv):
-        return copy_to(ref.at[mine], ref.at[mine], send.at[j], recv.at[j], column[j])
-
-    def column_in(j, ref, send, recv):
-        core_j = core if j < 3 else 1 - core
-        ten_j = lax.rem(ten + 3 - j, 4) if j < 3 else lax.rem(ten + 4 - (j - 3), 4)
-        at = (ten_j // 2) * 4 + lax.rem(ten_j, 2) + 2 * core_j
-        return copy_to(ref.at[at], ref.at[at], send.at[j], recv.at[j], column[j])
+        vec[0, i:i + 1, :] = sums[i]
+
+    class Total:
+        def __init__(self, own, sent, landing, send, recv):
+            self.own, self.sent, self.landing, self.send, self.recv = own, sent, landing, send, recv
+
+        def copy(self, j):
+            src = self.own if j < 3 else self.sent.at[j - 3]
+            device = (*cols, mate, far, across)[j]
+            return copy_to(src, self.landing.at[j], self.send.at[j], self.recv.at[j], device)
+
+        def begin(self):
+            if tight:
+                for j in range(3):
+                    self.copy(j).start()
+
+        def columns(self):
+            if tight:
+                for j in range(3):
+                    self.copy(j).wait_recv()
+                self.sent[0] = self.own[...] + self.landing[0] + self.landing[1] + self.landing[2]
+                self.copy(3).start()
+
+        def step(self, k):
+            if tight:
+                self.copy(2 + k).wait_recv()
+                self.sent[k] = self.sent[k - 1] + self.landing[2 + k]
+                if k < 3:
+                    self.copy(3 + k).start()
+
+        def sends_done(self):
+            for j in range(6):
+                self.copy(j).wait_send()
+
+    vec_total = Total(vec, vec_x, vec_in, vec_s, vec_r)
+    bias_total = Total(bias, bias_x, bias_in, bias_s, bias_r)
+    vec_total.begin()
+    first_send(UP)
 
     def heads_back(lo, n):
         here = slice(lo, lo + n)
@@ -664,7 +716,7 @@
         here = pl.ds(pl.multiple_of(s * rows, rows), rows)
         outs = []
         for head in range(3):
-            v_at, o_at = (256, 0) if head < 2 else (512, 128)
+            v_at, o_at = (384, 0) if head < 2 else (512, 128)
             grad_o = masked(do_s[here, o_at:o_at + 128], head)
             grad_p = nt(grad_o, qkv_s[:, v_at:v_at + 128])
             weight = probs[head, here, :]
@@ -673,97 +725,98 @@
             ds_s[head, here, :] = ds
             keys = qkv_s[:, 128:256] if head < 2 else k2_s[...]
             outs.append(nn(ds, keys) * scale)
-        dqkv_s[here, 0:128] = back(jnp.where(low_lane, outs[0], outs[1]), here).astype(BF16)
-        dqkv_s[here, 384:512] = back(outs[2], here).astype(BF16)
+        dqk_s[here, 0:128] = back(jnp.where(low_lane, outs[0], outs[1]), here).astype(BF16)
+        dqk_s[here, 256:384] = back(outs[2], here).astype(BF16)
         return carry
 
     q_t[0:128, :] = jnp.transpose(qkv_s[:, 0:128])
-    q_t[128:256, :] = jnp.transpose(qkv_s[:, 384:512])
+    q_t[128:256, :] = jnp.transpose(qkv_s[:, 256:384])
     ag_mate(3, g1_all)
     heads_back(*units[0])
+    g1_t[:, :2 * rows] = jnp.transpose(g1_all[:2 * rows, :])
     lax.fori_loop(0, 2, attend_back, 0)
+    first_land(DOWN)
+    vec_total.columns()
     ag_unit(3, g1_all, 0)
     heads_back(*units[1])
-    first_land(DOWN)
-    lax.fori_loop(2, 3, attend_back, 0)
     ag_unit(3, g1_all, 1)
     heads_back(*units[2])
-    first_land(UP)
-    lax.fori_loop(3, 4, attend_back, 0)
-    g1_t[...] = jnp.transpose(g1_all[...])
-    weight_grad(OUT, g1_t, o_s)
-    first_send(OUT)
+    vec_total.step(1)
+    g1_t[:, 2 * rows:] = jnp.transpose(g1_all[2 * rows:, :])
     do_t[0:128, :] = jnp.transpose(do_s[:, 0:128])
     do_t[128:256, :] = jnp.transpose(do_s[:, 128:256])
+    for head in range(2):
+        at = slice(head * 64, head * 64 + 64)
+        dv_t[at, :] = nn(do_t[at, :], probs_low[head])
+    dv_t[128:192, :] = jnp.zeros((64, length), F32)
+    dv_t[192:256, :] = nn(do_t[128:192, :], probs_low[2])
+    dv_s[:, 0:128] = jnp.transpose(dv_t[0:128, :]).astype(BF16)
+    dv_s[:, 128:256] = jnp.transpose(dv_t[128:256, :]).astype(BF16)
+
+    def out_value(at):
+        out = nn(g1_t[at, :], o_s[...])
+        value = nn(x_t[at, :], dv_s[...])
+        return jnp.concatenate(
+            [out[:, :128], value[:, :128], out[:, 128:] + value[:, 128:]], axis=1
+        )
+
+    weight_grad(4, out_value)
+    lax.fori_loop(2, 4, attend_back, 0)
+    first_land(UP)
+    vec_total.step(2)
     for head in range(3):
         at = slice(head * 64, head * 64 + 64)
         dk_t[at, :] = nn(q_t[at, :], ds_s[head])
-        dv_t[at, :] = nn(do_t[at, :], probs_low[head])
     dk_t[192:, :] = jnp.zeros((64, length), F32)
-    dv_t[192:, :] = jnp.zeros((64, length), F32)
-
     everything = slice(None)
-    dqkv_s[:, 128:256] = back(jnp.transpose(dk_t[0:128, :]), everything).astype(BF16)
+    dqk_s[:, 128:256] = back(jnp.transpose(dk_t[0:128, :]), everything).astype(BF16)
     key2 = back(jnp.transpose(dk_t[128:256, :]), everything)
-    query2 = dqkv_s[:, 384:512].astype(F32)
-    dqkv_s[:, 384:512] = jnp.where(low_lane, query2, pltpu.roll(key2, 64, 1)).astype(BF16)
-    dqkv_s[:, 256:384] = jnp.transpose(dv_t[0:128, :]).astype(BF16)
-    dqkv_s[:, 512:640] = jnp.transpose(dv_t[128:256, :]).astype(BF16)
-
-    weight_grad(QKV, x_t, dqkv_s)
-    if tight:
-        for j in range(3):
-            direct_copy(j).start()
+    query2 = dqk_s[:, 256:384].astype(F32)
+    dqk_s[:, 256:384] = jnp.where(low_lane, query2, pltpu.roll(key2, 64, 1)).astype(BF16)
+
+    query_key = jnp.sum(dqk_s[...].astype(F32), axis=0, keepdims=True)
+    values = jnp.sum(dv_s[...].astype(F32), axis=0, keepdims=True)
+    bias[...] = jnp.zeros(bias.shape, F32)
+    for i in range(3):
+        bias[slot, i:i + 1, :] = query_key[:, i * 128:(i + 1) * 128]
+    for i in range(2):
+        bias[slot, 3 + i:4 + i, :] = values[:, i * 128:(i + 1) * 128]
+    bias_total.begin()
+    direct_send(OV)
+    weight_grad(5, lambda at: nn(x_t[at, :], dqk_s[...]))
+    direct_send(QK)
+    second_land(DOWN)
+    value_low = jnp.where(
+        low_lane, pltpu.roll(dv_s[:, 128:256].astype(F32), 64, 1), 0.0
+    ).astype(BF16)
 
     def to_input(lo, n):
-        return nn(dqkv_s[lo:lo + n, :], wqkv[...])
+        term = nn(dqk_s[lo:lo + n, :], wqkv[0:384, :])
+        term = term + nn(dv_s[lo:lo + n, 0:128], wqkv[384:512, :])
+        return term + nn(value_low[lo:lo + n, :], wqkv[512:640, :])
 
     rs_unit(3, 0, to_input(*units[1]))
     rs_unit(3, 1, to_input(*units[2]))
     rs_pass(3, 0)
     rs_pass(3, 1)
     rs_mate(3, to_input(*units[0]))
-    total = jnp.sum(dqkv_s[...].astype(F32), axis=0, keepdims=True)
-    bias[...] = jnp.zeros((8, 128), F32)
-    for i in range(5):
-        bias[i:i + 1, :] = total[:, i * 128:(i + 1) * 128]
-    if tight:
-        for j in range(3):
-            bias_copy(j).start()
-        second_land(DOWN)
-        second_land(UP)
-        for j in range(3):
-            vec_copy(j).wait_recv()
-        vec_col[mine] = vec[...] + vec_in[0] + vec_in[1] + vec_in[2]
-        for j in range(7):
-            column_out(j, vec_col, vc_s, vc_r).start()
-        first_land(OUT)
-
+    bias_total.columns()
+    second_land(UP)
+    bias_total.step(1)
     for c in range(2):
         here = spot(c)
         out_rows[1, here, :] = (reduced(3, c) + g_own[1, here, :]).astype(BF16)
         hand_start(1, out_rows.at[1], grad_o, c)
-
+    bias_total.step(2)
+    direct_land(OV)
+    direct_land(QK)
+    vec_total.step(3)
+    bias_total.step(3)
     if tight:
-        for j in range(3):
-            bias_copy(j).wait_recv()
-        bias_col[mine] = bias[...] + bias_in[0] + bias_in[1] + bias_in[2]
-        for j in range(7):
-            column_out(j, bias_col, bc_s, bc_r).start()
-        second_land(OUT)
-        for j in range(3):
-            direct_copy(j).wait_recv()
-        total = grads[QKV][col_y, col_x].astype(F32)
-        for j in range(3):
-            total = total + grads_in[j].astype(F32)
-        finish_sum(QKV, total)
-        for j in range(7):
-            column_in(j, vec_col, vc_s, vc_r).wait_recv()
-            column_in(j, bias_col, bc_s, bc_r).wait_recv()
-        keep = [local(vec_col, vec_o, loc.at[0]), local(bias_col, bias_o, loc.at[1])]
+        keep = [local(vec_x.at[3], vec_o, loc.at[0]), local(bias_x.at[3], bias_o, loc.at[1])]
     else:
         keep = [local(vec, vec_o, loc.at[0]), local(bias, bias_o, loc.at[1])]
-        keep += [local(grads[i], sums_a[i], loc.at[2 + i]) for i in range(4)]
+        keep += [local(grads[i], sums_a[i], loc.at[2 + i]) for i in range(6)]
     for copy in keep:
         copy.start()
 
@@ -781,16 +834,15 @@
         for i in range(4):
             keep_sum(i).wait()
             away_sums(i)[0].wait_recv()
-        for i in (DOWN, UP, OUT):
-            first_copy(i).wait_send()
-            second_copy(i).wait_send()
-        for j in range(3):
-            direct_copy(j).wait_send()
-            vec_copy(j).wait_send()
-            bias_copy(j).wait_send()
-        for j in range(7):
-            column_out(j, vec_col, vc_s, vc_r).wait_send()
-            column_out(j, bias_col, bc_s, bc_r).wait_send()
+        for i in (DOWN, UP):
+            for h in range(2):
+                first_copy(i, h).wait_send()
+                second_copy(i, h).wait_send()
+        for i in (OV, QK):
+            for j in range(3):
+                direct_copy(i, j).wait_send()
+        vec_total.sends_done()
+        bias_total.sends_done()
 
         @pl.when(home)
         def _():
@@ -818,22 +870,20 @@
     length = 4 * rows
     chunk = rows // 2
     heads_wide, qkv_wide = 256, 640
-    widths = (hidden, hidden, heads_wide, qkv_wide)
+    widths = (hidden, hidden, 384, 384)
     any_space = pl.BlockSpec(memory_space=pl.ANY)
-    vmem = pl.BlockSpec(memory_space=pltpu.VMEM)
     quarter = width // 4
-    vec_rows = (8, 8) if tight else (8,)
     if tight:
         sums = [jax.ShapeDtypeStruct((quarter // 2, w), BF16) for w in widths]
     else:
-        sums = [jax.ShapeDtypeStruct((2, 2, quarter, w), BF16) for w in widths]
+        sums = [jax.ShapeDtypeStruct((2, 2, quarter, 384), BF16)] * 6
     out_shape = (
         jax.ShapeDtypeStruct((rows, width), BF16),
         jax.ShapeDtypeStruct((rows, width), BF16),
         sums,
         [jax.ShapeDtypeStruct((quarter // 2, w), BF16) for w in widths],
-        jax.ShapeDtypeStruct((*vec_rows, width), F32),
-        jax.ShapeDtypeStruct((*vec_rows, 128), F32),
+        jax.ShapeDtypeStruct((2, 8, width), F32),
+        jax.ShapeDtypeStruct((4, 8, 128), F32),
     )
     V = pltpu.VMEM
     D = pltpu.SemaphoreType.DMA
@@ -849,27 +899,25 @@
         V((length, qkv_wide), BF16), V((length, 128), BF16), V((3, length, length), F32),
         V((3, length, length), BF16), V((3, length, length), BF16), V((length, heads_wide), BF16),
         V((length, hidden), BF16), V((length, hidden), F32), V((length, hidden), BF16),
-        V((length, heads_wide), BF16), V((length, qkv_wide), BF16),
+        V((length, heads_wide), BF16), V((length, 384), BF16), V((length, heads_wide), BF16),
         V((heads_wide, length), BF16), V((heads_wide, length), BF16),
         V((heads_wide, length), F32), V((heads_wide, length), F32),
         V((2, rows, width), F32), V((2, rows, width), F32), V((2 * rows, width), F32),
-        [V((2, 2, quarter, w), BF16) for w in widths],
-        [V((2, quarter, w), BF16) for w in widths[:3]],
-        [V((quarter, w), BF16) for w in widths[:3]],
-        [V((2, quarter, w), BF16) for w in widths[:3]],
-        V((3, quarter, qkv_wide), BF16),
+        [V((2, 2, quarter, 384), BF16)] * 6,
+        V((4, 2, quarter, 384), BF16), V((4, quarter, 384), BF16), V((4, 2, quarter, 384), BF16),
+        V((2, 3, quarter, 384), BF16),
         [V((2, quarter // 2, w), BF16) for w in widths],
-        V((8, width), F32), V((3, 8, width), F32), V((8, 8, width), F32),
-        V((8, 128), F32), V((3, 8, 128), F32), V((8, 8, 128), F32),
+        V((2, 8, width), F32), V((4, 2, 8, width), F32), V((6, 2, 8, width), F32),
+        V((4, 8, 128), F32), V((4, 4, 8, 128), F32), V((6, 4, 8, 128), F32),
+        V((1, length), jnp.int32), [V(b.shape, BF16) for b in args[9:]],
         *[D((4, 2, 3))] * 4, D((12,)), D((12,)), D((8, 3)), D((8, 3)),
-        D((3, 2)), D((3, 2)), D((3,)), D((3,)), D((4, 2)), D((4, 2)),
-        D((3,)), D((3,)), D((7,)), D((7,)), D((3,)), D((3,)), D((7,)), D((7,)),
-        D((2, 2)), D((2, 2)), D((9,)),
+        D((2, 2, 2)), D((2, 2, 2)), D((2, 3)), D((2, 3)), D((4, 2)), D((4, 2)),
+        D((6,)), D((6,)), D((6,)), D((6,)), D((2, 2)), D((2, 2)), D((9,)), D((11,)),
     ]
     return pl.pallas_call(
         partial(layer_kernel, tight),
         out_shape=out_shape,
-        in_specs=[any_space] * 8 + [vmem] * 11,
+        in_specs=[any_space] * 19,
         out_specs=jax.tree.map(lambda _: any_space, out_shape),
         scratch_shapes=scratch,
         compiler_params=pltpu.CompilerParams(
@@ -903,22 +951,23 @@
     o_tokens[...] = take(1).astype(F32)
     o_down[...] = total(DOWN)
     o_up[...] = total(UP)
-    o_out[...] = jnp.transpose(total(OUT))[:192, :]
-    for ref, part in zip((o_query, o_key, o_value), split_qkv(total(QKV))):
+    out, query, key, value = split_pieces(total(OV), total(QK))
+    o_out[...] = jnp.transpose(out)
+    for ref, part in zip((o_query, o_key, o_value), (query, key, value)):
         ref[...] = part
     vec, bias = take(10), take(11)
-    everywhere = jnp.sum(vec, axis=0)
     rows = (o_b_out, o_gain_mixer, o_shift_mixer, o_b_down, o_gain_feed, o_shift_feed)
     for i, ref in enumerate(rows):
-        ref[...] = everywhere[i]
-    by_slot = [vec[k, 6:7, :] + vec[4 + k, 6:7, :] for k in range(4)]
-    o_b_up[...] = jnp.concatenate(by_slot, axis=1).reshape(o_b_up.shape)
-    blocks = [bias[k] + bias[4 + k] for k in range(4)]
-    for ref, (i, at) in zip((o_b_query, o_b_key, o_b_value), ((0, 0), (1, 64), (2, 0))):
-        j = 4 if i == 2 else 3
+        ref[...] = vec[0, i]
+    o_b_up[...] = jnp.concatenate([vec[1, k:k + 1, :] for k in range(4)], axis=1).reshape(
+        o_b_up.shape
+    )
+    for ref, (i, j, at) in zip(
+        (o_b_query, o_b_key, o_b_value), ((0, 2, 0), (1, 2, 64), (3, 4, 64))
+    ):
         parts = []
-        for b in blocks:
-            parts += [b[i:i + 1, :], b[j:j + 1, at:at + 64]]
+        for k in range(4):
+            parts += [bias[k, i:i + 1, :], bias[k, j:j + 1, at:at + 64]]
         ref[...] = jnp.concatenate(parts, axis=1).reshape(ref.shape)
 
 
@@ -936,11 +985,14 @@
     )(*args)
 
 
-def split_qkv(block):
-    query = jnp.concatenate([block[..., :128], block[..., 384:448]], axis=-1)
-    key = jnp.concatenate([block[..., 128:256], block[..., 448:512]], axis=-1)
-    value = jnp.concatenate([block[..., 256:384], block[..., 512:576]], axis=-1)
-    return query, key, value
+def split_pieces(out_value, query_key):
+    def pick(block, at, tail):
+        return jnp.concatenate([block[..., at:at + 128], block[..., tail:tail + 64]], axis=-1)
+
+    return (
+        pick(out_value, 0, 256), pick(query_key, 0, 256), pick(query_key, 128, 320),
+        pick(out_value, 128, 320),
+    )
 
 
 def on_device(
@@ -989,13 +1041,19 @@
         outs = finish_call(shapes, result, grad_rows, *sums_a, *sums_b, vec, bias)
         return (*outs[:14], outs[14].T, *outs[15:])
     flat = [a.reshape(width, a.shape[-1]).astype(F32) for a in sums_a]
+    flat = [jnp.concatenate(flat[:2], axis=1), jnp.concatenate(flat[2:4], axis=1), *flat[4:]]
     scatter = partial(lax.psum_scatter, axis_name="dp", scatter_dimension=0, tiled=True)
-    sum_query, sum_key, sum_value = (scatter(b) for b in split_qkv(flat[QKV]))
-    sum_out, sum_down = scatter(flat[OUT][:, :192]).T, scatter(flat[DOWN]).T
-    totals = lax.psum(vec, ("dp", "tensor"))
-    bias_up = lax.all_gather(lax.psum(vec[6], "dp"), "tensor").reshape(-1)
-    rows_qkv = lax.all_gather(lax.psum(bias[:5], "dp"), "tensor").reshape(-1, 640)
-    biases = [b.reshape(-1) for b in split_qkv(rows_qkv)]
+    sum_out, sum_query, sum_key, sum_value = (
+        scatter(b) for b in split_pieces(flat[OV], flat[QK])
+    )
+    sum_out, sum_down = sum_out.T, scatter(flat[DOWN]).T
+    vec = lax.psum(vec, ("dp", "tensor"))
+    bias = lax.psum(bias, ("dp", "tensor"))
+    totals, bias_up = vec[0], vec[1, :4].reshape(-1)
+    biases = [
+        jnp.concatenate([bias[:, i], bias[:, j, at:at + 64]], axis=1).reshape(-1)
+        for i, j, at in ((0, 2, 0), (1, 2, 64), (3, 4, 64))
+    ]
     return (
         result,
         grad_rows.astype(F32),

time: 128 us -> 116 us (0.906)
  Pallas kernels: 127 us -> 115 us
    pallas_call x1, Pallas kernels: 124 us -> 113 us  [layer_call(): pl.pallas_call(partial(layer_kernel, tight), out_shape=out_shape, in_spec...]
where the time goes in v3:
time: 116 us
  Pallas kernels  115 us (99%)
    pallas_call x1, Pallas kernels, layer_call(): pl.pallas_call(partial(layer_kernel, tight), out_shape=out_shape, in_spec...  113 us
    pallas_call x1, Pallas kernels, finish_call(): pl.pallas_call(finish_kernel, out_shape=shapes, in_specs=[pl.BlockSpec(me...  2.85 us

profile of v3, /device:TPU:1, one launch (start us, length us, event | category | flops | bytes accessed | tf_op | source)
XLA Modules:
  0.0 116.3 jit_solution(6500704108805423235)
XLA Ops:
  0.7 112.6 %shard_map.322 = (bf16[128,768]{1,0:T(8,128)(2,1)}, bf16[128,768]{1,0:T(8,128)(2,1)}, bf16[96,768]{1,0:T(8,128)(2,1)}, bf16[96,768]{1,0:T(8,128)(2,1)}, bf16[96,...) custom-call(bf16[128,768]{1,0:T(8,128)(2,1)} %tokens.1, ...), custom_call_target="tpu_custom_call" | custom-call | tf_op jit(solution)/shard_map/pallas_call | solution.py:917
  113.3 2.8 %shard_map.323 = (bf16[128,768]{1,0:T(8,128)(2,1)}, f32[128,768]{1,0:T(8,128)}, f32[96,192]{1,0:T(8,128)}, f32[768]{0:T(1024)}, f32[96,192]{1,0:T(8,128)}, /*ind...) custom-call(bf16[128,768]{1,0:T(8,128)(2,1)} %get-tuple-element.48.r, ...), custom_call_target="tpu_custom_call" | custom-call | tf_op jit(solution)/shard_map/pallas_call | solution.py:976

commit v4 on v3

--- a/solution.py
+++ b/solution.py
@@ -19,6 +19,10 @@
 
 def nn(left, right):
     return lax.dot_general(left, right, (((1,), (0,)), ((), ())), preferred_element_type=F32)
+
+
+def tn(left, right):
+    return lax.dot_general(left, right, (((0,), (0,)), ((), ())), preferred_element_type=F32)
 
 
 def nt(left, right):
@@ -59,7 +63,7 @@
     tight,
     tokens, cotangent, wq_t, wk_t, wv_t, w_out, w_up, w_down, segment_ids, b_refs,
     result_o, grad_o, sums_a, sums_b, vec_o, bias_o,
-    x_all, h_all, g2_all, g1_all, x_t, h_t, g2_t, g1_t,
+    x_all, h_all, g2_all, g1_all, wu_t, wd_t, wo_t,
     part_last, part_mate, land_last, land_mate, land_far, passed, out_rows,
     small_own, small_v, cot_v, staged, wqkv, wo, wu, wd,
     seg_nat, seg_cols, cos_t, sin_t,
@@ -357,14 +361,14 @@
                 for j in range(3):
                     spread(item, j).start()
             swap(6).start()
-            swap(7).start()
-            for c, follow in ((0, 8), (1, 9)):
+            for c, follow in ((0, 7), (1, 8)):
                 swap(4 + c).wait_recv()
                 ag_own(0, x_all, c)
                 swap(follow).start()
             swap(6).wait_recv()
             for j in range(3):
                 spread(6, j).start()
+            swap(9).start()
             swap(10).start()
 
     low_lane = lane < 64
@@ -391,7 +395,6 @@
         qkv_s[here, 256:384] = (jnp.where(low_lane, mixed, 0.0).astype(BF16) * scale).astype(BF16)
         qkv_s[here, 384:640] = pre[:, 384:640].astype(BF16)
         k2_s[here, :] = jnp.where(low_lane, pltpu.roll(mixed, 64, 1), 0.0).astype(BF16)
-        x_t[:, here] = jnp.transpose(x)
 
     weights_ready([raw_copy(i, wqkv) for i in range(6)], 1, 2, 3)
     ag_mate(0, x_all)
@@ -400,7 +403,6 @@
     project_rows(*units[1])
     ag_unit(0, x_all, 1)
     project_rows(*units[2])
-    relay(7, 11)
 
     def masked(block, head):
         if head == 2:
@@ -431,10 +433,11 @@
         return nn(o_s[lo:lo + n, :], wo[...])
 
     attend(2, 0)
-    relay(8)
+    relay(7)
     weights_ready([to_out], 6)
     rs_unit(0, 0, mix(*units[1]))
     attend(3, 0)
+    relay(8)
     rs_unit(0, 1, mix(*units[2]))
     rs_pass(0, 0)
     lax.fori_loop(0, 1, attend, 0)
@@ -442,7 +445,7 @@
     relay(9)
     lax.fori_loop(1, 2, attend, 0)
     rs_mate(0, mix(*units[0]))
-    relay(10)
+    relay(10, 11)
     factors = []
 
     def spot(c):
@@ -476,6 +479,8 @@
     weights_ready([to_up], 7, 8)
     ag_mate(1, h_all)
     feed(*units[0])
+    wu_t[...] = jnp.transpose(wu[...])
+    wo_t[...] = jnp.transpose(wo[...])
     ag_unit(1, h_all, 0)
     feed(*units[1])
     weights_ready([to_down], 9, 10)
@@ -486,7 +491,7 @@
     rs_unit(1, 1, shrink(*units[2]))
     rs_pass(1, 1)
     rs_mate(1, shrink(*units[0]))
-    h_t[...] = jnp.transpose(h_all[...])
+    wd_t[...] = jnp.transpose(wd[...])
 
     def hand_out(i, src, dst, c):
         src, dst = src.at[pl.ds(c * chunk, chunk)], dst.at[pl.ds(c * chunk, chunk)]
@@ -521,38 +526,14 @@
     for i in range(3):
         vec[0, 3 + i:4 + i, :] = sums[i]
 
-    def feed_back(lo, n):
-        here = slice(lo, lo + n)
-        dz_s[here, :] = (nt(g2_all[here, :], wd[...]) * dgelu[here, :]).astype(BF16)
-
-    def widen(lo, n):
-        return nt(dz_s[lo:lo + n, :], wu[...])
-
-    ag_mate(2, g2_all)
-    feed_back(*units[0])
-    g2_t[:, :2 * rows] = jnp.transpose(g2_all[:2 * rows, :])
-    ag_unit(2, g2_all, 0)
-    feed_back(*units[1])
-    rs_unit(2, 0, widen(*units[1]))
-    ag_unit(2, g2_all, 1)
-    rs_pass(2, 0)
-    feed_back(*units[2])
-    rs_unit(2, 1, widen(*units[2]))
-    rs_pass(2, 1)
-    rs_mate(2, widen(*units[0]))
-
     def weight_grad(at_piece, value):
         quarter = width // 4
-
-        def step(q, carry):
-            at = pl.ds(pl.multiple_of(q * quarter, quarter), quarter)
-            found = value(at).astype(BF16)
-            for h in range(found.shape[1] // 384):
-                part = found[:, h * 384:(h + 1) * 384]
-                grads[at_piece + h][q // 2, lax.rem(q, 2)] = part
-            return carry
-
-        lax.fori_loop(0, 4, step, 0)
+        for y in range(2):
+            found = value(slice(2 * y * quarter, 2 * (y + 1) * quarter)).astype(BF16)
+            for x in range(2):
+                for h in range(found.shape[1] // 384):
+                    part = found[x * quarter:(x + 1) * quarter, h * 384:(h + 1) * 384]
+                    grads[at_piece + h][y, x] = part
 
     def first_copy(i, h):
         if h == 0:
@@ -648,10 +629,28 @@
             ),
         )
 
-    g2_t[:, 2 * rows:] = jnp.transpose(g2_all[2 * rows:, :])
-    weight_grad(0, lambda at: nn(g2_t[at, :], act[...]))
+    def feed_back(lo, n):
+        here = slice(lo, lo + n)
+        dz_s[here, :] = (nn(g2_all[here, :], wd_t[...]) * dgelu[here, :]).astype(BF16)
+
+    def widen(lo, n):
+        return nn(dz_s[lo:lo + n, :], wu_t[...])
+
+    ag_mate(2, g2_all)
+    feed_back(*units[0])
+    ag_unit(2, g2_all, 0)
+    feed_back(*units[1])
+    rs_unit(2, 0, widen(*units[1]))
+    ag_unit(2, g2_all, 1)
+    rs_pass(2, 0)
+    weight_grad(0, lambda at: tn(g2_all[:, at], act[...]))
     first_send(DOWN)
-    weight_grad(2, lambda at: nn(h_t[at, :], dz_s[...]))
+    feed_back(*units[2])
+    rs_unit(2, 1, widen(*units[2]))
+    rs_pass(2, 1)
+    rs_mate(2, widen(*units[0]))
+
+    weight_grad(2, lambda at: tn(h_all[:, at], dz_s[...]))
     vec[1, pl.ds(slot, 1), :] = jnp.sum(dz_s[...].astype(F32), axis=0, keepdims=True)
 
     sums = [0.0, 0.0, 0.0]
@@ -703,11 +702,10 @@
     vec_total = Total(vec, vec_x, vec_in, vec_s, vec_r)
     bias_total = Total(bias, bias_x, bias_in, bias_s, bias_r)
     vec_total.begin()
-    first_send(UP)
 
     def heads_back(lo, n):
         here = slice(lo, lo + n)
-        do_s[here, :] = nt(g1_all[here, :], wo[...]).astype(BF16)
+        do_s[here, :] = nn(g1_all[here, :], wo_t[...]).astype(BF16)
 
     def back(values, here):
         return values * cos_t[here, :] - turn(values) * sin_t[here, :]
@@ -733,16 +731,17 @@
     q_t[128:256, :] = jnp.transpose(qkv_s[:, 256:384])
     ag_mate(3, g1_all)
     heads_back(*units[0])
-    g1_t[:, :2 * rows] = jnp.transpose(g1_all[:2 * rows, :])
-    lax.fori_loop(0, 2, attend_back, 0)
     first_land(DOWN)
+    lax.fori_loop(0, 1, attend_back, 0)
+    first_send(UP)
+    lax.fori_loop(1, 2, attend_back, 0)
     vec_total.columns()
     ag_unit(3, g1_all, 0)
     heads_back(*units[1])
     ag_unit(3, g1_all, 1)
     heads_back(*units[2])
     vec_total.step(1)
-    g1_t[:, 2 * rows:] = jnp.transpose(g1_all[2 * rows:, :])
+    second_land(DOWN)
     do_t[0:128, :] = jnp.transpose(do_s[:, 0:128])
     do_t[128:256, :] = jnp.transpose(do_s[:, 128:256])
     for head in range(2):
@@ -754,8 +753,8 @@
     dv_s[:, 128:256] = jnp.transpose(dv_t[128:256, :]).astype(BF16)
 
     def out_value(at):
-        out = nn(g1_t[at, :], o_s[...])
-        value = nn(x_t[at, :], dv_s[...])
+        out = tn(g1_all[:, at], o_s[...])
+        value = tn(x_all[:, at], dv_s[...])
         return jnp.concatenate(
             [out[:, :128], value[:, :128], out[:, 128:] + value[:, 128:]], axis=1
         )
@@ -783,9 +782,8 @@
         bias[slot, 3 + i:4 + i, :] = values[:, i * 128:(i + 1) * 128]
     bias_total.begin()
     direct_send(OV)
-    weight_grad(5, lambda at: nn(x_t[at, :], dqk_s[...]))
+    weight_grad(5, lambda at: tn(x_all[:, at], dqk_s[...]))
     direct_send(QK)
-    second_land(DOWN)
     value_low = jnp.where(
         low_lane, pltpu.roll(dv_s[:, 128:256].astype(F32), 64, 1), 0.0
     ).astype(BF16)
@@ -800,17 +798,17 @@
     rs_pass(3, 0)
     rs_pass(3, 1)
     rs_mate(3, to_input(*units[0]))
+    second_land(UP)
     bias_total.columns()
-    second_land(UP)
-    bias_total.step(1)
     for c in range(2):
         here = spot(c)
         out_rows[1, here, :] = (reduced(3, c) + g_own[1, here, :]).astype(BF16)
         hand_start(1, out_rows.at[1], grad_o, c)
+    bias_total.step(1)
+    vec_total.step(3)
+    direct_land(OV)
     bias_total.step(2)
-    direct_land(OV)
     direct_land(QK)
-    vec_total.step(3)
     bias_total.step(3)
     if tight:
         keep = [local(vec_x.at[3], vec_o, loc.at[0]), local(bias_x.at[3], bias_o, loc.at[1])]
@@ -890,7 +888,7 @@
     pieces = V((4, 2, chunk, width), BF16)
     scratch = [
         *[V((length, width), BF16)] * 4,
-        *[V((width, length), BF16)] * 4,
+        V((hidden, width), BF16), V((width, hidden), BF16), V((width, heads_wide), BF16),
         *[pieces] * 6, V((2, rows, width), BF16),
         V((16, width), F32), V((16, width), F32), V((rows, width), BF16),
         V((576, width), BF16), V((qkv_wide, width), BF16), V((heads_wide, width), BF16),

time: 116 us -> 110 us (0.948)
  Pallas kernels: 115 us -> 109 us
    pallas_call x1, Pallas kernels: 113 us -> 106 us  [layer_call(): pl.pallas_call(partial(layer_kernel, tight), out_shape=out_shape, in_spec...]
where the time goes in v4:
time: 110 us
  Pallas kernels  109 us (99%)
    pallas_call x1, Pallas kernels, layer_call(): pl.pallas_call(partial(layer_kernel, tight), out_shape=out_shape, in_spec...  106 us
    pallas_call x1, Pallas kernels, finish_call(): pl.pallas_call(finish_kernel, out_shape=shapes, in_specs=[pl.BlockSpec(me...  2.85 us

profile of v4, /device:TPU:1, one launch (start us, length us, event | category | flops | bytes accessed | tf_op | source)
XLA Modules:
  0.0 109.6 jit_solution(8608905529863873047)
XLA Ops:
  0.7 105.9 %shard_map.322 = (bf16[128,768]{1,0:T(8,128)(2,1)}, bf16[128,768]{1,0:T(8,128)(2,1)}, bf16[96,768]{1,0:T(8,128)(2,1)}, bf16[96,768]{1,0:T(8,128)(2,1)}, bf16[96,...) custom-call(bf16[128,768]{1,0:T(8,128)(2,1)} %tokens.1, ...), custom_call_target="tpu_custom_call" | custom-call | tf_op jit(solution)/shard_map/pallas_call | solution.py:915
  106.6 2.8 %shard_map.323 = (bf16[128,768]{1,0:T(8,128)(2,1)}, f32[128,768]{1,0:T(8,128)}, f32[96,192]{1,0:T(8,128)}, f32[768]{0:T(1024)}, f32[96,192]{1,0:T(8,128)}, /*ind...) custom-call(bf16[128,768]{1,0:T(8,128)(2,1)} %get-tuple-element.48.r, ...), custom_call_target="tpu_custom_call" | custom-call | tf_op jit(solution)/shard_map/pallas_call | solution.py:974

commit v5 on v4

--- a/solution.py
+++ b/solution.py
@@ -13,7 +13,9 @@
 F32 = jnp.float32
 BF16 = jnp.bfloat16
 LN_EPS = 1e-12
-B_QKV, B_UP, B_OUT, G_MIX, S_MIX, B_DOWN, G_FEED, S_FEED = range(8)
+CHUNKS = 2
+B_QKV, B_UP, SEGMENTS = range(3)
+B_OUT, G_MIX, S_MIX, B_DOWN, G_FEED, S_FEED = range(8, 14)
 DOWN, UP, OV, QK = range(4)
 
 
@@ -105,8 +107,10 @@
 
     rows, width = tokens.shape
     length = 4 * rows
-    chunk = rows // 2
-    units = ((0, 2 * rows), (2 * rows, rows), (3 * rows, rows))
+    chunk = rows // CHUNKS
+    token_part = rows // 2
+    both = (0, 2 * rows)
+    units = [(2 * rows + 2 * c * chunk, 2 * chunk) for c in range(CHUNKS)]
 
     def local(src, dst, sem):
         return pltpu.make_async_copy(src, dst, sem)
@@ -129,10 +133,13 @@
         return local(src, ref.at[pl.ds(at, size)], loc.at[i])
 
     to_tokens = [
-        local(tokens.at[pl.ds(c * chunk, chunk)], x_all.at[pl.ds(c * chunk, chunk)], sw_r.at[4 + c])
+        local(
+            tokens.at[pl.ds(c * token_part, token_part)],
+            x_all.at[pl.ds(c * token_part, token_part)], sw_r.at[4 + c],
+        )
         for c in range(2)
     ]
-    to_small = local(small_own, small_v, sw_r.at[0])
+    to_small = local(small_own, small_v.at[pl.ds(0, 8)], sw_r.at[0])
     to_cot = local(cotangent, cot_v, sw_r.at[11])
     wo_rows = w_out.shape[0]
     to_out = local(w_out, wo.at[pl.ds(0, wo_rows)], loc.at[6])
@@ -171,10 +178,11 @@
     small_own[0:1, 256:384] = jnp.concatenate([bq[:, 128:], bk[:, 128:]], axis=1)
     small_own[0:1, 512:640] = jnp.concatenate([bv[:, 128:], jnp.zeros((1, 64), F32)], axis=1)
     small_own[0:1, 640:] = jnp.zeros((1, width - 640), F32)
-    for i in range(7):
-        small_own[B_UP + i:B_UP + i + 1, :] = vector(b_v[3 + i])
-    small_own[8:16, :] = jnp.zeros((8, width), F32)
-    small_own[8:9, :length] = seg_v[...].astype(F32)
+    small_own[B_UP:B_UP + 1, :] = vector(b_v[3])
+    small_own[SEGMENTS:8, :] = jnp.zeros((8 - SEGMENTS, width), F32)
+    small_own[SEGMENTS:SEGMENTS + 1, :length] = seg_v[...].astype(F32)
+    for i in range(6):
+        small_v[B_OUT + i:B_OUT + i + 1, :] = vector(b_v[4 + i])
     pl.semaphore_wait(barrier, len(met))
 
     weight_items = {
@@ -196,11 +204,11 @@
             at = item_rows(item, col)
             src, dst = src.at[at], dst.at[at]
         elif item == 0:
-            src, dst = small_own, small_v
+            src, dst = small_own, small_v.at[pl.ds(0, 8)]
         elif item == 11:
             src, dst = cotangent, cot_v
         else:
-            at = pl.ds((item - 4) * chunk, chunk)
+            at = pl.ds((item - 4) * token_part, token_part)
             src, dst = tokens.at[at], x_all.at[at]
         return copy_to(src, dst, sw_s.at[item], sw_r.at[item], partner)
 
@@ -278,8 +286,12 @@
         gather_copy(i, buf, c, 1).start()
         gather_copy(i, buf, c, 0).start()
 
+    def own_tokens(part):
+        for c in range(CHUNKS // 2):
+            ag_own(0, x_all, part * (CHUNKS // 2) + c)
+
     def ag_mate(i, buf):
-        for c in range(2):
+        for c in range(CHUNKS):
             gather_copy(i, buf, c, 0).wait_recv()
 
     def ag_unit(i, buf, c):
@@ -295,6 +307,9 @@
         )[kind]
         return copy_to(src, dst, rs_s.at[i, c, kind], rs_r.at[i, c, kind], device)
 
+    def rs_whole(i):
+        return copy_to(part_mate.at[i], land_mate.at[i], rs_s.at[i, 0, 1], rs_r.at[i, 0, 1], mate)
+
     def rs_unit(i, c, term):
         part_last[i, c] = term[chunk:].astype(BF16)
         rs_copy(i, c, 0).start()
@@ -307,13 +322,14 @@
         rs_copy(i, c, 2).start()
 
     def rs_mate(i, term):
-        for c in range(2):
+        for c in range(CHUNKS):
             part_mate[i, c] = term[rows + c * chunk:rows + (c + 1) * chunk].astype(BF16)
-            rs_copy(i, c, 1).start()
+        rs_whole(i).start()
         own_part[0:rows, :] = term[:rows]
 
     def reduced(i, c):
-        rs_copy(i, c, 1).wait_recv()
+        if c == 0:
+            rs_whole(i).wait_recv()
         rs_copy(i, c, 2).wait_recv()
         term = own_part[c * chunk:(c + 1) * chunk, :]
         return term + land_mate[i, c].astype(F32) + land_far[i, c].astype(F32)
@@ -321,16 +337,16 @@
     if not tight:
         for c in range(2):
             to_tokens[c].wait()
-            ag_own(0, x_all, c)
+            own_tokens(c)
     else:
         @pl.when(home)
         def _():
             for c in range(2):
                 to_tokens[c].wait()
-                ag_own(0, x_all, c)
+                own_tokens(c)
 
     to_small.wait()
-    seg_row = small_v[8:9, :length]
+    seg_row = small_v[SEGMENTS:SEGMENTS + 1, :length]
     seg_nat[...] = jnp.transpose(jnp.broadcast_to(seg_row, (128, length)))
     segs = seg_nat[...]
     place = lax.broadcasted_iota(jnp.int32, (length, 128), 0).astype(F32)
@@ -339,8 +355,10 @@
         before = jnp.sum(jnp.where(seg_row < s, 1.0, 0.0), axis=1, keepdims=True)
         start = jnp.where(segs == s, before, start)
     cos_t[...] = place - start
-    order = [(0, slot, 0), (1, slot, 1), (2, mate_slot, 0), (3, mate_slot, 1)]
-    order += [(4, far_slot, 0), (5, last_slot, 0), (6, far_slot, 1), (7, last_slot, 1)]
+    order = [(c, slot, c) for c in range(CHUNKS)]
+    order += [(CHUNKS + c, mate_slot, c) for c in range(CHUNKS)]
+    for c in range(CHUNKS):
+        order += [(2 * (CHUNKS + c), far_slot, c), (2 * (CHUNKS + c) + 1, last_slot, c)]
     for to, from_slot, c in order:
         at = pl.ds(pl.multiple_of(from_slot * rows + c * chunk, chunk), chunk)
         seg_cols[to * chunk:(to + 1) * chunk, :] = seg_nat[at, :]
@@ -353,23 +371,6 @@
     sin_t[...] = jnp.sin(angle) * sign
     seg_row = jnp.transpose(seg_cols[...])[0:1, :]
 
-    if tight:
-        @pl.when(away)
-        def _():
-            for item in (1, 2, 3):
-                swap(item).wait_recv()
-                for j in range(3):
-                    spread(item, j).start()
-            swap(6).start()
-            for c, follow in ((0, 7), (1, 8)):
-                swap(4 + c).wait_recv()
-                ag_own(0, x_all, c)
-                swap(follow).start()
-            swap(6).wait_recv()
-            for j in range(3):
-                spread(6, j).start()
-            swap(9).start()
-            swap(10).start()
 
     low_lane = lane < 64
 
@@ -396,13 +397,36 @@
         qkv_s[here, 384:640] = pre[:, 384:640].astype(BF16)
         k2_s[here, :] = jnp.where(low_lane, pltpu.roll(mixed, 64, 1), 0.0).astype(BF16)
 
+    if tight:
+        @pl.when(away)
+        def _():
+            swap(1).wait_recv()
+            for j in range(3):
+                spread(1, j).start()
+            swap(2).wait_recv()
+            for j in range(3):
+                spread(2, j).start()
+            swap(6).start()
+            swap(4 + 0).wait_recv()
+            own_tokens(0)
+            swap(7).start()
+            swap(4 + 1).wait_recv()
+            own_tokens(1)
+            swap(3).wait_recv()
+            for j in range(3):
+                spread(3, j).start()
+            swap(8).start()
+            swap(6).wait_recv()
+            for j in range(3):
+                spread(6, j).start()
+            swap(9).start()
+            swap(10).start()
     weights_ready([raw_copy(i, wqkv) for i in range(6)], 1, 2, 3)
     ag_mate(0, x_all)
-    project_rows(*units[0])
-    ag_unit(0, x_all, 0)
-    project_rows(*units[1])
-    ag_unit(0, x_all, 1)
-    project_rows(*units[2])
+    project_rows(*both)
+    for c in range(CHUNKS):
+        ag_unit(0, x_all, c)
+    project_rows(2 * rows, 2 * rows)
 
     def masked(block, head):
         if head == 2:
@@ -433,19 +457,44 @@
         return nn(o_s[lo:lo + n, :], wo[...])
 
     attend(2, 0)
-    relay(7)
+    if tight:
+        @pl.when(away)
+        def _():
+            swap(7).wait_recv()
+            for j in range(3):
+                spread(7, j).start()
     weights_ready([to_out], 6)
-    rs_unit(0, 0, mix(*units[1]))
+    for c in range(CHUNKS // 2):
+        rs_unit(0, c, mix(*units[c]))
     attend(3, 0)
-    relay(8)
-    rs_unit(0, 1, mix(*units[2]))
-    rs_pass(0, 0)
+    if tight:
+        @pl.when(away)
+        def _():
+            swap(8).wait_recv()
+            for j in range(3):
+                spread(8, j).start()
+    for c in range(CHUNKS // 2, CHUNKS):
+        rs_unit(0, c, mix(*units[c]))
+    for c in range(CHUNKS // 2):
+        rs_pass(0, c)
     lax.fori_loop(0, 1, attend, 0)
-    rs_pass(0, 1)
-    relay(9)
+    for c in range(CHUNKS // 2, CHUNKS):
+        rs_pass(0, c)
+    if tight:
+        @pl.when(away)
+        def _():
+            swap(9).wait_recv()
+            for j in range(3):
+                spread(9, j).start()
     lax.fori_loop(1, 2, attend, 0)
-    rs_mate(0, mix(*units[0]))
-    relay(10, 11)
+    rs_mate(0, mix(*both))
+    if tight:
+        @pl.when(away)
+        def _():
+            swap(10).wait_recv()
+            for j in range(3):
+                spread(10, j).start()
+            swap(11).start()
     factors = []
 
     def spot(c):
@@ -454,7 +503,7 @@
     def row_of(at):
         return small_v[at:at + 1, :]
 
-    for c in range(2):
+    for c in range(CHUNKS):
         here = spot(c)
         into = reduced(0, c) + x_all[here, :].astype(F32) + row_of(B_OUT)
         normal1, factor1 = norm_stats(into)
@@ -465,6 +514,7 @@
         h_all[here, :] = normed.astype(BF16)
         ag_own(1, h_all, c)
 
+
     def feed(lo, n):
         here = slice(lo, lo + n)
         h = h_all[here, :]
@@ -478,19 +528,19 @@
 
     weights_ready([to_up], 7, 8)
     ag_mate(1, h_all)
-    feed(*units[0])
+    feed(*both)
     wu_t[...] = jnp.transpose(wu[...])
     wo_t[...] = jnp.transpose(wo[...])
-    ag_unit(1, h_all, 0)
-    feed(*units[1])
-    weights_ready([to_down], 9, 10)
-    rs_unit(1, 0, shrink(*units[1]))
-    ag_unit(1, h_all, 1)
-    rs_pass(1, 0)
-    feed(*units[2])
-    rs_unit(1, 1, shrink(*units[2]))
-    rs_pass(1, 1)
-    rs_mate(1, shrink(*units[0]))
+    for c in range(CHUNKS):
+        ag_unit(1, h_all, c)
+        if c > 0:
+            rs_pass(1, c - 1)
+        feed(*units[c])
+        if c == 0:
+            weights_ready([to_down], 9, 10)
+        rs_unit(1, c, shrink(*units[c]))
+    rs_pass(1, CHUNKS - 1)
+    rs_mate(1, shrink(*both))
     wd_t[...] = jnp.transpose(wd[...])
 
     def hand_out(i, src, dst, c):
@@ -509,7 +559,7 @@
 
     to_cot.wait()
     sums = [0.0, 0.0, 0.0]
-    for c in range(2):
+    for c in range(CHUNKS):
         here = spot(c)
         into = reduced(1, c) + h_own[0, here, :] + row_of(B_DOWN)
         normal2, factor2 = norm_stats(into)
@@ -637,24 +687,24 @@
         return nn(dz_s[lo:lo + n, :], wu_t[...])
 
     ag_mate(2, g2_all)
-    feed_back(*units[0])
-    ag_unit(2, g2_all, 0)
-    feed_back(*units[1])
-    rs_unit(2, 0, widen(*units[1]))
-    ag_unit(2, g2_all, 1)
-    rs_pass(2, 0)
-    weight_grad(0, lambda at: tn(g2_all[:, at], act[...]))
-    first_send(DOWN)
-    feed_back(*units[2])
-    rs_unit(2, 1, widen(*units[2]))
-    rs_pass(2, 1)
-    rs_mate(2, widen(*units[0]))
+    feed_back(*both)
+    for c in range(CHUNKS):
+        ag_unit(2, g2_all, c)
+        if c > 0:
+            rs_pass(2, c - 1)
+        if c == CHUNKS - 1:
+            weight_grad(0, lambda at: tn(g2_all[:, at], act[...]))
+            first_send(DOWN)
+        feed_back(*units[c])
+        rs_unit(2, c, widen(*units[c]))
+    rs_pass(2, CHUNKS - 1)
+    rs_mate(2, widen(*both))
 
     weight_grad(2, lambda at: tn(h_all[:, at], dz_s[...]))
     vec[1, pl.ds(slot, 1), :] = jnp.sum(dz_s[...].astype(F32), axis=0, keepdims=True)
 
     sums = [0.0, 0.0, 0.0]
-    for c in range(2):
+    for c in range(CHUNKS):
         here = spot(c)
         dh = reduced(2, c) + g_own[0, here, :]
         normal1 = h_own[1, here, :]
@@ -730,16 +780,15 @@
     q_t[0:128, :] = jnp.transpose(qkv_s[:, 0:128])
     q_t[128:256, :] = jnp.transpose(qkv_s[:, 256:384])
     ag_mate(3, g1_all)
-    heads_back(*units[0])
+    heads_back(*both)
     first_land(DOWN)
     lax.fori_loop(0, 1, attend_back, 0)
     first_send(UP)
     lax.fori_loop(1, 2, attend_back, 0)
     vec_total.columns()
-    ag_unit(3, g1_all, 0)
-    heads_back(*units[1])
-    ag_unit(3, g1_all, 1)
-    heads_back(*units[2])
+    for c in range(CHUNKS):
+        ag_unit(3, g1_all, c)
+    heads_back(2 * rows, 2 * rows)
     vec_total.step(1)
     second_land(DOWN)
     do_t[0:128, :] = jnp.transpose(do_s[:, 0:128])
@@ -760,7 +809,8 @@
         )
 
     weight_grad(4, out_value)
-    lax.fori_loop(2, 4, attend_back, 0)
+    lax.fori_loop(2, 3, attend_back, 0)
+    lax.fori_loop(3, 4, attend_back, 0)
     first_land(UP)
     vec_total.step(2)
     for head in range(3):
@@ -780,33 +830,69 @@
         bias[slot, i:i + 1, :] = query_key[:, i * 128:(i + 1) * 128]
     for i in range(2):
         bias[slot, 3 + i:4 + i, :] = values[:, i * 128:(i + 1) * 128]
+    value_low = jnp.where(
+        low_lane, pltpu.roll(dv_s[:, 128:256].astype(F32), 64, 1), 0.0
+    ).astype(BF16)
+
+    def to_input(lo, n):
+        term = nn(dqk_s[lo:lo + n, :], wqkv[0:384, :])
+        term = term + nn(dv_s[lo:lo + n, 0:128], wqkv[384:512, :])
+        return term + nn(value_low[lo:lo + n, :], wqkv[512:640, :])
+
     bias_total.begin()
     direct_send(OV)
     weight_grad(5, lambda at: tn(x_all[:, at], dqk_s[...]))
     direct_send(QK)
-    value_low = jnp.where(
-        low_lane, pltpu.roll(dv_s[:, 128:256].astype(F32), 64, 1), 0.0
-    ).astype(BF16)
-
-    def to_input(lo, n):
-        term = nn(dqk_s[lo:lo + n, :], wqkv[0:384, :])
-        term = term + nn(dv_s[lo:lo + n, 0:128], wqkv[384:512, :])
-        return term + nn(value_low[lo:lo + n, :], wqkv[512:640, :])
-
-    rs_unit(3, 0, to_input(*units[1]))
-    rs_unit(3, 1, to_input(*units[2]))
-    rs_pass(3, 0)
-    rs_pass(3, 1)
-    rs_mate(3, to_input(*units[0]))
+    for c in range(CHUNKS):
+        rs_unit(3, c, to_input(*units[c]))
+    for c in range(CHUNKS):
+        rs_pass(3, c)
+    rs_mate(3, to_input(*both))
     second_land(UP)
     bias_total.columns()
-    for c in range(2):
+    for c in range(CHUNKS):
         here = spot(c)
         out_rows[1, here, :] = (reduced(3, c) + g_own[1, here, :]).astype(BF16)
         hand_start(1, out_rows.at[1], grad_o, c)
     bias_total.step(1)
     vec_total.step(3)
+    for i, buf in enumerate((x_all, h_all, g2_all, g1_all)):
+        for c in range(CHUNKS):
+            for kind in range(3):
+                gather_copy(i, buf, c, kind).wait_send()
+                if kind != 1:
+                    rs_copy(i, c, kind).wait_send()
+        rs_whole(i).wait_send()
+
+    def out_waits(i, dst):
+        for c in range(CHUNKS):
+            hand_out(i, out_rows.at[i], dst, c)[0].wait()
+        if tight:
+            @pl.when(away)
+            def _():
+                for c in range(CHUNKS):
+                    hand_out(i, out_rows.at[i], dst, c)[1].wait_send()
+
+    out_waits(0, result_o)
+    if tight:
+        for i in (DOWN, UP):
+            for h in range(2):
+                first_copy(i, h).wait_send()
+                second_copy(i, h).wait_send()
+        vec_total.sends_done()
+
+        @pl.when(away)
+        def _():
+            for item in weight_items:
+                for j in range(3):
+                    spread(item, j).wait_send()
+            for item in range(12):
+                swap(item).wait_send()
+
     direct_land(OV)
+    if tight:
+        for j in range(3):
+            direct_copy(OV, j).wait_send()
     bias_total.step(2)
     direct_land(QK)
     bias_total.step(3)
@@ -818,28 +904,15 @@
     for copy in keep:
         copy.start()
 
-    for i, dst in enumerate((result_o, grad_o)):
-        for c in range(2):
-            hand_out(i, out_rows.at[i], dst, c)[0].wait()
-    for i, buf in enumerate((x_all, h_all, g2_all, g1_all)):
-        for c in range(2):
-            for kind in range(3):
-                gather_copy(i, buf, c, kind).wait_send()
-                rs_copy(i, c, kind).wait_send()
+    out_waits(1, grad_o)
     for copy in keep:
         copy.wait()
     if tight:
         for i in range(4):
             keep_sum(i).wait()
             away_sums(i)[0].wait_recv()
-        for i in (DOWN, UP):
-            for h in range(2):
-                first_copy(i, h).wait_send()
-                second_copy(i, h).wait_send()
-        for i in (OV, QK):
-            for j in range(3):
-                direct_copy(i, j).wait_send()
-        vec_total.sends_done()
+        for j in range(3):
+            direct_copy(QK, j).wait_send()
         bias_total.sends_done()
 
         @pl.when(home)
@@ -852,21 +925,13 @@
             for i in range(4):
                 for copy in away_sums(i):
                     copy.wait_send()
-            for item in weight_items:
-                for j in range(3):
-                    spread(item, j).wait_send()
-            for item in range(12):
-                swap(item).wait_send()
-            for i, dst in enumerate((result_o, grad_o)):
-                for c in range(2):
-                    hand_out(i, out_rows.at[i], dst, c)[1].wait_send()
 
 
 def layer_call(tight, shapes, *args):
     rows, width = shapes
     hidden = width
     length = 4 * rows
-    chunk = rows // 2
+    chunk = rows // CHUNKS
     heads_wide, qkv_wide = 256, 640
     widths = (hidden, hidden, 384, 384)
     any_space = pl.BlockSpec(memory_space=pl.ANY)
@@ -885,12 +950,12 @@
     )
     V = pltpu.VMEM
     D = pltpu.SemaphoreType.DMA
-    pieces = V((4, 2, chunk, width), BF16)
+    pieces = V((4, CHUNKS, chunk, width), BF16)
     scratch = [
         *[V((length, width), BF16)] * 4,
         V((hidden, width), BF16), V((width, hidden), BF16), V((width, heads_wide), BF16),
         *[pieces] * 6, V((2, rows, width), BF16),
-        V((16, width), F32), V((16, width), F32), V((rows, width), BF16),
+        V((8, width), F32), V((16, width), F32), V((rows, width), BF16),
         V((576, width), BF16), V((qkv_wide, width), BF16), V((heads_wide, width), BF16),
         V((width, hidden), BF16), V((hidden, width), BF16),
         *[V((length, 128), F32)] * 4,
@@ -908,9 +973,9 @@
         V((2, 8, width), F32), V((4, 2, 8, width), F32), V((6, 2, 8, width), F32),
         V((4, 8, 128), F32), V((4, 4, 8, 128), F32), V((6, 4, 8, 128), F32),
         V((1, length), jnp.int32), [V(b.shape, BF16) for b in args[9:]],
-        *[D((4, 2, 3))] * 4, D((12,)), D((12,)), D((8, 3)), D((8, 3)),
+        *[D((4, CHUNKS, 3))] * 4, D((12,)), D((12,)), D((8, 3)), D((8, 3)),
         D((2, 2, 2)), D((2, 2, 2)), D((2, 3)), D((2, 3)), D((4, 2)), D((4, 2)),
-        D((6,)), D((6,)), D((6,)), D((6,)), D((2, 2)), D((2, 2)), D((9,)), D((11,)),
+        D((6,)), D((6,)), D((6,)), D((6,)), D((2, CHUNKS)), D((2, CHUNKS)), D((9,)), D((11,)),
     ]
     return pl.pallas_call(
         partial(layer_kernel, tight),
@@ -927,11 +992,14 @@
 def finish_kernel(*refs):
     sources, refs = refs[:12], refs[12:]
     outs, refs = refs[:18], refs[18:]
-    held, sem = refs[:12], refs[12]
+    held, made, sem, out_sem = refs[:12], refs[12:30], refs[30], refs[31]
     (
         o_result, o_tokens, o_query, o_b_query, o_key, o_b_key, o_value, o_b_value, o_out, o_b_out,
         o_gain_mixer, o_shift_mixer, o_up, o_b_up, o_down, o_b_down, o_gain_feed, o_shift_feed,
-    ) = outs
+    ) = made
+    writes = [
+        pltpu.make_async_copy(src, dst, out_sem.at[i]) for i, (src, dst) in enumerate(zip(made, outs))
+    ]
     copies = [
         pltpu.make_async_copy(src, dst, sem.at[i]) for i, (src, dst) in enumerate(zip(sources, held))
     ]
@@ -946,13 +1014,19 @@
         return take(2 + i).astype(F32) + take(6 + i).astype(F32)
 
     o_result[...] = take(0)
+    writes[0].start()
     o_tokens[...] = take(1).astype(F32)
+    writes[1].start()
     o_down[...] = total(DOWN)
+    writes[14].start()
     o_up[...] = total(UP)
+    writes[12].start()
     out, query, key, value = split_pieces(total(OV), total(QK))
     o_out[...] = jnp.transpose(out)
     for ref, part in zip((o_query, o_key, o_value), (query, key, value)):
         ref[...] = part
+    for i in (8, 2, 4, 6):
+        writes[i].start()
     vec, bias = take(10), take(11)
     rows = (o_b_out, o_gain_mixer, o_shift_mixer, o_b_down, o_gain_feed, o_shift_feed)
     for i, ref in enumerate(rows):
@@ -967,17 +1041,23 @@
         for k in range(4):
             parts += [bias[k, i:i + 1, :], bias[k, j:j + 1, at:at + 64]]
         ref[...] = jnp.concatenate(parts, axis=1).reshape(ref.shape)
+    for i in (3, 5, 7, 9, 10, 11, 13, 15, 16, 17):
+        writes[i].start()
+    for write in writes:
+        write.wait()
 
 
 def finish_call(shapes, *args):
-    vmem = pl.BlockSpec(memory_space=pltpu.VMEM)
+    any_space = pl.BlockSpec(memory_space=pl.ANY)
     return pl.pallas_call(
         finish_kernel,
         out_shape=shapes,
-        in_specs=[pl.BlockSpec(memory_space=pl.ANY)] * len(args),
-        out_specs=tuple(vmem for _ in shapes),
+        in_specs=[any_space] * len(args),
+        out_specs=tuple(any_space for _ in shapes),
         scratch_shapes=[
-            *[pltpu.VMEM(a.shape, a.dtype) for a in args], pltpu.SemaphoreType.DMA((len(args),))
+            *[pltpu.VMEM(a.shape, a.dtype) for a in args],
+            *[pltpu.VMEM(a.shape, a.dtype) for a in shapes],
+            pltpu.SemaphoreType.DMA((len(args),)), pltpu.SemaphoreType.DMA((len(shapes),)),
         ],
         compiler_params=pltpu.CompilerParams(vmem_limit_bytes=61 << 20),
     )(*args)

time: 110 us -> 109 us (level)
  no operation moved by 1% of the time
where the time goes in v5:
time: 109 us
  Pallas kernels  108 us (99%)
    pallas_call x1, Pallas kernels, layer_call(): pl.pallas_call(partial(layer_kernel, tight), out_shape=out_shape, in_spec...  106 us
    pallas_call x1, Pallas kernels, finish_call(): pl.pallas_call(finish_kernel, out_shape=shapes, in_specs=[any_space] * le...  2.56 us

profile of v5, /device:TPU:1, one launch (start us, length us, event | category | flops | bytes accessed | tf_op | source)
XLA Modules:
  0.0 109.0 jit_solution(212520303596738856)
XLA Ops:
  0.7 105.6 %shard_map.322 = (bf16[128,768]{1,0:T(8,128)(2,1)}, bf16[128,768]{1,0:T(8,128)(2,1)}, bf16[96,768]{1,0:T(8,128)(2,1)}, bf16[96,768]{1,0:T(8,128)(2,1)}, bf16[96,...) custom-call(bf16[128,768]{1,0:T(8,128)(2,1)} %tokens.1, ...), custom_call_target="tpu_custom_call" | custom-call | tf_op jit(solution)/shard_map/pallas_call | solution.py:980
  106.2 2.6 %shard_map.323 = (bf16[128,768]{1,0:T(8,128)(2,1)}, f32[128,768]{1,0:T(8,128)}, f32[96,192]{1,0:T(8,128)}, f32[768]{0:T(1024)}, f32[96,192]{1,0:T(8,128)}, /*ind...) custom-call(bf16[128,768]{1,0:T(8,128)(2,1)} %get-tuple-element.48.r, ...), custom_call_target="tpu_custom_call" | custom-call | tf_op jit(solution)/shard_map/pallas_call | solution.py:1052

commit v6 on v5

--- a/solution.py
+++ b/solution.py
@@ -640,26 +640,47 @@
             for copy in away_sums(i):
                 copy.start()
 
-    def direct_copy(i, j):
+    share = width // 8
+
+    def direct_copy(i, j, part):
         to = lax.rem(col + 1 + j, 4)
+        at = pl.ds(part * share, share)
         return copy_to(
-            grads[i + 2].at[to // 2, lax.rem(to, 2)], grads_in.at[i - OV, j],
-            dq_s.at[i - OV, j], dq_r.at[i - OV, j], cols[j],
+            grads[i + 2].at[to // 2, lax.rem(to, 2), at], grads_in.at[i - OV, j, at],
+            dq_s.at[i - OV, j, part], dq_r.at[i - OV, j, part], cols[j],
         )
 
     def direct_send(i):
         if tight:
-            for j in range(3):
-                direct_copy(i, j).start()
+            for part in range(2):
+                for j in range(3):
+                    direct_copy(i, j, part).start()
 
     def direct_land(i):
         if not tight:
             return
-        total = grads[i + 2][col_y, col_x].astype(F32)
-        for j in range(3):
-            direct_copy(i, j).wait_recv()
-            total = total + grads_in[i - OV, j].astype(F32)
-        finish_sum(i, total)
+        for part in range(2):
+            at = slice(part * share, (part + 1) * share)
+            total = grads[i + 2][col_y, col_x, at].astype(F32)
+            for j in range(3):
+                direct_copy(i, j, part).wait_recv()
+                total = total + grads_in[i - OV, j, at].astype(F32)
+            grads_sum[i][part] = total.astype(BF16)
+
+            @pl.when(home)
+            def _():
+                pl.when(core == part)(keep_sum(i).start)
+                pl.when(core != part)(mate_sum(i).start)
+
+            @pl.when(away)
+            def _():
+                pl.when(core == part)(away_sums(i)[0].start)
+                pl.when(core != part)(away_sums(i)[1].start)
+
+    def direct_sent(i):
+        for part in range(2):
+            for j in range(3):
+                direct_copy(i, j, part).wait_send()
 
     def keep_sum(i):
         return local(grads_sum[i].at[core], sums_a[i], dz_sem_r.at[i, 0])
@@ -841,13 +862,13 @@
 
     bias_total.begin()
     direct_send(OV)
-    weight_grad(5, lambda at: tn(x_all[:, at], dqk_s[...]))
-    direct_send(QK)
     for c in range(CHUNKS):
         rs_unit(3, c, to_input(*units[c]))
     for c in range(CHUNKS):
         rs_pass(3, c)
     rs_mate(3, to_input(*both))
+    weight_grad(5, lambda at: tn(x_all[:, at], dqk_s[...]))
+    direct_send(QK)
     second_land(UP)
     bias_total.columns()
     for c in range(CHUNKS):
@@ -891,8 +912,7 @@
 
     direct_land(OV)
     if tight:
-        for j in range(3):
-            direct_copy(OV, j).wait_send()
+        direct_sent(OV)
     bias_total.step(2)
     direct_land(QK)
     bias_total.step(3)
@@ -911,8 +931,7 @@
         for i in range(4):
             keep_sum(i).wait()
             away_sums(i)[0].wait_recv()
-        for j in range(3):
-            direct_copy(QK, j).wait_send()
+        direct_sent(QK)
         bias_total.sends_done()
 
         @pl.when(home)
@@ -974,7 +993,7 @@
         V((4, 8, 128), F32), V((4, 4, 8, 128), F32), V((6, 4, 8, 128), F32),
         V((1, length), jnp.int32), [V(b.shape, BF16) for b in args[9:]],
         *[D((4, CHUNKS, 3))] * 4, D((12,)), D((12,)), D((8, 3)), D((8, 3)),
-        D((2, 2, 2)), D((2, 2, 2)), D((2, 3)), D((2, 3)), D((4, 2)), D((4, 2)),
+        D((2, 2, 2)), D((2, 2, 2)), D((2, 3, 2)), D((2, 3, 2)), D((4, 2)), D((4, 2)),
         D((6,)), D((6,)), D((6,)), D((6,)), D((2, CHUNKS)), D((2, CHUNKS)), D((9,)), D((11,)),
     ]
     return pl.pallas_call(

time: 109 us -> 109 us (level)
  no operation moved by 1% of the time
where the time goes in v6:
time: 109 us
  Pallas kernels  108 us (99%)
    pallas_call x1, Pallas kernels, layer_call(): pl.pallas_call(partial(layer_kernel, tight), out_shape=out_shape, in_spec...  105 us
    pallas_call x1, Pallas kernels, finish_call(): pl.pallas_call(finish_kernel, out_shape=shapes, in_specs=[any_space] * le...  2.56 us

profile of v6, /device:TPU:1, one launch (start us, length us, event | category | flops | bytes accessed | tf_op | source)
XLA Modules:
  0.0 108.9 jit_solution(11962722694463948059)
XLA Ops:
  0.7 105.5 %shard_map.322 = (bf16[128,768]{1,0:T(8,128)(2,1)}, bf16[128,768]{1,0:T(8,128)(2,1)}, bf16[96,768]{1,0:T(8,128)(2,1)}, bf16[96,768]{1,0:T(8,128)(2,1)}, bf16[96,...) custom-call(bf16[128,768]{1,0:T(8,128)(2,1)} %tokens.1, ...), custom_call_target="tpu_custom_call" | custom-call | tf_op jit(solution)/shard_map/pallas_call | solution.py:999
  106.2 2.6 %shard_map.323 = (bf16[128,768]{1,0:T(8,128)(2,1)}, f32[128,768]{1,0:T(8,128)}, f32[96,192]{1,0:T(8,128)}, f32[768]{0:T(1024)}, f32[96,192]{1,0:T(8,128)}, /*ind...) custom-call(bf16[128,768]{1,0:T(8,128)(2,1)} %get-tuple-element.48.r, ...), custom_call_target="tpu_custom_call" | custom-call | tf_op jit(solution)/shard_map/pallas_call | solution.py:1071
